TPU v7x, 128 devices: a whole 4x4x4 slice. The times are simulated.
128 devices in a mesh: dp: 4 (over z), expert: 32 (over x, y, core).
Axes of the slice: x: 4, y: 4, z: 4, core: 2. Of those that a mesh axis runs over, the one named last changes fastest.
Arguments:
- block_input: bfloat16 [32, 1024, 1024], P('expert', 'dp'), may hold values from -6 to 6
- attn_norm_gain: float32 [1024], replicated, may hold values from 0.1 to 1.9
- query_proj: bfloat16 [1024, 1024], replicated, may hold values from -0.1875 to 0.1875
- key_proj: bfloat16 [1024, 512], replicated, may hold values from -0.1875 to 0.1875
- value_proj: bfloat16 [1024, 512], replicated, may hold values from -0.1875 to 0.1875
- query_gain: float32 [64], replicated, may hold values from 0.1 to 1.9
- key_gain: float32 [64], replicated, may hold values from 0.1 to 1.9
- output_proj: bfloat16 [1024, 1024], replicated, may hold values from -1 to 1
- ffn_norm_gain: float32 [1024], replicated, may hold values from 0.1 to 1.9
- router_proj: bfloat16 [1024, 32], replicated, may hold values from -0.09375 to 0.09375
- expert_routes: int32 [32, 1024, 8], P('expert', 'dp'), may hold values from 0 to 31, all different within a row; in each aligned block of 256 rows (0 to 255, 256 to 511, ..., all dimensions but the last counted through in order) at most 80 rows name the same one
- document_ids: int32 [32, 1024], P('expert'), may hold values from 0 to 2, as said below
- expert_gate: bfloat16 [32, 1024, 512], P('expert'), may hold values from -0.1875 to 0.1875
- expert_up: bfloat16 [32, 1024, 512], P('expert'), may hold values from -0.1875 to 0.1875
- expert_down: bfloat16 [32, 512, 1024], P('expert'), may hold values from -1 to 1
- cotangent: bfloat16 [32, 1024, 1024], P('expert', 'dp'), may hold values from -6 to 6
Outputs:
- block_output: bfloat16 [32, 1024, 1024], P('expert', 'dp')
- input_grad: float32 [32, 1024, 1024], P('expert', 'dp')
- attn_gain_grad: float32 [1024], replicated
- query_grad: float32 [1024, 1024], replicated
- key_grad: float32 [1024, 512], replicated
- value_grad: float32 [1024, 512], replicated
- query_gain_grad: float32 [64], replicated
- key_gain_grad: float32 [64], replicated
- output_grad: float32 [1024, 1024], replicated
- ffn_gain_grad: float32 [1024], replicated
- router_grad: float32 [1024, 32], replicated
- gate_grad: float32 [32, 1024, 512], P('expert', 'dp')
- up_grad: float32 [32, 1024, 512], P('expert', 'dp')
- down_grad: float32 [32, 512, 1024], P('expert', None, 'dp')
Inputs may be any that keep to these rules, and one draw needn't show every extreme that they name: `expert_routes`: each row names 8 different experts; among the 256 tokens of one device no expert is chosen more than 80 times. `document_ids`: never falling along a sequence; document 1 begins within the first 256 tokens and ends within the last 256 tokens.
All inputs are finite; a program needn't handle non-finite values.
Results may differ from a plain program's by a relative error of at most 0.022.
Values may be sent and summed in bfloat16 or wider, within the bound.
No kernel may reach another device: no remote copies, remote signals or barrier semaphores. Data moves between devices by JAX's collectives and lax.ppermute only.
A program may use at most 192 MiB of HBM per device.

v0:
```python
import math

import jax
import jax.numpy as jnp
from jax import lax
from jax.sharding import PartitionSpec as P

CAP = 80


epsilon = 1e-06
theta = 10000.0
masked = -1e30


def in_one_piece(arrays, axis, dim, along):
    both = jnp.concatenate(arrays, axis=along)
    whole, at, gathered = (lax.all_gather(both, axis, axis=dim, tiled=True), 0, [])
    for a in arrays:
        gathered.append(lax.slice_in_dim(whole, at, at + a.shape[along], axis=along))
        at += a.shape[along]
    return tuple(gathered)


def in_one_piece_2(arrays, axis, dim, along):
    ends, at = ([], 0)
    for a in arrays[:-1]:
        at += a.shape[along]
        ends.append(at)
    both = jnp.concatenate(arrays, axis=along)
    return tuple(
        jnp.split(lax.psum_scatter(both, axis, scatter_dimension=dim, tiled=True), ends, axis=along)
    )


def rms_apply(values, gain):
    scale = lax.rsqrt(jnp.mean(values * values, axis=-1, keepdims=True) + epsilon)
    return (values * scale * gain, scale)


def rms_back(values, scale, gain, upstream):
    gain_grad = jnp.sum(upstream * values * scale, axis=tuple(range(values.ndim - 1)))
    weighted = upstream * gain
    inner = jnp.mean(weighted * values, axis=-1, keepdims=True)
    return (scale * weighted - values * (scale * scale * scale) * inner, gain_grad)


def positions(doc_row):
    order = jnp.arange(doc_row.shape[0], dtype=jnp.int32)
    change = jnp.concatenate([jnp.ones((1,), jnp.bool_), doc_row[1:] != doc_row[:-1]])
    starts = lax.cummax(jnp.where(change, order, jnp.zeros_like(order)), axis=0)
    return order - starts


def rope_tables(position, head_width):
    half_width = head_width // 2
    frequency = theta ** (-jnp.arange(half_width, dtype=jnp.float32) * 2.0 / head_width)
    angles = position.astype(jnp.float32)[:, None] * frequency[None, :]
    return (jnp.cos(angles)[:, None, :], jnp.sin(angles)[:, None, :])


def rotate(values, cosine, sine_table, direction):
    half_width = values.shape[-1] // 2
    first_half = values[..., :half_width]
    second = values[..., half_width:]
    return jnp.concatenate(
        [
            first_half * cosine - direction * second * sine_table,
            second * cosine + direction * first_half * sine_table,
        ],
        axis=-1,
    )


def score_table(query_four, key_rows, query_order, query_doc, key_order, key_doc):
    raw = jnp.einsum("qkgd,skd->kgqs", query_four, key_rows, preferred_element_type=jnp.float32)
    scores = raw / math.sqrt(query_four.shape[-1])
    allowed = (key_order[None, :] <= query_order[:, None]) & (
        key_doc[None, :] == query_doc[:, None]
    )
    return jnp.where(allowed, scores, masked)


def attend(query_four, key_rows, value_rows, query_order, query_doc, key_order, key_doc):
    scores = score_table(query_four, key_rows, query_order, query_doc, key_order, key_doc)
    top_value = jnp.max(scores, axis=-1, keepdims=True)
    expo = jnp.exp(scores - top_value)
    total = jnp.sum(expo, axis=-1, keepdims=True)
    probs_low = (expo / total).astype(jnp.bfloat16)
    attended = jnp.einsum(
        "kgqs,skd->qkgd", probs_low, value_rows, preferred_element_type=jnp.float32
    )
    return (attended, top_value, total)


def attend_back(
    query_four,
    key_rows,
    value_rows,
    query_order,
    query_doc,
    key_order,
    key_doc,
    top_value,
    total,
    grad_four,
):
    scores = score_table(query_four, key_rows, query_order, query_doc, key_order, key_doc)
    probs = jnp.exp(scores - top_value) / total
    probs_low = probs.astype(jnp.bfloat16)
    d_probs = jnp.einsum(
        "qkgd,skd->kgqs", grad_four, value_rows, preferred_element_type=jnp.float32
    )
    inner = jnp.sum(probs * d_probs, axis=-1, keepdims=True)
    d_raw = (probs * (d_probs - inner) / math.sqrt(query_four.shape[-1])).astype(jnp.bfloat16)
    d_query = jnp.einsum("kgqs,skd->qkgd", d_raw, key_rows, preferred_element_type=jnp.float32)
    d_key = jnp.einsum("kgqs,qkgd->skd", d_raw, query_four, preferred_element_type=jnp.float32)
    d_value = jnp.einsum("kgqs,qkgd->skd", probs_low, grad_four, preferred_element_type=jnp.float32)
    return (d_query, d_key, d_value)


def body(
    block_input,
    attn_norm_gain,
    query_proj,
    key_proj,
    value_proj,
    query_gain,
    key_gain,
    output_proj,
    ffn_norm_gain,
    router_proj,
    expert_routes,
    document_ids,
    expert_gate,
    expert_up,
    expert_down,
    cotangent,
):
    tokens = block_input.shape[1]
    width = block_input.shape[2]
    head_width = query_gain.shape[0]
    heads = query_proj.shape[1] // head_width
    kv_heads = key_proj.shape[1] // head_width
    group_size = heads // kv_heads
    topk_count = expert_routes.shape[2]
    experts_all = router_proj.shape[1]
    local_experts = expert_gate.shape[0]
    capacity = CAP
    expert_devices = lax.axis_size("expert")
    offset = lax.axis_index("dp") * tokens
    inputs = block_input[0].astype(jnp.float32)
    doc_row = document_ids[0]
    seq_length = doc_row.shape[0]
    order_all = jnp.arange(seq_length, dtype=jnp.int32)
    position_all = positions(doc_row)
    position_here = lax.dynamic_slice_in_dim(position_all, offset, tokens)
    doc_here = lax.dynamic_slice_in_dim(doc_row, offset, tokens)
    order_here = lax.dynamic_slice_in_dim(order_all, offset, tokens)
    normed, scale_one = rms_apply(inputs, attn_norm_gain)
    normed_low = normed.astype(jnp.bfloat16)
    query_raw = jnp.dot(normed_low, query_proj, preferred_element_type=jnp.float32).reshape(
        tokens, heads, head_width
    )
    key_raw = jnp.dot(normed_low, key_proj, preferred_element_type=jnp.float32).reshape(
        tokens, kv_heads, head_width
    )
    value_low = jnp.dot(normed_low, value_proj, preferred_element_type=jnp.float32).astype(
        jnp.bfloat16
    )
    value_low = value_low.reshape(tokens, kv_heads, head_width)
    query_normed, query_scale = rms_apply(query_raw, query_gain)
    key_normed, key_scale = rms_apply(key_raw, key_gain)
    cosine, sine_table = rope_tables(position_here, head_width)
    query_low = rotate(query_normed, cosine, sine_table, 1.0).astype(jnp.bfloat16)
    key_low = rotate(key_normed, cosine, sine_table, 1.0).astype(jnp.bfloat16)
    key_all, value_all = in_one_piece((key_low, value_low), "dp", 0, 1)
    query_four = query_low.reshape(tokens, kv_heads, group_size, head_width)
    attended, top_value, total = attend(
        query_four, key_all, value_all, order_here, doc_here, order_all, doc_row
    )
    attended_low = attended.reshape(tokens, heads * head_width).astype(jnp.bfloat16)
    middle = inputs + jnp.dot(attended_low, output_proj, preferred_element_type=jnp.float32)
    normed_two, scale_two = rms_apply(middle, ffn_norm_gain)
    normed_two_low = normed_two.astype(jnp.bfloat16)
    logits = jnp.dot(normed_two_low, router_proj, preferred_element_type=jnp.float32)
    routes = expert_routes[0]
    chosen = jnp.take_along_axis(logits, routes, axis=1)
    chosen_top = jnp.max(chosen, axis=-1, keepdims=True)
    chosen_expo = jnp.exp(chosen - chosen_top)
    gate_rows = chosen_expo / jnp.sum(chosen_expo, axis=-1, keepdims=True)
    flat_routes = routes.reshape(-1)
    member = (flat_routes[:, None] == jnp.arange(experts_all, dtype=jnp.int32)[None, :]).astype(
        jnp.int32
    )
    rank = jnp.sum(
        (jnp.cumsum(member, axis=0, dtype=jnp.int32) - 1) * member, axis=1, dtype=jnp.int32
    )
    slot_index = flat_routes * capacity + rank
    slot_table = jnp.full((experts_all * capacity,), tokens * topk_count, jnp.int32)
    slot_table = slot_table.at[slot_index].set(jnp.arange(tokens * topk_count, dtype=jnp.int32))
    padded_two = jnp.concatenate([normed_two_low, jnp.zeros((1, width), jnp.bfloat16)], axis=0)
    dispatch_rows = padded_two[slot_table // topk_count].reshape(
        expert_devices, local_experts, capacity, width
    )
    received = lax.all_to_all(dispatch_rows, "expert", split_axis=0, concat_axis=0, tiled=True)
    gate_act = jnp.einsum(
        "slcd,ldf->slcf", received, expert_gate, preferred_element_type=jnp.float32
    )
    up_act = jnp.einsum("slcd,ldf->slcf", received, expert_up, preferred_element_type=jnp.float32)
    hidden_low = (gate_act / (1.0 + jnp.exp(-gate_act)) * up_act).astype(jnp.bfloat16)
    result = jnp.einsum(
        "slcf,lfd->slcd", hidden_low, expert_down, preferred_element_type=jnp.float32
    )
    returned = lax.all_to_all(
        result.astype(jnp.bfloat16), "expert", split_axis=0, concat_axis=0, tiled=True
    )
    expert_out = returned.reshape(experts_all * capacity, width)[slot_index].reshape(
        tokens, topk_count, width
    )
    mixture = jnp.sum(gate_rows[:, :, None] * expert_out, axis=1)
    block_output = (middle + mixture).astype(jnp.bfloat16)
    upstream = cotangent[0].astype(jnp.float32)
    d_gates = jnp.sum(upstream[:, None, :] * expert_out, axis=2)
    slot_grad = (
        (gate_rows[:, :, None] * upstream[:, None, :])
        .astype(jnp.bfloat16)
        .reshape(tokens * topk_count, width)
    )
    padded_grad = jnp.concatenate([slot_grad, jnp.zeros((1, width), jnp.bfloat16)], axis=0)
    send_grads = padded_grad[slot_table].reshape(expert_devices, local_experts, capacity, width)
    recv_grads = lax.all_to_all(send_grads, "expert", split_axis=0, concat_axis=0, tiled=True)
    gate_act = jnp.einsum(
        "slcd,ldf->slcf", received, expert_gate, preferred_element_type=jnp.float32
    )
    up_act = jnp.einsum("slcd,ldf->slcf", received, expert_up, preferred_element_type=jnp.float32)
    sigmoid_part = 1.0 / (1.0 + jnp.exp(-gate_act))
    silu_part = gate_act / (1.0 + jnp.exp(-gate_act))
    hidden_low = (silu_part * up_act).astype(jnp.bfloat16)
    d_hidden = jnp.einsum(
        "slcd,lfd->slcf", recv_grads, expert_down, preferred_element_type=jnp.float32
    )
    d_gate_low = (d_hidden * up_act * (sigmoid_part + silu_part * (1.0 - sigmoid_part))).astype(
        jnp.bfloat16
    )
    d_up_low = (d_hidden * silu_part).astype(jnp.bfloat16)
    d_rows = jnp.einsum(
        "slcf,ldf->slcd", d_gate_low, expert_gate, preferred_element_type=jnp.float32
    )
    d_rows = d_rows + jnp.einsum(
        "slcf,ldf->slcd", d_up_low, expert_up, preferred_element_type=jnp.float32
    )
    returned_grads = lax.all_to_all(
        d_rows.astype(jnp.bfloat16), "expert", split_axis=0, concat_axis=0, tiled=True
    )
    gate_w = jnp.einsum("slcd,slcf->ldf", received, d_gate_low, preferred_element_type=jnp.float32)
    up_w = jnp.einsum("slcd,slcf->ldf", received, d_up_low, preferred_element_type=jnp.float32)
    down_w = jnp.einsum(
        "slcd,slcf->ldf", recv_grads, hidden_low, preferred_element_type=jnp.float32
    )
    gate_grad, up_grad, down_turned = tuple(
        (
            part.astype(jnp.float32)
            for part in in_one_piece_2(
                (
                    gate_w.astype(jnp.bfloat16),
                    up_w.astype(jnp.bfloat16),
                    down_w.astype(jnp.bfloat16),
                ),
                "dp",
                1,
                0,
            )
        )
    )
    down_grad = jnp.transpose(down_turned, (0, 2, 1))
    back_rows = returned_grads.reshape(experts_all * capacity, width)[slot_index].reshape(
        tokens, topk_count, width
    )
    d_chosen = gate_rows * (d_gates - jnp.sum(gate_rows * d_gates, axis=-1, keepdims=True))
    route_match = routes[:, :, None] == jnp.arange(experts_all, dtype=jnp.int32)[None, None, :]
    d_logits_low = jnp.sum(jnp.where(route_match, d_chosen[:, :, None], 0.0), axis=1).astype(
        jnp.bfloat16
    )
    router_local = jnp.dot(normed_two_low.T, d_logits_low, preferred_element_type=jnp.float32)
    d_normed_two = jnp.sum(back_rows.astype(jnp.float32), axis=1)
    d_normed_two = d_normed_two + jnp.dot(
        d_logits_low, router_proj.T, preferred_element_type=jnp.float32
    )
    d_middle_norm, ffn_gain_local = rms_back(middle, scale_two, ffn_norm_gain, d_normed_two)
    d_middle = upstream + d_middle_norm
    d_branch = d_middle.astype(jnp.bfloat16)
    output_local = jnp.dot(attended_low.T, d_branch, preferred_element_type=jnp.float32)
    d_attended_low = jnp.dot(d_branch, output_proj.T, preferred_element_type=jnp.float32).astype(
        jnp.bfloat16
    )
    d_query, d_key, d_value = attend_back(
        query_four,
        key_all,
        value_all,
        order_here,
        doc_here,
        order_all,
        doc_row,
        top_value,
        total,
        d_attended_low.reshape(tokens, kv_heads, group_size, head_width),
    )
    d_key_rot, d_value_sum = tuple(
        (
            part.astype(jnp.float32)
            for part in in_one_piece_2(
                (d_key.astype(jnp.bfloat16), d_value.astype(jnp.bfloat16)), "dp", 0, 1
            )
        )
    )
    d_query_rot = d_query.reshape(tokens, heads, head_width)
    d_query_normed = rotate(d_query_rot, cosine, sine_table, -1.0)
    d_key_normed = rotate(d_key_rot, cosine, sine_table, -1.0)
    d_query_raw, query_gain_local = rms_back(query_raw, query_scale, query_gain, d_query_normed)
    d_key_raw, key_gain_local = rms_back(key_raw, key_scale, key_gain, d_key_normed)
    d_query_low = d_query_raw.reshape(tokens, heads * head_width).astype(jnp.bfloat16)
    d_key_low = d_key_raw.reshape(tokens, kv_heads * head_width).astype(jnp.bfloat16)
    d_value_low = d_value_sum.reshape(tokens, kv_heads * head_width).astype(jnp.bfloat16)
    query_local = jnp.dot(normed_low.T, d_query_low, preferred_element_type=jnp.float32)
    key_local = jnp.dot(normed_low.T, d_key_low, preferred_element_type=jnp.float32)
    value_local = jnp.dot(normed_low.T, d_value_low, preferred_element_type=jnp.float32)
    d_normed = jnp.dot(d_query_low, query_proj.T, preferred_element_type=jnp.float32)
    d_normed = d_normed + jnp.dot(d_key_low, key_proj.T, preferred_element_type=jnp.float32)
    d_normed = d_normed + jnp.dot(d_value_low, value_proj.T, preferred_element_type=jnp.float32)
    d_input_norm, attn_gain_local = rms_back(inputs, scale_one, attn_norm_gain, d_normed)
    input_grad = d_middle + d_input_norm
    (
        attn_gain_sum,
        query_sum,
        key_sum,
        value_sum,
        query_gain_sum,
        key_gain_sum,
        output_sum,
        ffn_gain_sum,
        router_sum,
    ) = lax.psum(
        (
            attn_gain_local,
            query_local,
            key_local,
            value_local,
            query_gain_local,
            key_gain_local,
            output_local,
            ffn_gain_local,
            router_local,
        ),
        ("dp", "expert"),
    )
    return (
        block_output[None],
        input_grad[None],
        attn_gain_sum,
        query_sum,
        key_sum,
        value_sum,
        query_gain_sum,
        key_gain_sum,
        output_sum,
        ffn_gain_sum,
        router_sum,
        gate_grad,
        up_grad,
        down_grad,
    )


def solution(mesh):
    placed = (
        P("expert", "dp", None),
        P(),
        P(),
        P(),
        P(),
        P(),
        P(),
        P(),
        P(),
        P(),
        P("expert", "dp", None),
        P("expert", None),
        P("expert", None, None),
        P("expert", None, None),
        P("expert", None, None),
        P("expert", "dp", None),
    )
    return jax.shard_map(
        body,
        mesh=mesh,
        in_specs=placed,
        out_specs=(
            P("expert", "dp", None),
            P("expert", "dp", None),
            P(),
            P(),
            P(),
            P(),
            P(),
            P(),
            P(),
            P(),
            P(),
            P("expert", "dp", None),
            P("expert", "dp", None),
            P("expert", None, "dp"),
        ),
        check_vma=False,
    )
```

profile of v0, /device:TPU:6, one launch (start us, length us, event | category | flops | bytes accessed | tf_op | source)
XLA Modules:
  0.0 753.3 jit_solution(10781498785199869663)
XLA Ops:
  12.8 2.3 copy.79
  22.5 17.7 %reduce-window.19 = s32[32,16,128]{2,1,0:T(8,128)} reduce-window(s32[32,16,128]{2,1,0:T(8,128)} %fusion.119, s32[]{:T(128)} %constant.49.clone.1), window={size=1x1x128 pad=0_0x0_0x127_0}, to_apply=%region_10.11 | reduce-window | flops 8323072 | bytes 524292 | tf_op jit(solution)/shard_map/reduce-window.2
  43.3 4.0 copy.81
  48.6 8.1 %scatter_custom_fusion = s32[2560]{0:T(1024)S(1)} fusion(s32[2048]{0:T(1024)S(1)} %bitcast.414, s32[2048]{0:T(1024)S(1)} %iota.50, s32[]{:T(128)} %constant.99.clone.1), kind=kCustom, calls=%fused_computation.212 | custom fusion | bytes 10244 | tf_op jit(solution)/shard_map/scatter | solution.py:201
  57.3 2.4 multiply_reduce_fusion.5
  61.9 10.3 %fusion.150 = (f32[8,2,256]{2,1,0:T(2,128)S(1)}, f32[8,2,256,1024]{2,3,1,0:T(8,128)}) fusion(pred[256,1024]{0,1:T(8,128)(4,1)} %fusion.97, bf16[1024,16,64]{0,2,1:T(8,128)(2,1)} %all-gather.2.cloned.1.call-done, bf16[256,8,2,32]{0,3,2,1:T(8,128)(2,1)S(1)} %bitcast.407, bf16[256,8,2,32]{0,3,2,1:T(8,128)(2,1)S(1)} %bitcast.405), kind=kOutput, calls=%fused_computation.241 | convolution fusion | flops 554697728 | bytes 18628608 | tf_op jit(solution)/shard_map/sub | solution.py:87
  72.3 7.7 %fusion.76 = bf16[8,64,2,256]{3,1,2,0:T(8,128)(2,1)S(1)} fusion(bf16[1024,16,64]{0,2,1:T(8,128)(2,1)} %all-gather.2.cloned.1.call-done, f32[8,2,256,1024]{2,3,1,0:T(8,128)} %get-tuple-element.125, f32[8,2,256]{2,1,0:T(2,128)S(1)} %get-tuple-element.124), kind=kOutput, calls=%fused_computation.90 | convolution fusion | flops 545521664 | bytes 18366464 | tf_op jit(solution)/shard_map/kgqs,skd->qkgd/dot_general | solution.py:90
  82.8 9.0 %gather_fusion = bf16[2560,1024]{1,0:T(8,128)(2,1)} fusion(bf16[257,1024]{1,0:T(8,128)(2,1)S(1)} %concatenate.46, s32[3072]{0:T(1024)S(1)} %get-tuple-element.131), kind=kCustom, calls=%fused_computation | custom fusion | bytes 10496000 | tf_op jit(solution)/shard_map/gather | solution.py:203
  91.8 7.8 %all-to-all-start = ((bf16[32,1,80,1024]{3,2,1,0:T(8,128)(2,1)}), bf16[32,1,80,1024]{3,2,1,0:T(8,128)(2,1)}, u32[]{:S(2)}, u32[]{:S(2)}) async-start(bf16[32,1,80,1024]{3,2,1,0:T(8,128)(2,1)} %bitcast.388), calls=%async_computation | async-start | bytes 10485760 | tf_op jit(solution)/shard_map/all_to_all | solution.py:206
  102.3 16.8 %gather_fusion.4 = f32[2048]{0:T(1024)S(1)} fusion(f32[256,32]{0,1:T(8,128)S(1)} %fusion.155, s32[2048]{0:T(1024)S(1)} %reshape.612), kind=kCustom, calls=%fused_computation.4 | custom fusion | bytes 32768 | tf_op jit(solution)/shard_map/jit(take_along_axis)/gather | solution.py:188
  123.7 2.5 concatenate.47
  126.2 14.8 %gather_fusion.2 = bf16[2560,1024]{1,0:T(8,128)(2,1)} fusion(bf16[2049,1024]{1,0:T(8,128)(2,1)} %concatenate.47, s32[3072]{0:T(1024)S(1)} %copy-done.42), kind=kCustom, calls=%fused_computation.2 | custom fusion | bytes 10496000 | tf_op jit(solution)/shard_map/gather | solution.py:231
  141.0 22.6 %all-to-all-done = bf16[32,1,80,1024]{3,2,1,0:T(8,128)(2,1)} async-done(((bf16[32,1,80,1024]{3,2,1,0:T(8,128)(2,1)}), bf16[32,1,80,1024]{3,2,1,0:T(8,128)(2,1)}, u32[]{:S(2)}, u32[]{:S(2)}) %all-to-all-start) | async-done | bytes 5242912 | tf_op jit(solution)/shard_map/all_to_all | solution.py:206
  163.6 10.3 %all-to-all-start.2 = ((bf16[32,1,80,1024]{3,2,1,0:T(8,128)(2,1)}), bf16[32,1,80,1024]{3,2,1,0:T(8,128)(2,1)}, u32[]{:S(2)}, u32[]{:S(2)}) async-start(bf16[32,1,80,1024]{3,2,1,0:T(8,128)(2,1)} %bitcast.389), calls=%async_computation.2 | async-start | bytes 10485760 | tf_op jit(solution)/shard_map/all_to_all | solution.py:232
  174.0 8.0 %fusion.31 = f32[32,80,512]{2,1,0:T(8,128)} fusion(bf16[32,1,80,1024]{3,2,1,0:T(8,128)(2,1)} %all-to-all-done, bf16[1,1024,512]{2,1,0:T(8,128)(2,1)} %param.29), kind=kOutput, calls=%fused_computation.52 | convolution fusion | flops 2684354560 | bytes 11534336 | tf_op jit(solution)/shard_map/slcd,ldf->slcf/dot_general | solution.py:210
  182.0 56.2 %all-to-all-done.2 = bf16[32,1,80,1024]{3,2,1,0:T(8,128)(2,1)} async-done(((bf16[32,1,80,1024]{3,2,1,0:T(8,128)(2,1)}), bf16[32,1,80,1024]{3,2,1,0:T(8,128)(2,1)}, u32[]{:S(2)}, u32[]{:S(2)}) %all-to-all-start.2) | async-done | bytes 5242912 | tf_op jit(solution)/shard_map/all_to_all | solution.py:232
  238.2 5.3 fusion.22
  243.6 9.0 %fusion.40 = (bf16[32,80,512]{2,1,0:T(8,128)(2,1)}, bf16[32,1,80,512]{3,2,0,1:T(8,128)(2,1)}, bf16[32,80,512]{2,1,0:T(8,128)(2,1)S(1)}) fusion(f32[32,80,512]{2,1,0:T(8,128)S(1)} %fusion.22, f32[32,80,512]{2,1,0:T(8,128)S(1)} %copy-done.66, bf16[1,1024,512]{2,1,0:T(8,128)(2,1)S(1)} %copy-done.60, bf16[32,1,80,1024]{3,2,1,0:T(8,128)(2,1)} %all-to-all-done), kind=kOutput, calls=%fused_computation.63 | convolution fusion | flops 2702704640 | bytes 24641536 | tf_op jit(solution)/shard_map/slcd,ldf->slcf/dot_general | solution.py:207
  254.1 4.5 convert_bitcast_fusion
  258.6 8.6 %all-to-all-start.1 = ((bf16[32,1,80,1024]{3,2,1,0:T(8,128)(2,1)}), bf16[32,1,80,1024]{3,2,1,0:T(8,128)(2,1)}, u32[]{:S(2)}, u32[]{:S(2)}) async-start(bf16[32,1,80,1024]{3,2,1,0:T(8,128)(2,1)} %convert_bitcast_fusion), calls=%async_computation.1 | async-start | bytes 10485760 | tf_op jit(solution)/shard_map/all_to_all | solution.py:215
  267.2 5.3 fusion.42
  272.5 5.1 fusion.15
  277.6 53.8 %all-to-all-done.1 = bf16[32,1,80,1024]{3,2,1,0:T(8,128)(2,1)} async-done(((bf16[32,1,80,1024]{3,2,1,0:T(8,128)(2,1)}), bf16[32,1,80,1024]{3,2,1,0:T(8,128)(2,1)}, u32[]{:S(2)}, u32[]{:S(2)}) %all-to-all-start.1) | async-done | bytes 5242912 | tf_op jit(solution)/shard_map/all_to_all | solution.py:215
  331.5 19.8 %all-to-all-start.3 = ((bf16[32,1,80,1024]{3,2,1,0:T(8,128)(2,1)}), bf16[32,1,80,1024]{3,2,1,0:T(8,128)(2,1)}, u32[]{:S(2)}, u32[]{:S(2)}) async-start(bf16[32,1,80,1024]{3,2,1,0:T(8,128)(2,1)} %fusion.15), calls=%async_computation.3 | async-start | bytes 10485760 | tf_op jit(solution)/shard_map/all_to_all | solution.py:253
  352.4 14.1 %gather_fusion.1 = bf16[2048,1024]{1,0:T(8,128)(2,1)} fusion(bf16[2560,1024]{1,0:T(8,128)(2,1)} %bitcast.50, s32[2048]{0:T(1024)S(1)} %broadcast_clamp_fusion), kind=kCustom, calls=%fused_computation.1 | custom fusion | bytes 8396800 | tf_op jit(solution)/shard_map/gather | solution.py:218
  366.5 6.2 fusion.7
  372.9 42.6 %all-to-all-done.3 = bf16[32,1,80,1024]{3,2,1,0:T(8,128)(2,1)} async-done(((bf16[32,1,80,1024]{3,2,1,0:T(8,128)(2,1)}), bf16[32,1,80,1024]{3,2,1,0:T(8,128)(2,1)}, u32[]{:S(2)}, u32[]{:S(2)}) %all-to-all-start.3) | async-done | bytes 5242912 | tf_op jit(solution)/shard_map/all_to_all | solution.py:253
  415.5 14.1 %gather_fusion.3 = bf16[2048,1024]{1,0:T(8,128)(2,1)} fusion(bf16[2560,1024]{1,0:T(8,128)(2,1)} %bitcast.72, s32[2048]{0:T(1024)S(1)} %broadcast_clamp_fusion), kind=kCustom, calls=%fused_computation.3 | custom fusion | bytes 8396800 | tf_op jit(solution)/shard_map/gather | solution.py:277
  429.6 5.6 convert_reduce_fusion
  439.1 9.5 %fusion.57 = bf16[1024,8,64]{0,2,1:T(8,128)(2,1)} fusion(bf16[256,8,2,64]{0,3,2,1:T(8,128)(2,1)S(1)} %bitcast.392, f32[8,2,256,1024]{2,3,1,0:T(8,128)} %get-tuple-element.125, f32[8,2,256]{2,1,0:T(2,128)S(1)} %copy-done.68), kind=kOutput, calls=%fused_computation.75 | convolution fusion | flops 545783808 | bytes 18366464 | tf_op jit(solution)/shard_map/kgqs,qkgd->skd/dot_general | solution.py:118
  448.6 8.1 %fusion.98 = f32[8,1024,256,2]{2,1,3,0:T(8,128)} fusion(bf16[256,8,2,64]{0,3,2,1:T(8,128)(2,1)S(1)} %bitcast.393, bf16[1024,16,64]{0,2,1:T(8,128)(2,1)S(1)} %copy-done.24), kind=kOutput, calls=%fused_computation.127 | convolution fusion | flops 536870912 | bytes 18350080 | tf_op jit(solution)/shard_map/qkgd,skd->kgqs/dot_general | solution.py:111
  456.7 23.5 %fusion.56 = bf16[1024,8,64]{0,2,1:T(8,128)(2,1)} fusion(f32[8,1024,256,2]{2,1,3,0:T(8,128)} %fusion.98, bf16[256,8,2,32]{0,3,2,1:T(8,128)(2,1)} %bitcast.408, bf16[256,8,2,32]{0,3,2,1:T(8,128)(2,1)S(1)} %bitcast.406, f32[8,2,256,1024]{2,3,1,0:T(8,128)} %get-tuple-element.125, f32[8,2,256]{2,1,0:T(2,128)S(1)} %copy-done.68), kind=kOutput, calls=%fused_computation.74 | convolution fusion | flops 567809024 | bytes 35143680 | tf_op jit(solution)/shard_map/kgqs,qkgd->skd/dot_general | solution.py:117
  480.3 2.7 pad_maximum_fusion.1
  483.3 6.3 fusion.68
  489.7 5.6 fusion.65
  495.2 5.4 fusion.60
  503.0 24.0 %fusion.14 = f32[8,64,2,256]{3,1,2,0:T(8,128)} fusion(f32[8,1024,256,2]{2,1,3,0:T(8,128)} %fusion.98, bf16[1024,16,64]{0,2,1:T(8,128)(2,1)} %all-gather.2.cloned.1.call-done, f32[8,2,256,1024]{2,3,1,0:T(8,128)} %get-tuple-element.125, f32[8,2,256]{2,1,0:T(2,128)S(1)} %copy-done.68), kind=kOutput, calls=%fused_computation.30 | convolution fusion | flops 566236160 | bytes 69238784 | tf_op jit(solution)/shard_map/kgqs,skd->qkgd/dot_general | solution.py:116
  532.6 2.9 fusion.106
  535.5 2.7 fusion.116
  544.7 3.4 fusion.156
  548.1 8.8 %reduce-scatter.5.cloned.1.call-done = bf16[3,256,512]{2,1,0:T(8,128)(2,1)} async-done(((bf16[3,1024,512]{2,1,0:T(8,128)(2,1)}), bf16[3,256,512]{2,1,0:T(8,128)(2,1)}) %reduce-scatter.5.cloned.1.call-update) | async-done | bytes 786448 | tf_op jit(solution)/shard_map/reduce_scatter | solution.py:32
  556.9 2.3 convert_bitcast_fusion.2
  560.2 2.1 convolution_add_fusion.2
  562.3 2.9 fusion.88
  565.2 65.3 %all-reduce.2 = (f32[1024]{0:T(1024)}, f32[64]{0:T(128)}, f32[64]{0:T(128)}, f32[1024]{0:T(1024)}) all-reduce(f32[1024]{0:T(1024)S(1)} %get-tuple-element.76, f32[64]{0:T(128)S(1)} %get-tuple-element.74, f32[64]{0:T(128)S(1)} %get-tuple-element.78, f32[1024]{0:T(1024)S(1)} %get-tuple-element.72), channel_id=1, replica_groups=mesh['dp'=4,'expert'=32] {'dp','expert'}, use_global_device_ids=true, to_apply=%region_26.27 | all-reduce | flops 2176 | bytes 17408 | tf_op jit(solution)/shard_map/psum | solution.py:343
  630.5 2.8 fusion.85
  633.3 101.7 %all-reduce.6.cloned.1.call-done = (f32[1024,1024]{1,0:T(8,128)}, f32[1024,512]{1,0:T(8,128)}, f32[1024,512]{1,0:T(8,128)}, f32[1024,1024]{1,0:T(8,128)}, f32[1024,32]{0,1:T(8,128)}) async-done(((f32[1024,1024]{1,0:T(8,128)}, f32[1024,512]{1,0:T(8,128)}, f32[1024,512]{1,0:T(8,128)}, f32[1024,1024]{1,0:T(8,128)}, f32[1024,32]{0,1:T(8,128)}), (f32[1024,1024]{1,0:T(8,128)}, f32[1024,512]{1,0:T(8,128)}, ...) | async-done | bytes 12714000 | tf_op jit(solution)/shard_map/psum | solution.py:343
  735.0 4.9 copy.118
  (238 shorter events, 58.4 us)
Async XLA Ops:
  7.2 72.8 %copy-start = (bf16[1024,1024]{1,0:T(8,128)(2,1)S(1)}, bf16[1024,1024]{1,0:T(8,128)(2,1)}, u32[]{:S(2)}) copy-start(bf16[1024,1024]{1,0:T(8,128)(2,1)} %param.23) | copy-start | bytes 6291460
  7.2 7.9 %copy-start.1 = (bf16[1,256,1024]{2,1,0:T(8,128)(2,1)S(1)}, bf16[1,256,1024]{2,1,0:T(8,128)(2,1)}, u32[]{:S(2)}) copy-start(bf16[1,256,1024]{2,1,0:T(8,128)(2,1)} %param.16) | copy-start | bytes 1572868
  7.2 7.9 %copy-start.39 = (f32[1024]{0:T(1024)S(1)}, f32[1024]{0:T(1024)}, u32[]{:S(2)}) copy-start(f32[1024]{0:T(1024)} %param.17) | copy-start | bytes 12292
  7.2 11.2 %copy-start.53 = (f32[64]{0:T(128)S(1)}, f32[64]{0:T(128)}, u32[]{:S(2)}) copy-start(f32[64]{0:T(128)} %param.22) | copy-start | bytes 772
  7.2 54.6 %all-gather.2.cloned.1.call-start = ((), (), s32[]{:S(2)}) async-start(), calls=%async_computation.6 | async-start | bytes 2621440 | tf_op jit(solution)/shard_map/all_gather | solution.py:18
  10.1 47.2 %copy-start.46 = (f32[256]{0:T(256)}, f32[256]{0:T(256)S(1)}, u32[]{:S(2)}) copy-start(f32[256]{0:T(256)S(1)} %get-tuple-element.117) | copy-start | bytes 3076
  10.7 8.7 %copy-start.38 = (s32[1,256,8]{1,2,0:T(8,128)S(1)}, s32[1,256,8]{1,2,0:T(8,128)}, u32[]{:S(2)}) copy-start(s32[1,256,8]{1,2,0:T(8,128)} %param.26) | copy-start | bytes 24580
  16.9 31.5 %copy-start.11 = (f32[256,8,64]{0,2,1:T(8,128)}, f32[256,8,64]{0,2,1:T(8,128)S(1)}, u32[]{:S(2)}) copy-start(f32[256,8,64]{0,2,1:T(8,128)S(1)} %get-tuple-element.121) | copy-start | bytes 1572868
  17.5 30.9 %copy-start.35 = (f32[256,8]{0,1:T(8,128)}, f32[256,8]{0,1:T(8,128)S(1)}, u32[]{:S(2)}) copy-start(f32[256,8]{0,1:T(8,128)S(1)} %get-tuple-element.112) | copy-start | bytes 24580
  18.4 43.2 %copy-start.26 = (f32[256,32]{0,1:T(8,128)}, f32[256,32]{0,1:T(8,128)S(1)}, u32[]{:S(2)}) copy-start(f32[256,32]{0,1:T(8,128)S(1)} %get-tuple-element.115) | copy-start | bytes 98308
  18.4 38.2 %copy-start.43 = (s32[1,1024]{1,0:T(1,128)S(1)}, s32[1,1024]{1,0:T(1,128)}, u32[]{:S(2)}) copy-start(s32[1,1024]{1,0:T(1,128)} %param.27) | copy-start | bytes 12292
  42.0 19.5 %copy-start.55 = (f32[64]{0:T(128)S(1)}, f32[64]{0:T(128)}, u32[]{:S(2)}) copy-start(f32[64]{0:T(128)} %param.21) | copy-start | bytes 772
  48.5 8.1 %copy-start.49 = (s32[2048,1]{0,1:T(1,128)}, s32[2048,1]{0,1:T(1,128)S(1)}, u32[]{:S(2)}) copy-start(s32[2048,1]{0,1:T(1,128)S(1)} %compare_select_fusion.1) | copy-start | bytes 24580
  60.4 11.8 %copy-start.29 = (f32[256,16]{0,1:T(8,128)}, f32[256,16]{0,1:T(8,128)S(1)}, u32[]{:S(2)}) copy-start(f32[256,16]{0,1:T(8,128)S(1)} %get-tuple-element.108) | copy-start | bytes 49156
  61.8 10.4 %copy-start.31 = (bf16[256,16,32]{0,2,1:T(8,128)(2,1)}, bf16[256,16,32]{0,2,1:T(8,128)(2,1)S(1)}, u32[]{:S(2)}) copy-start(bf16[256,16,32]{0,2,1:T(8,128)(2,1)S(1)} %get-tuple-element.94) | copy-start | bytes 786436
  61.8 10.4 %copy-start.33 = (bf16[256,16,32]{0,2,1:T(8,128)(2,1)}, bf16[256,16,32]{0,2,1:T(8,128)(2,1)S(1)}, u32[]{:S(2)}) copy-start(bf16[256,16,32]{0,2,1:T(8,128)(2,1)S(1)} %get-tuple-element.95) | copy-start | bytes 786436
  72.2 7.7 %copy-start.67 = (f32[8,2,256]{2,1,0:T(2,128)}, f32[8,2,256]{2,1,0:T(2,128)S(1)}, u32[]{:S(2)}) copy-start(f32[8,2,256]{2,1,0:T(2,128)S(1)} %get-tuple-element.124) | copy-start | bytes 49156
  72.2 9.6 %copy-start.44 = (f32[1024]{0:T(1024)S(1)}, f32[1024]{0:T(1024)}, u32[]{:S(2)}) copy-start(f32[1024]{0:T(1024)} %param.24) | copy-start | bytes 12292
  81.4 10.3 %copy-start.51 = (f32[256]{0:T(256)}, f32[256]{0:T(256)S(1)}, u32[]{:S(2)}) copy-start(f32[256]{0:T(256)S(1)} %get-tuple-element.119) | copy-start | bytes 3076
  91.8 9.2 %copy-start.34 = (bf16[1024,32]{0,1:T(8,128)(2,1)S(1)}, bf16[1024,32]{0,1:T(8,128)(2,1)}, u32[]{:S(2)}) copy-start(bf16[1024,32]{0,1:T(8,128)(2,1)} %param.25) | copy-start | bytes 196612
  91.8 71.9 %all-to-all-start = ((bf16[32,1,80,1024]{3,2,1,0:T(8,128)(2,1)}), bf16[32,1,80,1024]{3,2,1,0:T(8,128)(2,1)}, u32[]{:S(2)}, u32[]{:S(2)}) async-start(bf16[32,1,80,1024]{3,2,1,0:T(8,128)(2,1)} %bitcast.388), calls=%async_computation | async-start | bytes 10485760 | tf_op jit(solution)/shard_map/all_to_all | solution.py:206
  119.2 7.1 copy-start.19
  163.6 74.6 %all-to-all-start.2 = ((bf16[32,1,80,1024]{3,2,1,0:T(8,128)(2,1)}), bf16[32,1,80,1024]{3,2,1,0:T(8,128)(2,1)}, u32[]{:S(2)}, u32[]{:S(2)}) async-start(bf16[32,1,80,1024]{3,2,1,0:T(8,128)(2,1)} %bitcast.389), calls=%async_computation.2 | async-start | bytes 10485760 | tf_op jit(solution)/shard_map/all_to_all | solution.py:232
  243.6 10.5 %copy-start.59 = (bf16[1,512,1024]{2,1,0:T(8,128)(2,1)S(1)}, bf16[1,512,1024]{2,1,0:T(8,128)(2,1)}, u32[]{:S(2)}) copy-start(bf16[1,512,1024]{2,1,0:T(8,128)(2,1)} %param.30) | copy-start | bytes 3145732
  258.6 72.9 %all-to-all-start.1 = ((bf16[32,1,80,1024]{3,2,1,0:T(8,128)(2,1)}), bf16[32,1,80,1024]{3,2,1,0:T(8,128)(2,1)}, u32[]{:S(2)}, u32[]{:S(2)}) async-start(bf16[32,1,80,1024]{3,2,1,0:T(8,128)(2,1)} %convert_bitcast_fusion), calls=%async_computation.1 | async-start | bytes 10485760 | tf_op jit(solution)/shard_map/all_to_all | solution.py:215
  277.6 73.7 %copy-start.50 = (s32[2048,1]{0,1:T(1,128)S(1)}, s32[2048,1]{0,1:T(1,128)}, u32[]{:S(2)}) copy-start(s32[2048,1]{0,1:T(1,128)} %copy-done.49) | copy-start | bytes 24580
  331.5 84.1 %all-to-all-start.3 = ((bf16[32,1,80,1024]{3,2,1,0:T(8,128)(2,1)}), bf16[32,1,80,1024]{3,2,1,0:T(8,128)(2,1)}, u32[]{:S(2)}, u32[]{:S(2)}) async-start(bf16[32,1,80,1024]{3,2,1,0:T(8,128)(2,1)} %fusion.15), calls=%async_computation.3 | async-start | bytes 10485760 | tf_op jit(solution)/shard_map/all_to_all | solution.py:253
  351.3 186.9 %reduce-scatter.3.cloned.1.call-start = ((), (), s32[]{:S(2)}) async-start(), calls=%async_computation.7 | async-start | bytes 2621440 | tf_op jit(solution)/shard_map/reduce_scatter | solution.py:32
  429.6 5.7 copy-start.52
  429.6 6.3 copy-start.16
  429.6 6.3 copy-start.18
  429.6 6.3 copy-start.58
  439.1 9.5 %copy-start.24 = (bf16[1024,16,64]{0,2,1:T(8,128)(2,1)S(1)}, bf16[1024,16,64]{0,2,1:T(8,128)(2,1)}, u32[]{:S(2)}) copy-start(bf16[1024,16,64]{0,2,1:T(8,128)(2,1)} %all-gather.2.cloned.1.call-done) | copy-start | bytes 6291460
  448.6 8.1 %copy-start.32 = (bf16[256,16,32]{0,2,1:T(8,128)(2,1)S(1)}, bf16[256,16,32]{0,2,1:T(8,128)(2,1)}, u32[]{:S(2)}) copy-start(bf16[256,16,32]{0,2,1:T(8,128)(2,1)} %copy-done.31) | copy-start | bytes 786436
  456.7 23.5 %copy-start.25 = (bf16[1024,8,64]{0,2,1:T(8,128)(2,1)S(1)}, bf16[1024,8,64]{0,2,1:T(8,128)(2,1)}, u32[]{:S(2)}) copy-start(bf16[1024,8,64]{0,2,1:T(8,128)(2,1)} %fusion.57) | copy-start | bytes 3145732
  483.0 73.9 %reduce-scatter.5.cloned.1.call-start = ((), (), s32[]{:S(2)}) async-start(), calls=%async_computation.8 | async-start | bytes 3932160 | tf_op jit(solution)/shard_map/reduce_scatter | solution.py:32
  483.3 6.4 copy-start.63
  502.7 24.4 %copy-start.27 = (f32[256,32]{0,1:T(8,128)S(1)}, f32[256,32]{0,1:T(8,128)}, u32[]{:S(2)}) copy-start(f32[256,32]{0,1:T(8,128)} %copy-done.26) | copy-start | bytes 98308
  502.7 24.4 %copy-start.28 = (f32[256,32]{0,1:T(8,128)S(1)}, f32[256,32]{0,1:T(8,128)}, u32[]{:S(2)}) copy-start(f32[256,32]{0,1:T(8,128)} %get-tuple-element.113) | copy-start | bytes 98308
  502.7 26.0 %copy-start.30 = (f32[256,16]{0,1:T(8,128)S(1)}, f32[256,16]{0,1:T(8,128)}, u32[]{:S(2)}) copy-start(f32[256,16]{0,1:T(8,128)} %copy-done.29) | copy-start | bytes 49156
  502.7 26.0 %copy-start.56 = (f32[64]{0:T(128)S(1)}, f32[64]{0:T(128)}, u32[]{:S(2)}) copy-start(f32[64]{0:T(128)} %param.21) | copy-start | bytes 772
  502.7 27.9 %copy-start.10 = (bf16[256,1024]{1,0:T(8,128)(2,1)S(1)}, bf16[256,1024]{1,0:T(8,128)(2,1)}, u32[]{:S(2)}) copy-start(bf16[256,1024]{1,0:T(8,128)(2,1)} %copy-done.9) | copy-start | bytes 1572868
  502.7 28.7 %copy-start.41 = (f32[256,16]{0,1:T(8,128)S(1)}, f32[256,16]{0,1:T(8,128)}, u32[]{:S(2)}) copy-start(f32[256,16]{0,1:T(8,128)} %get-tuple-element.107) | copy-start | bytes 49156
  502.7 232.3 %all-reduce.6.cloned.1.call-start = ((), (), s32[]{:S(2)}) async-start(), calls=%async_computation.9 | async-start | bytes 25427968 | tf_op jit(solution)/shard_map/psum | solution.py:343
  528.7 6.7 copy-start.4
  528.7 6.7 copy-start.23
  548.1 82.4 %copy-start.57 = (f32[256]{0:T(256)S(1)}, f32[256]{0:T(256)}, u32[]{:S(2)}) copy-start(f32[256]{0:T(256)} %get-tuple-element.116) | copy-start | bytes 3076
  735.0 6.3 copy-start.20
  (29 other events, 102.6 us)
Sparse Core Ops, SparseCore 0:
  19.6 37.1 all-gather.1
  483.1 33.0 reduce-scatter.2
  518.8 38.0 reduce-scatter.4
  564.9 170.0 all-reduce.5
where the time goes:
time: 766 us; the launch traced here: 753 us
  waiting for transfers between devices  286 us (37%)
  matrix products  166 us (22%)
  local copies, waits for them, and re-layouts  113 us (15%)
  blocking collectives  65.3 us (9%)
  other arithmetic  60.4 us (8%)
  starting transfers between devices  47.2 us (6%)
  between operations  15.3 us (2%)
    psum x1, waiting for transfers between devices, body(): lax.psum((attn_gain_local, query_local, key_local, value_local, query_gai...  102 us
    psum x1, blocking collectives, body(): lax.psum((attn_gain_local, query_local, key_local, value_local, query_gai...  65.3 us
    all_to_all x1, waiting for transfers between devices, body(): lax.all_to_all(send_grads, 'expert', split_axis=0, concat_axis=0, tiled=T...  56.2 us
    all_to_all x1, waiting for transfers between devices, body(): lax.all_to_all(result.astype(jnp.bfloat16), 'expert', split_axis=0, conca...  53.8 us
    all_to_all x1, waiting for transfers between devices, body(): lax.all_to_all(d_rows.astype(jnp.bfloat16), 'expert', split_axis=0, conca...  42.6 us
    unnamed x147, local copies, waits for them, and re-layouts  24.3 us
    dot_general x1, matrix products, attend_back(): jnp.einsum('kgqs,skd->qkgd', d_raw, key_rows, preferred_element_type=jnp....  24 us
    dot_general x1, matrix products, attend_back(): jnp.einsum('kgqs,qkgd->skd', d_raw, query_four, preferred_element_type=jn...  23.5 us
  transfers between devices with their start and end apart: 8, of which 6 were waited for; matrix products, arithmetic and copies ran while one was open for 26% of the time, Pallas kernels for 0%

commit v1 on v0

v1 whole, which is shorter than its diff:
```python
import jax
import jax.numpy as jnp
from jax import lax
from jax.experimental import pallas as pl
from jax.experimental.pallas import tpu as pltpu
from jax.sharding import PartitionSpec as P

CAP = 80
SIDE = 4
TOP = 8
BF = jnp.bfloat16
F32 = jnp.float32
MIB = 1024 * 1024

epsilon = 1e-06
theta = 10000.0
masked = -1e30


def place(x, y, core):
    return (x * SIDE + y) * 2 + core


def step_pairs(dx, dy, flip=0):
    pairs = []
    for x in range(SIDE):
        for y in range(SIDE):
            for core in range(2):
                there = place((x + dx) % SIDE, (y + dy) % SIDE, core ^ flip)
                pairs.append((place(x, y, core), there))
    return pairs


def along_x(value, step):
    return lax.ppermute(value, "expert", step_pairs(step, 0))


def along_y(value, step):
    return lax.ppermute(value, "expert", step_pairs(0, step))


def along_z(value, step):
    return lax.ppermute(value, "dp", [(i, (i + step) % SIDE) for i in range(SIDE)])


def swap_core(value):
    return lax.ppermute(value, "expert", step_pairs(0, 0, 1))


def plane_groups():
    return [[2 * chip + core for chip in range(SIDE * SIDE)] for core in range(2)]


def tied(*values):
    return lax.optimization_barrier(values)


def ring_start(parts, move):
    half = parts.shape[1] // 2
    return move(parts[2, :half], 1), move(parts[2, half:], -1)


def ring_middle(parts, first, move):
    half = parts.shape[1] // 2
    ahead, behind = first
    up = jnp.concatenate([parts[1, :half] + ahead, parts[1, half:]], axis=0)
    down = jnp.concatenate([parts[3, :half], parts[3, half:] + behind], axis=0)
    return move(up, 1), move(down, -1)


def ring_end(parts, second):
    return parts[0].astype(F32) + second[0].astype(F32) + second[1].astype(F32)


def plane_sum(part_a, part_b):
    for move_a, move_b in ((along_x, along_y), (along_y, along_x)):
        first_a, first_b = ring_start(part_a, move_a), ring_start(part_b, move_b)
        second_a = ring_middle(part_a, first_a, move_a)
        second_b = ring_middle(part_b, first_b, move_b)
        part_a, part_b = ring_end(part_a, second_a), ring_end(part_b, second_b)
        if part_a.ndim == 3:
            part_a, part_b = part_a.astype(BF), part_b.astype(BF)
    return part_a, part_b


def block_at(whole, index, rows):
    return lax.dynamic_slice_in_dim(whole, (index % SIDE) * rows, rows, axis=0)


def scatter_sum(whole, tail, here, move):
    rows = whole.shape[0] // SIDE
    total = jnp.concatenate([block_at(whole, here, rows), tail], axis=0).astype(F32)
    for r, step in ((1, 1), (2, 2), (3, -1)):
        send = jnp.concatenate([block_at(whole, here + r, rows), tail], axis=0)
        total = total + move(send, step).astype(F32)
    total = total.astype(BF)
    return total[:rows], total[rows:]


def gather_rows(part, here, move):
    rows = part.shape[0]
    whole = jnp.zeros((SIDE * rows,) + part.shape[1:], part.dtype)
    pieces = [part, move(part, -1), move(part, 2), move(part, 1)]
    for r, piece in enumerate(pieces):
        whole = lax.dynamic_update_slice_in_dim(whole, piece, ((here + r) % SIDE) * rows, 0)
    return whole


def nt(a, b):
    return lax.dot_general(a, b, (((1,), (1,)), ((), ())), preferred_element_type=F32)


def tn(a, b):
    return lax.dot_general(a, b, (((0,), (0,)), ((), ())), preferred_element_type=F32)


def nn(a, b):
    return jnp.dot(a, b, preferred_element_type=F32)


def head_mean(values, head):
    n = values.shape[1]
    same = lax.broadcasted_iota(jnp.int32, (n, n), 0) // head == (
        lax.broadcasted_iota(jnp.int32, (n, n), 1) // head
    )
    ones = jnp.where(same, 1.0, 0.0).astype(BF)
    high = values.astype(BF)
    rest = values - high.astype(F32)
    middle = rest.astype(BF)
    low = (rest - middle.astype(F32)).astype(BF)
    return (nn(high, ones) + nn(middle, ones) + nn(low, ones)) * (1.0 / head)


def turn(values, cosine, sine, head):
    half = head // 2
    pieces = []
    lane = lax.broadcasted_iota(jnp.int32, (values.shape[0], 128), 1) % head
    for at in range(0, values.shape[1], 128):
        piece = values[:, at : at + 128]
        other = jnp.where(
            lane < half, pltpu.roll(piece, 128 - half, 1), pltpu.roll(piece, half, 1)
        )
        pieces.append(piece * cosine + other * sine)
    return pieces[0] if len(pieces) == 1 else jnp.concatenate(pieces, axis=1)


def allowed_keys(start, block, rows):
    length = (block + 1) * rows
    key = lax.broadcasted_iota(jnp.int32, (rows, length), 1)
    query = lax.broadcasted_iota(jnp.int32, (rows, length), 0) + block * rows
    return (key <= query) & (key >= start)


def attend_kernel(
    at_ref,
    x0_ref,
    x1_ref,
    x2_ref,
    x3_ref,
    gain_ref,
    wq_ref,
    wk_ref,
    wv_ref,
    qgain_ref,
    kgain_ref,
    cos_ref,
    sin_ref,
    start_ref,
    normed_ref,
    q_ref,
    k_ref,
    v_ref,
    qraw_ref,
    kraw_ref,
    out_ref,
    head,
):
    z = at_ref[0]
    rows = x0_ref.shape[0]
    for r, x_ref in enumerate((x0_ref, x1_ref, x2_ref, x3_ref)):
        here = pl.ds(pl.multiple_of(lax.rem(z - r + SIDE, SIDE) * rows, rows), rows)
        x = x_ref[...].astype(F32)
        scale = lax.rsqrt(jnp.mean(x * x, axis=-1, keepdims=True) + epsilon)
        normed = (x * scale * gain_ref[...]).astype(BF)
        normed_ref[here] = normed
        cosine, sine = cos_ref[here], sin_ref[here]
        q_raw = nn(normed, wq_ref[...])
        k_raw = nn(normed, wk_ref[...])
        v_ref[here] = nn(normed, wv_ref[...]).astype(BF)
        qraw_ref[here] = q_raw
        kraw_ref[here] = k_raw
        q = q_raw * lax.rsqrt(head_mean(q_raw * q_raw, head) + epsilon) * qgain_ref[...]
        k = k_raw * lax.rsqrt(head_mean(k_raw * k_raw, head) + epsilon) * kgain_ref[...]
        q_ref[here] = turn(q, cosine, sine, head).astype(BF) * (head**-0.5)
        k_ref[here] = turn(k, cosine, sine, head).astype(BF)
    for i in range(SIDE):
        length = (i + 1) * rows
        keep = allowed_keys(start_ref[i * rows : (i + 1) * rows], i, rows)
        outs = []
        for h in range(q_ref.shape[1] // head):
            j = h // 2
            q = q_ref[i * rows : (i + 1) * rows, h * head : (h + 1) * head]
            k = k_ref[:length, j * head : (j + 1) * head]
            v = v_ref[:length, j * head : (j + 1) * head]
            expo = jnp.where(keep, jnp.exp(nt(q, k)), 0.0)
            total = jnp.sum(expo, axis=1, keepdims=True)
            outs.append(nn(expo.astype(BF), v) / total)
        out_ref[lax.rem(i - z + SIDE, SIDE)] = jnp.concatenate(outs, axis=1).astype(BF)


def attend(at, x_rel, gain, query_proj, key_proj, value_proj, qgain, kgain, cosine, sine, start):
    rows, width = x_rel[0].shape
    length = SIDE * rows
    head = qgain.shape[0]
    q_cols, k_cols = query_proj.shape[1] // SIDE, key_proj.shape[1] // SIDE

    def whole(shape):
        return pl.BlockSpec(shape, lambda g, at: (0,) * len(shape))

    def columns(cols):
        return pl.BlockSpec((width, cols), lambda g, at: (0, at[0]))

    shapes = [
        ((length, width), BF),
        ((length, q_cols), BF),
        ((length, k_cols), BF),
        ((length, k_cols), BF),
        ((length, q_cols), F32),
        ((length, k_cols), F32),
        ((SIDE, rows, q_cols), BF),
    ]

    def kernel(*refs):
        attend_kernel(*refs, head=head)

    return pl.pallas_call(
        kernel,
        grid_spec=pltpu.PrefetchScalarGridSpec(
            num_scalar_prefetch=1,
            grid=(1,),
            in_specs=[whole((rows, width))] * SIDE
            + [whole((1, width)), columns(q_cols), columns(k_cols), columns(k_cols)]
            + [whole((1, q_cols)), whole((1, k_cols))]
            + [whole((length, 128)), whole((length, 128)), whole((length, 1))],
            out_specs=[whole(shape) for shape, _ in shapes],
        ),
        out_shape=[jax.ShapeDtypeStruct(shape, dtype) for shape, dtype in shapes],
        compiler_params=pltpu.CompilerParams(vmem_limit_bytes=48 * MIB),
        cost_estimate=pl.CostEstimate(
            flops=6_000_000_000, bytes_accessed=12_000_000, transcendentals=4_000_000
        ),
        name="attend",
    )(
        at,
        *x_rel,
        gain[None],
        query_proj,
        key_proj,
        value_proj,
        jnp.tile(qgain, q_cols // head)[None],
        jnp.tile(kgain, k_cols // head)[None],
        cosine,
        sine,
        start,
    )


def norm_back(raw, upstream, gain, head):
    scale = lax.rsqrt(head_mean(raw * raw, head) + epsilon)
    gain_grad = jnp.sum(upstream * raw * scale, axis=0, keepdims=True)
    weighted = upstream * gain
    inner = head_mean(weighted * raw, head)
    return scale * weighted - raw * (scale * scale * scale) * inner, gain_grad


def attend_back_kernel(
    at_ref,
    d0_ref,
    d1_ref,
    d2_ref,
    d3_ref,
    q_ref,
    k_ref,
    v_ref,
    qraw_ref,
    kraw_ref,
    qgain_ref,
    kgain_ref,
    cos_ref,
    sin_ref,
    start_ref,
    dqkv_ref,
    gains_ref,
    do_scr,
    dk_scr,
    dv_scr,
    head,
):
    z = at_ref[0]
    rows = d0_ref.shape[0]
    q_cols, k_cols = q_ref.shape[1], k_ref.shape[1]
    for r, d_ref in enumerate((d0_ref, d1_ref, d2_ref, d3_ref)):
        here = pl.ds(pl.multiple_of(lax.rem(z - r + SIDE, SIDE) * rows, rows), rows)
        do_scr[here] = d_ref[...]
    gains_ref[...] = jnp.zeros_like(gains_ref)
    for i in reversed(range(SIDE)):
        length = (i + 1) * rows
        here = slice(i * rows, (i + 1) * rows)
        keep = allowed_keys(start_ref[here], i, rows)
        d_queries = []
        for j in range(k_cols // head):
            k = k_ref[:length, j * head : (j + 1) * head]
            v = v_ref[:length, j * head : (j + 1) * head]
            d_key, d_value = 0.0, 0.0
            for h in (2 * j, 2 * j + 1):
                q = q_ref[here, h * head : (h + 1) * head]
                grad = do_scr[here, h * head : (h + 1) * head]
                expo = jnp.where(keep, jnp.exp(nt(q, k)), 0.0)
                probs = expo * (1.0 / jnp.sum(expo, axis=1, keepdims=True))
                d_probs = nt(grad, v)
                inner = jnp.sum(probs * d_probs, axis=1, keepdims=True)
                d_scores = (probs * (d_probs - inner)).astype(BF)
                d_queries.append(nn(d_scores, k) * (head**-0.5))
                d_key = d_key + tn(d_scores, q)
                d_value = d_value + tn(probs.astype(BF), grad)
            if i == SIDE - 1:
                dk_scr[j] = d_key
                dv_scr[j] = d_value
            else:
                dk_scr[j, :length] += d_key
                dv_scr[j, :length] += d_value
        d_query = jnp.concatenate(d_queries, axis=1)
        d_query = turn(d_query, cos_ref[here], -sin_ref[here], head)
        d_raw, d_gain = norm_back(qraw_ref[here], d_query, qgain_ref[...], head)
        dqkv_ref[here, :q_cols] = d_raw.astype(BF)
        gains_ref[0:1] += d_gain
        d_key = jnp.concatenate([dk_scr[0, here], dk_scr[1, here]], axis=1)
        d_key = turn(d_key, cos_ref[here], -sin_ref[here], head)
        d_raw, d_gain = norm_back(kraw_ref[here], d_key, kgain_ref[...], head)
        dqkv_ref[here, q_cols : q_cols + k_cols] = d_raw.astype(BF)
        gains_ref[1:2, :k_cols] += d_gain
        d_value = jnp.concatenate([dv_scr[0, here], dv_scr[1, here]], axis=1)
        dqkv_ref[here, q_cols + k_cols :] = d_value.astype(BF)


def attend_back(at, d_rel, q, k, v, q_raw, k_raw, qgain, kgain, cosine, sine, start):
    rows = d_rel[0].shape[0]
    length, q_cols = q.shape
    k_cols = k.shape[1]
    head = qgain.shape[0]

    def whole(shape):
        return pl.BlockSpec(shape, lambda g, at: (0,) * len(shape))

    def kernel(*refs):
        attend_back_kernel(*refs, head=head)

    operands = [
        *d_rel,
        q,
        k,
        v,
        q_raw,
        k_raw,
        jnp.tile(qgain, q_cols // head)[None],
        jnp.tile(kgain, k_cols // head)[None],
        cosine,
        sine,
        start,
    ]
    shapes = [((length, q_cols + 2 * k_cols), BF), ((8, q_cols), F32)]
    return pl.pallas_call(
        kernel,
        grid_spec=pltpu.PrefetchScalarGridSpec(
            num_scalar_prefetch=1,
            grid=(1,),
            in_specs=[whole(a.shape) for a in operands],
            out_specs=[whole(shape) for shape, _ in shapes],
            scratch_shapes=[
                pltpu.VMEM((length, q_cols), BF),
                pltpu.VMEM((k_cols // head, length, head), F32),
                pltpu.VMEM((k_cols // head, length, head), F32),
            ],
        ),
        out_shape=[jax.ShapeDtypeStruct(shape, dtype) for shape, dtype in shapes],
        compiler_params=pltpu.CompilerParams(vmem_limit_bytes=48 * MIB),
        cost_estimate=pl.CostEstimate(
            flops=8_000_000_000, bytes_accessed=8_000_000, transcendentals=4_000_000
        ),
        name="attend_back",
    )(at, *operands)


def moe_kernel(
    at_ref,
    rows_ref,
    cot_ref,
    router_ref,
    gate_ref,
    up_ref,
    down_ref,
    out_a_ref,
    out_b_ref,
    back_a_ref,
    back_b_ref,
    x_ref,
    dgate_ref,
    dup_ref,
    hidden_ref,
    slot_ref,
    pick_scr,
    up_scr,
    gate_scr,
    dgs_scr,
    o_scr,
    b_scr,
):
    tokens = rows_ref.shape[2]
    width = rows_ref.shape[3]
    half = width // 2
    experts = router_ref.shape[0]
    y_here, chip = at_ref[2], at_ref[3]
    pick_iota = lax.broadcasted_iota(jnp.int32, (CAP, tokens), 0).astype(F32)
    expert_iota = lax.broadcasted_iota(jnp.int32, (experts, tokens), 0).astype(F32)
    chip_row = lax.broadcasted_iota(jnp.int32, (SIDE * SIDE, half), 0) == chip
    tri = (
        lax.broadcasted_iota(jnp.int32, (tokens, tokens), 0)
        <= lax.broadcasted_iota(jnp.int32, (tokens, tokens), 1)
    ).astype(BF)
    mine = [at_ref[4 + j].astype(F32) for j in range(2)]
    members, gates = [], []
    for s in range(SIDE):
        rows = rows_ref[0, s]
        routes = cot_ref[0, s, tokens : tokens + 16, :tokens].astype(F32)
        logits = nt(router_ref[...], rows)
        chosen = expert_iota == routes[0:1]
        for k in range(1, TOP):
            chosen = chosen | (expert_iota == routes[k : k + 1])
        top = jnp.max(jnp.where(chosen, logits, masked), axis=0, keepdims=True)
        expo = jnp.where(chosen, jnp.exp(jnp.minimum(logits - top, 0.0)), 0.0)
        share = expo / jnp.sum(expo, axis=0, keepdims=True)
        for j in range(2):
            picked = expert_iota == mine[j]
            gates.append(jnp.sum(jnp.where(picked, share, 0.0), axis=0, keepdims=True))
            members.append(jnp.sum(jnp.where(picked & chosen, 1.0, 0.0), axis=0, keepdims=True))
    member_all = jnp.concatenate(members, axis=0)
    rank_all = nn(member_all.astype(BF), tri)
    rank_all = jnp.where(member_all > 0.5, rank_all - 1.0, -1.0)
    for s in range(SIDE):
        for j in range(2):
            n = s * 2 + j
            hit = pick_iota == rank_all[n : n + 1]
            pick_scr[s, j * CAP : (j + 1) * CAP] = jnp.where(hit, 1.0, 0.0).astype(BF)
            gate_scr[j, s * CAP : (s + 1) * CAP] = jnp.sum(
                jnp.where(hit, gates[n], 0.0), axis=1, keepdims=True
            )
        pick = pick_scr[s]
        took = nn(pick, rows_ref[0, s]).astype(BF)
        took_up = nn(pick, cot_ref[0, s, :tokens]).astype(BF)
        for j in range(2):
            x_ref[j, s * CAP : (s + 1) * CAP] = took[j * CAP : (j + 1) * CAP]
            up_scr[j, s * CAP : (s + 1) * CAP] = took_up[j * CAP : (j + 1) * CAP]
    for j in range(2):
        x = x_ref[j]
        gate_act = nn(x, gate_ref[j])
        up_act = nn(x, up_ref[j])
        sig = 1.0 / (1.0 + jnp.exp(-gate_act))
        silu = gate_act * sig
        hidden = (silu * up_act).astype(BF)
        hidden_ref[j] = hidden
        upstream = up_scr[j].astype(F32)
        gate_col = gate_scr[j]
        slot = (gate_col * upstream).astype(BF)
        slot_ref[j] = slot
        result = nn(hidden, down_ref[j]).astype(BF).astype(F32)
        dgs_scr[j] = jnp.sum(upstream * result, axis=1, keepdims=True)
        gated = (gate_col * result).astype(BF)
        d_hidden = nt(slot, down_ref[j])
        d_gate = (d_hidden * up_act * (sig + silu * (1.0 - sig))).astype(BF)
        d_up = (d_hidden * silu).astype(BF)
        dgate_ref[j] = d_gate
        dup_ref[j] = d_up
        d_rows = (nt(d_gate, gate_ref[j]) + nt(d_up, up_ref[j])).astype(BF)
        for s in range(SIDE):
            o_scr[s, j * CAP : (j + 1) * CAP] = gated[s * CAP : (s + 1) * CAP]
            b_scr[s, j * CAP : (j + 1) * CAP] = d_rows[s * CAP : (s + 1) * CAP]
    for s in range(SIDE):
        dy = lax.rem(s - y_here + SIDE, SIDE)
        pick = pick_scr[s]
        back = tn(pick, b_scr[s]).astype(BF)
        back_a_ref[0, dy, :tokens] = back[:, :half]
        back_b_ref[dy, 0, :tokens] = back[:, half:]
        out = tn(pick, o_scr[s]).astype(BF)
        out_a_ref[0, dy] = out[:, :half]
        out_b_ref[dy, 0] = out[:, half:]
        found = []
        for j in range(2):
            hit = pick_iota == rank_all[s * 2 + j : s * 2 + j + 1]
            col = dgs_scr[j, s * CAP : (s + 1) * CAP]
            found.append(jnp.sum(jnp.where(hit, col, 0.0), axis=0, keepdims=True))
        found = jnp.where(chip_row, jnp.concatenate(found, axis=1), 0.0)
        high = found.astype(BF)
        back_a_ref[0, dy, tokens:] = high
        back_b_ref[dy, 0, tokens:] = (found - high.astype(F32)).astype(BF)


def moe(at, rows, cot, router_t, gate, up, down):
    _, _, tokens, width = rows.shape
    padded = cot.shape[2]
    ff = gate.shape[2]
    slots = SIDE * CAP
    half = width // 2

    def whole(shape):
        return pl.BlockSpec(shape, lambda g, at: (0,) * len(shape))

    def source(g, at):
        return (at[1] + 2 + g) % SIDE

    def first(g, at):
        return ((2 + g) % SIDE, 0, 0, 0)

    def second(g, at):
        return (0, (2 + g) % SIDE, 0, 0)

    kept = [width, ff, ff, ff, width]
    return pl.pallas_call(
        moe_kernel,
        grid_spec=pltpu.PrefetchScalarGridSpec(
            num_scalar_prefetch=1,
            grid=(SIDE,),
            in_specs=[
                pl.BlockSpec((1, SIDE, tokens, width), lambda g, at: (source(g, at), 0, 0, 0)),
                pl.BlockSpec((1, SIDE, padded, width), lambda g, at: (source(g, at), 0, 0, 0)),
                whole(router_t.shape),
                whole(gate.shape),
                whole(up.shape),
                whole(down.shape),
            ],
            out_specs=[
                pl.BlockSpec((1, SIDE, tokens, half), first),
                pl.BlockSpec((SIDE, 1, tokens, half), second),
                pl.BlockSpec((1, SIDE, padded, half), first),
                pl.BlockSpec((SIDE, 1, padded, half), second),
            ]
            + [pl.BlockSpec((2, slots, n), lambda g, at: (0, g, 0)) for n in kept],
            scratch_shapes=[
                pltpu.VMEM((SIDE, 2 * CAP, tokens), BF),
                pltpu.VMEM((2, slots, width), BF),
                pltpu.VMEM((2, slots, 1), F32),
                pltpu.VMEM((2, slots, 1), F32),
                pltpu.VMEM((SIDE, 2 * CAP, width), BF),
                pltpu.VMEM((SIDE, 2 * CAP, width), BF),
            ],
        ),
        out_shape=[jax.ShapeDtypeStruct((SIDE, SIDE, tokens, half), BF)] * 2
        + [jax.ShapeDtypeStruct((SIDE, SIDE, padded, half), BF)] * 2
        + [jax.ShapeDtypeStruct((2, SIDE * slots, n), BF) for n in kept],
        compiler_params=pltpu.CompilerParams(vmem_limit_bytes=60 * MIB),
        cost_estimate=pl.CostEstimate(
            flops=22_000_000_000, bytes_accessed=60_000_000, transcendentals=0
        ),
        name="moe",
    )(at, rows, cot, router_t, gate, up, down)


def rms_apply(values, gain):
    scale = lax.rsqrt(jnp.mean(values * values, axis=-1, keepdims=True) + epsilon)
    return (values * scale * gain, scale)


def rms_back(values, scale, gain, upstream):
    weighted = upstream * gain
    inner = jnp.mean(weighted * values, axis=-1, keepdims=True)
    return scale * weighted - values * (scale * scale * scale) * inner


def body(
    block_input,
    attn_norm_gain,
    query_proj,
    key_proj,
    value_proj,
    query_gain,
    key_gain,
    output_proj,
    ffn_norm_gain,
    router_proj,
    expert_routes,
    document_ids,
    expert_gate,
    expert_up,
    expert_down,
    cotangent,
):
    tokens, width = block_input.shape[1:]
    head = query_gain.shape[0]
    experts_all = router_proj.shape[1]
    z = lax.axis_index("dp")
    expert_at = lax.axis_index("expert")
    chip, core = expert_at // 2, expert_at % 2
    x_at, y_at = chip // SIDE, chip % SIDE
    at = jnp.stack([z, x_at, y_at, chip, expert_at, expert_at + 1 - 2 * core]).astype(jnp.int32)

    own = block_input[0]
    x_rel = [own, along_z(own, 1), along_z(own, 2), along_z(own, -1)]
    routes = expert_routes[0]
    route_rows = jnp.full((16, width), -1.0, BF)
    route_rows = lax.dynamic_update_slice(route_rows, routes.T.astype(BF), (0, 0))
    cot_all = lax.all_gather(
        jnp.concatenate([cotangent[0], route_rows], axis=0),
        "expert",
        axis_index_groups=plane_groups(),
    ).reshape(SIDE, SIDE, tokens + 16, width)

    doc = document_ids[0]
    below_one = jnp.sum((doc < 1).astype(jnp.int32))
    below_two = jnp.sum((doc < 2).astype(jnp.int32))
    start = jnp.where(doc < 1, 0, jnp.where(doc < 2, below_one, below_two)).astype(jnp.int32)
    position = (jnp.arange(doc.shape[0], dtype=jnp.int32) - start).astype(F32)
    frequency = theta ** (-jnp.arange(head // 2, dtype=F32) * 2.0 / head)
    angles = position[:, None] * frequency[None, :]
    cosine, sine = jnp.cos(angles), jnp.sin(angles)
    cosine = jnp.tile(cosine, (1, 4))
    sine = jnp.tile(jnp.concatenate([-sine, sine], axis=1), (1, 2))
    start = start[:, None]

    normed_all, q, k, v, q_raw, k_raw, out_rel = attend(
        at,
        x_rel,
        attn_norm_gain,
        query_proj,
        key_proj,
        value_proj,
        query_gain,
        key_gain,
        cosine,
        sine,
        start,
    )
    q_cols, k_cols = q.shape[1], k.shape[1]

    def from_heads(pieces):
        whole = jnp.zeros((tokens, SIDE, pieces[0].shape[1]), pieces[0].dtype)
        for r, piece in enumerate(pieces):
            whole = lax.dynamic_update_slice(whole, piece[:, None], (0, (z - r) % SIDE, 0))
        return whole

    attended = from_heads(
        [out_rel[0], along_z(out_rel[1], 1), along_z(out_rel[2], 2), along_z(out_rel[3], -1)]
    ).reshape(tokens, SIDE * q_cols)
    inputs = own.astype(F32)
    middle = inputs + nn(attended, output_proj)
    normed_two, scale_two = rms_apply(middle, ffn_norm_gain)
    normed_two = normed_two.astype(BF)
    rows_all = lax.all_gather(
        normed_two, "expert", axis_index_groups=plane_groups()
    ).reshape(SIDE, SIDE, tokens, width)
    gate_two = jnp.concatenate([expert_gate, swap_core(expert_gate)], axis=0)
    up_two = jnp.concatenate([expert_up, swap_core(expert_up)], axis=0)
    down_two = jnp.concatenate([expert_down, swap_core(expert_down)], axis=0)
    out_a, out_b, back_a, back_b, kept_x, kept_dg, kept_du, kept_h, kept_s = moe(
        at, rows_all, cot_all, router_proj.T, gate_two, up_two, down_two
    )

    logits = nn(normed_two, router_proj)
    experts = jnp.arange(experts_all, dtype=jnp.int32)
    chosen = jnp.any(routes[:, :, None] == experts[None, None, :], axis=1)
    logits = jnp.where(chosen, logits, masked)
    expo = jnp.where(chosen, jnp.exp(logits - jnp.max(logits, axis=-1, keepdims=True)), 0.0)
    gate_rows = expo / jnp.sum(expo, axis=-1, keepdims=True)

    sum_a, sum_b = plane_sum(back_a, back_b)
    back_sum = jnp.concatenate([sum_a[:tokens], sum_b[:tokens]], axis=1)
    d_gates = (sum_a[tokens:] + sum_b[tokens:]).reshape(SIDE * SIDE, 2, tokens)
    d_gates = jnp.where(core == 0, d_gates, d_gates[:, ::-1]).reshape(experts_all, tokens).T
    d_gates = jnp.where(chosen, d_gates, 0.0)

    def slots_grad(a, b):
        return jnp.einsum("jrd,jrf->jdf", a, b, preferred_element_type=F32).astype(BF)

    whole_w = jnp.stack(
        [slots_grad(kept_x, kept_dg), slots_grad(kept_x, kept_du), slots_grad(kept_s, kept_h)],
        axis=1,
    )
    whole_w = (whole_w[0].astype(F32) + swap_core(whole_w[1]).astype(F32)).astype(BF)
    expert_sum = lax.psum_scatter(whole_w, "dp", scatter_dimension=1, tiled=True).astype(F32)
    gate_grad, up_grad = expert_sum[0:1], expert_sum[1:2]
    down_grad = jnp.transpose(expert_sum[2:3], (0, 2, 1))

    upstream = cotangent[0].astype(F32)
    d_chosen = gate_rows * (d_gates - jnp.sum(gate_rows * d_gates, axis=-1, keepdims=True))
    d_logits = d_chosen.astype(BF)
    router_local = tn(d_logits, normed_two)
    d_normed_two = back_sum + nt(d_logits, router_proj)
    ffn_gain_local = jnp.sum(d_normed_two * middle * scale_two, axis=0)
    d_middle = upstream + rms_back(middle, scale_two, ffn_norm_gain, d_normed_two)
    d_branch = d_middle.astype(BF)
    d_attended = nt(d_branch, output_proj).astype(BF).reshape(tokens, SIDE, q_cols)

    def heads_of(r):
        return lax.dynamic_index_in_dim(d_attended, (z + r) % SIDE, axis=1, keepdims=False)

    d_rel = [heads_of(0)] + [along_z(heads_of(r), s) for r, s in ((1, 1), (2, 2), (3, -1))]
    dqkv, gains = attend_back(
        at, d_rel, q, k, v, q_raw, k_raw, query_gain, key_gain, cosine, sine, start
    )
    output_local = tn(attended, d_branch)
    early = jnp.concatenate(
        [output_local, router_local, jnp.pad(ffn_gain_local[None], ((0, 15), (0, 0)))], axis=0
    )
    early = lax.psum(early.astype(BF), ("dp", "expert"))

    local = tn(normed_all, dqkv).astype(BF)
    tail = jnp.concatenate([gains[0], gains[1]])
    tail = jnp.pad(tail[None], ((0, 15), (0, 0))).astype(BF)
    half = width // 2
    mine = lax.dynamic_slice_in_dim(local, core * half, half, axis=0)
    other = lax.dynamic_slice_in_dim(local, (1 - core) * half, half, axis=0)
    got = swap_core(jnp.concatenate([other, tail], axis=0)).astype(F32)
    part = (mine.astype(F32) + got[:half]).astype(BF)
    tail = (tail.astype(F32) + got[half:]).astype(BF)
    part, tail = scatter_sum(part, tail, x_at, along_x)
    part, tail = scatter_sum(part, tail, y_at, along_y)
    part = gather_rows(part, y_at, along_y)
    part = gather_rows(part, x_at, along_x)
    part = jnp.concatenate([part, tail], axis=0)
    blocks = gather_heads(part, z)
    tails = jnp.sum(blocks[:, half].astype(F32), axis=0)
    query_gain_sum = jnp.sum(tails[:q_cols].reshape(-1, head), axis=0)
    key_gain_sum = jnp.sum(tails[q_cols : q_cols + k_cols].reshape(-1, head), axis=0)
    blocks = blocks[:, :half]
    blocks_other = swap_core(blocks)
    both = jnp.where(
        core == 0, jnp.stack([blocks, blocks_other]), jnp.stack([blocks_other, blocks])
    )
    both = both.transpose(0, 2, 1, 3).reshape(width, SIDE, q_cols + 2 * k_cols).astype(F32)
    query_sum = both[:, :, :q_cols].reshape(width, -1)
    key_sum = both[:, :, q_cols : q_cols + k_cols].reshape(width, -1)
    value_sum = both[:, :, q_cols + k_cols :].reshape(width, -1)
    attn_gain_sum = (
        jnp.sum(query_sum * query_proj.astype(F32), axis=1)
        + jnp.sum(key_sum * key_proj.astype(F32), axis=1)
        + jnp.sum(value_sum * value_proj.astype(F32), axis=1)
    ) / attn_norm_gain

    def block_of(r):
        return block_at(dqkv, z + r, tokens)

    back = from_heads(
        [block_of(0)] + [along_z(block_of(r), s) for r, s in ((1, 1), (2, 2), (3, -1))]
    )
    d_query = back[:, :, :q_cols].reshape(tokens, -1)
    d_key = back[:, :, q_cols : q_cols + k_cols].reshape(tokens, -1)
    d_value = back[:, :, q_cols + k_cols :].reshape(tokens, -1)
    d_normed = nt(d_query, query_proj) + nt(d_key, key_proj) + nt(d_value, value_proj)
    scale_one = lax.rsqrt(jnp.mean(inputs * inputs, axis=-1, keepdims=True) + epsilon)
    input_grad = d_middle + rms_back(inputs, scale_one, attn_norm_gain, d_normed)

    out_a, out_b, _ = tied(out_a, out_b, d_branch)
    out_a, out_b = plane_sum(out_a, out_b)
    block_output = (middle + jnp.concatenate([out_a, out_b], axis=1)).astype(BF)

    early = early.astype(F32)
    return (
        block_output[None],
        input_grad[None],
        attn_gain_sum,
        query_sum,
        key_sum,
        value_sum,
        query_gain_sum,
        key_gain_sum,
        early[:width],
        early[width + experts_all],
        early[width : width + experts_all].T,
        gate_grad,
        up_grad,
        down_grad,
    )


def gather_heads(part, z):
    pieces = [part, along_z(part, 1), along_z(part, 2), along_z(part, -1)]
    whole = jnp.zeros((SIDE,) + part.shape, part.dtype)
    for r, piece in enumerate(pieces):
        whole = lax.dynamic_update_index_in_dim(whole, piece, (z - r) % SIDE, 0)
    return whole


def solution(mesh):
    tokens = P("expert", "dp", None)
    experts = P("expert", None, None)
    return jax.shard_map(
        body,
        mesh=mesh,
        in_specs=(tokens,)
        + (P(),) * 9
        + (tokens, P("expert", None), experts, experts, experts, tokens),
        out_specs=(tokens, tokens)
        + (P(),) * 9
        + (tokens, tokens, P("expert", None, "dp")),
        check_vma=False,
    )
```

time: 766 us -> 623 us (0.81)
  matrix products: 166 us -> 31.8 us
  blocking collectives: 65.3 us -> 0 us
  Pallas kernels: 0 us -> 64.1 us
  waiting for transfers between devices: 286 us -> 232 us
  starting transfers between devices: 47.2 us -> 96.5 us
  local copies, waits for them, and re-layouts: 113 us -> 103 us
  other arithmetic: 60.4 us -> 70 us
    all_to_all x4 -> x0, waiting for transfers between devices: 175 us -> none  [the longest x1 56.2 us: body(): lax.all_to_all(send_grads, 'expert', split_axis=0, concat_axis=0, tiled=T...]
    dot_general x29 -> x13, matrix products: 156 us -> 31.8 us  [the longest x3 18.8 us: slots_grad(): jnp.einsum('jrd,jrf->jdf', a, b, preferred_element_type=F32).astype(BF)]
    all_gather x1 -> x2, waiting for transfers between devices: 0.02 us -> 123 us  [the longest x1 75.5 us: body(): lax.all_gather(jnp.concatenate([cotangent[0], route_rows], axis=0), 'expe...]
    ppermute x0 -> x65, starting transfers between devices: none -> 96.3 us  [the longest x22 44.6 us: along_y(): return lax.ppermute(value, 'expert', step_pairs(0, step))]
    ppermute x0 -> x65, waiting for transfers between devices: none -> 79.4 us  [the longest x22 40.5 us: along_x(): return lax.ppermute(value, 'expert', step_pairs(step, 0))]
    psum x1, waiting for transfers between devices: 102 us -> 29.5 us  [body(): early = lax.psum(early.astype(BF), ('dp', 'expert'))]
    gather x8 -> x0, local copies, waits for them, and re-layouts: 69.1 us -> none  [the longest x4 17.1 us: body(): chosen = jnp.take_along_axis(logits, routes, axis=1)]
    psum x1 -> x0, blocking collectives: 65.3 us -> none  [body(): lax.psum((attn_gain_local, query_local, key_local, value_local, query_gai...]
  transfers between devices with their start and end apart: 8 -> 69, of which waited for: 6 -> 24; matrix products, arithmetic and copies ran while one was open for 26% -> 29% of each run, Pallas kernels for 0% -> 2%
where the time goes in v1:
time: 623 us; the launch traced here: 613 us
  waiting for transfers between devices  232 us (37%)
  local copies, waits for them, and re-layouts  103 us (17%)
  starting transfers between devices  96.5 us (15%)
  other arithmetic  70 us (11%)
  Pallas kernels  64.1 us (10%)
  matrix products  31.8 us (5%)
  between operations  15.6 us (3%)
    all_gather x1, waiting for transfers between devices, body(): lax.all_gather(jnp.concatenate([cotangent[0], route_rows], axis=0), 'expe...  75.5 us
    all_gather x1, waiting for transfers between devices, body(): lax.all_gather(normed_two, 'expert', axis_index_groups=plane_groups())  47.8 us
    ppermute x22, starting transfers between devices, along_y(): return lax.ppermute(value, 'expert', step_pairs(0, step))  44.6 us
    ppermute x22, waiting for transfers between devices, along_x(): return lax.ppermute(value, 'expert', step_pairs(step, 0))  40.5 us
    pallas_call x1, Pallas kernels, moe(): pl.pallas_call(moe_kernel, grid_spec=pltpu.PrefetchScalarGridSpec(num_sca...  38.8 us
    unnamed x141, local copies, waits for them, and re-layouts  31.3 us
    psum x1, waiting for transfers between devices, body(): early = lax.psum(early.astype(BF), ('dp', 'expert'))  29.5 us
    ppermute x22, starting transfers between devices, along_x(): return lax.ppermute(value, 'expert', step_pairs(step, 0))  26.4 us
  transfers between devices with their start and end apart: 69, of which 24 were waited for; matrix products, arithmetic and copies ran while one was open for 29% of the time, Pallas kernels for 2%

profile of v1, /device:TPU:6, one launch (start us, length us, event | category | flops | bytes accessed | tf_op | source)
XLA Modules:
  0.0 613.2 jit_solution(15325297995014938048)
XLA Ops:
  9.2 3.6 collective-permute-start.1
  25.4 10.6 %collective-permute-done.1.refs_3_ = bf16[256,1024]{1,0:T(8,128)(2,1)} collective-permute-done((bf16[256,1024]{1,0:T(8,128)(2,1)}, bf16[256,1024]{1,0:T(8,128)(2,1)}, u32[]{:S(2)}, u32[]{:S(2)}) %collective-permute-start.1) | collective-permute-done | bytes 524320 | tf_op jit(solution)/shard_map/ppermute | solution.py:43
  38.1 10.7 %attend.1 = (bf16[1024,1024]{1,0:T(8,128)(2,1)}, bf16[1024,256]{1,0:T(8,128)(2,1)S(1)}, bf16[1024,128]{1,0:T(8,128)(2,1)S(1)}, bf16[1024,128]{1,0:T(8,128)(2,1)S...) custom-call(s32[6]{0:T(128)S(1)} %stack.53.refs_0_.at_ref, ...), custom_call_target="tpu_custom_call" | custom-call | flops 6000000000 | bytes 12000000 | tf_op jit(solution)/shard_map/attend/pallas_call | solution.py:236
  74.6 3.9 copy.139
  85.2 3.1 pad_maximum_fusion.1.gate_ref
  88.3 2.8 pad_maximum_fusion.2.up_ref
  91.2 2.8 pad_maximum_fusion.3.down_ref
  94.0 47.8 %all-gather.5.cloned.1.call-done = bf16[4096,1024]{1,0:T(8,128)(2,1)} async-done(((bf16[256,1024]{1,0:T(8,128)(2,1)}), bf16[4096,1024]{1,0:T(8,128)(2,1)}) %all-gather.5.cloned.1.call-update) | async-done | bytes 8388624 | tf_op jit(solution)/shard_map/all_gather | solution.py:656
  141.8 75.5 %all-gather.7.cloned.1.call-done = bf16[4352,1024]{1,0:T(8,128)(2,1)} async-done(((bf16[272,1024]{1,0:T(8,128)(2,1)}), bf16[4352,1024]{1,0:T(8,128)(2,1)}) %all-gather.7.cloned.1.call-update) | async-done | bytes 8912912 | tf_op jit(solution)/shard_map/all_gather | solution.py:610
  217.3 38.8 %moe.1 = (bf16[4,4,256,512]{3,2,1,0:T(8,128)(2,1)}, bf16[4,4,256,512]{3,2,1,0:T(8,128)(2,1)}, bf16[4,4,272,512]{3,2,1,0:T(8,128)(2,1)}, bf16[4,4,272,512]{3,2,1,...) custom-call(s32[6]{0:T(128)} %copy-done.8, ...), custom_call_target="tpu_custom_call" | custom-call | flops 22000001024 | bytes 60000000 | tf_op jit(solution)/shard_map/moe/pallas_call | solution.py:527
  262.0 3.0 collective-permute-start.19
  265.0 6.4 %convert_bitcast_fusion.1 = bf16[2,1,1024,512]{3,2,0,1:T(8,128)(2,1)S(1)} fusion(bf16[2,1280,1024]{2,1,0:T(8,128)(2,1)} %get-tuple-element.49, bf16[2,1280,512]{2,1,0:T(8,128)(2,1)} %get-tuple-element.51), kind=kOutput, calls=%fused_computation.27 | convolution fusion | flops 2685403136 | bytes 9961472 | tf_op jit(solution)/shard_map/jrd,jrf->jdf/dot_general | solution.py:680
  271.3 6.3 %convert_bitcast_fusion.2 = bf16[2,1,1024,512]{3,2,0,1:T(8,128)(2,1)S(1)} fusion(bf16[2,1280,1024]{2,1,0:T(8,128)(2,1)} %get-tuple-element.49, bf16[2,1280,512]{2,1,0:T(8,128)(2,1)} %get-tuple-element.50), kind=kOutput, calls=%fused_computation.28 | convolution fusion | flops 2685403136 | bytes 9961472 | tf_op jit(solution)/shard_map/jrd,jrf->jdf/dot_general | solution.py:680
  281.5 3.2 collective-permute-start.20
  284.8 6.2 %convert_bitcast_fusion = bf16[2,1,1024,512]{3,2,0,1:T(8,128)(2,1)S(1)} fusion(bf16[2,1280,1024]{2,1,0:T(8,128)(2,1)} %get-tuple-element.52, bf16[2,1280,512]{2,1,0:T(8,128)(2,1)} %get-tuple-element.53), kind=kOutput, calls=%fused_computation.26 | convolution fusion | flops 2685403136 | bytes 9961472 | tf_op jit(solution)/shard_map/jrd,jrf->jdf/dot_general | solution.py:680
  291.8 11.3 %collective-permute-done.10 = bf16[4,272,512]{2,1,0:T(8,128)(2,1)S(1)} collective-permute-done((bf16[4,272,512]{2,1,0:T(8,128)(2,1)S(1)}, bf16[4,272,512]{2,1,0:T(8,128)(2,1)S(1)}, u32[]{:S(2)}, u32[]{:S(2)}) %collective-permute-start.10) | collective-permute-done | bytes 1114144 | tf_op jit(solution)/shard_map/ppermute | solution.py:35
  305.3 3.2 collective-permute-start.15
  312.7 3.3 collective-permute-start.16
  316.0 2.6 collective-permute-done.23
  347.7 2.9 collective-permute-start.42
  352.1 3.0 slice_bitcast_fusion.18
  357.9 14.6 %attend_back.1 = (bf16[1024,512]{1,0:T(8,128)(2,1)S(1)}, f32[8,256]{1,0:T(8,128)S(1)}) custom-call(s32[6]{0:T(128)S(1)} %copy-done.9, bf16[256,256]{1,0:T(8,128)(2,1)S(1)} %bitcast.286, bf16[256,256]{1,0:T(8,128)(2,1)S(1)} %collective-permute-done.41.refs_2_, bf16[256,256]{1,0:T(8,128)(2,1)S(1)} %collective-permute-done.42.refs_3_, ...), custom_call_target="tpu_custom_call" | custom-call | flops 8000000000 | bytes 8000000 | tf_op jit(solution)/shard_map/attend_back/pallas_call | solution.py:372
  379.6 9.0 %collective-permute-done.44 = bf16[256,512]{1,0:T(8,128)(2,1)S(1)} collective-permute-done((bf16[256,512]{1,0:T(8,128)(2,1)}, bf16[256,512]{1,0:T(8,128)(2,1)S(1)}, u32[]{:S(2)}, u32[]{:S(2)}) %collective-permute-start.44) | collective-permute-done | bytes 262176 | tf_op jit(solution)/shard_map/ppermute | solution.py:43
  408.9 4.4 collective-permute-done.48
  413.3 3.2 collective-permute-start.35
  419.9 2.8 collective-permute-start.52
  422.7 2.6 collective-permute-start.53
  429.6 5.6 collective-permute-start.54
  436.7 3.3 collective-permute-start.55
  442.2 3.1 collective-permute-done.56
  446.4 4.7 collective-permute-start.58
  451.2 9.1 %collective-permute-done.57 = bf16[128,512]{1,0:T(8,128)(2,1)S(1)} collective-permute-done((bf16[128,512]{1,0:T(8,128)(2,1)S(1)}, bf16[128,512]{1,0:T(8,128)(2,1)S(1)}, u32[]{:S(2)}, u32[]{:S(2)}) %collective-permute-start.57) | collective-permute-done | bytes 131104 | tf_op jit(solution)/shard_map/ppermute | solution.py:35
  465.5 4.5 fusion
  477.6 29.5 %all-reduce.5.cloned.1.call-done = bf16[1072,1024]{1,0:T(8,128)(2,1)} async-done(((bf16[1072,1024]{1,0:T(8,128)(2,1)}), bf16[1072,1024]{1,0:T(8,128)(2,1)}) %all-reduce.5.cloned.1.call-update) | async-done | bytes 2195472 | tf_op jit(solution)/shard_map/psum | solution.py:712
  510.0 2.5 slice.426
  520.1 3.2 slice_bitcast_fusion.52
  529.0 11.2 %collective-permute-done.34 = bf16[4,256,512]{2,1,0:T(8,128)(2,1)S(1)} collective-permute-done((bf16[4,256,512]{2,1,0:T(8,128)(2,1)}, bf16[4,256,512]{2,1,0:T(8,128)(2,1)S(1)}, u32[]{:S(2)}, u32[]{:S(2)}) %collective-permute-start.34) | collective-permute-done | bytes 1048608 | tf_op jit(solution)/shard_map/ppermute | solution.py:39
  546.6 2.8 collective-permute-start.32
  557.1 4.2 collective-permute-done.40
  563.5 3.0 fusion.2
  566.5 3.3 copy-done.17
  569.8 2.5 slice.422
  572.4 5.4 copy.138
  577.8 4.6 fusion.45
  584.2 2.9 copy.142
  587.1 5.3 copy.148
  594.3 2.9 copy.150
  597.2 3.6 multiply_reduce_fusion
  (422 shorter events, 192.6 us)
Async XLA Ops:
  7.2 134.6 %all-gather.5.cloned.1.call-start = ((), (), s32[]{:S(2)}) async-start(), calls=%async_computation.3 | async-start | bytes 8912896 | tf_op jit(solution)/shard_map/all_gather | solution.py:656
  7.2 18.1 %collective-permute-start = (bf16[256,1024]{1,0:T(8,128)(2,1)}, bf16[256,1024]{1,0:T(8,128)(2,1)}, u32[]{:S(2)}, u32[]{:S(2)}) collective-permute-start(bf16[256,1024]{1,0:T(8,128)(2,1)} %bitcast.282), channel_id=1, source_target_pairs={{0,32},{32,64},{64,96},{96,0},{1,33},{33,65},{65,97},{97,1},{2,34}... | collective-permute-start | bytes 1572872 | tf_op jit(solution)/shard_map/ppermute | solution.py:43
  9.2 26.8 %collective-permute-start.1 = (bf16[256,1024]{1,0:T(8,128)(2,1)}, bf16[256,1024]{1,0:T(8,128)(2,1)}, u32[]{:S(2)}, u32[]{:S(2)}) collective-permute-start(bf16[256,1024]{1,0:T(8,128)(2,1)} %bitcast.283), channel_id=1, source_target_pairs={{0,64},{32,96},{64,0},{96,32},{1,65},{33,97},{65,1},{97,33},{2,66}... | collective-permute-start | bytes 1572872 | tf_op jit(solution)/shard_map/ppermute | solution.py:43
  12.8 23.2 %collective-permute-start.2 = (bf16[256,1024]{1,0:T(8,128)(2,1)}, bf16[256,1024]{1,0:T(8,128)(2,1)}, u32[]{:S(2)}, u32[]{:S(2)}) collective-permute-start(bf16[256,1024]{1,0:T(8,128)(2,1)} %bitcast.284), channel_id=1, source_target_pairs={{0,96},{32,0},{64,32},{96,64},{1,97},{33,1},{65,33},{97,65},{2,98}... | collective-permute-start | bytes 1572872 | tf_op jit(solution)/shard_map/ppermute | solution.py:43
  71.9 145.4 %all-gather.7.cloned.1.call-start = ((), (), s32[]{:S(2)}) async-start(), calls=%async_computation.4 | async-start | bytes 9469952 | tf_op jit(solution)/shard_map/all_gather | solution.py:610
  73.9 433.2 %all-reduce.5.cloned.1.call-start = ((), (), s32[]{:S(2)}) async-start(), calls=%async_computation.1 | async-start | bytes 4390912 | tf_op jit(solution)/shard_map/psum | solution.py:712
  73.9 11.2 %collective-permute-start.6 = (bf16[1,1024,512]{2,1,0:T(8,128)(2,1)}, bf16[1,1024,512]{2,1,0:T(8,128)(2,1)}, u32[]{:S(2)}, u32[]{:S(2)}) collective-permute-start(bf16[1,1024,512]{2,1,0:T(8,128)(2,1)} %param.28), channel_id=1, source_target_pairs={{0,1},{1,0},{2,3},{3,2},{4,5},{5,4},{6,7},{7,6},{8,9},{9,8},{10,11... | collective-permute-start | bytes 3145736 | tf_op jit(solution)/shard_map/ppermute | solution.py:47
  74.0 14.3 %collective-permute-start.7 = (bf16[1,1024,512]{2,1,0:T(8,128)(2,1)}, bf16[1,1024,512]{2,1,0:T(8,128)(2,1)}, u32[]{:S(2)}, u32[]{:S(2)}) collective-permute-start(bf16[1,1024,512]{2,1,0:T(8,128)(2,1)} %param.29), channel_id=1, source_target_pairs={{0,1},{1,0},{2,3},{3,2},{4,5},{5,4},{6,7},{7,6},{8,9},{9,8},{10,11... | collective-permute-start | bytes 3145736 | tf_op jit(solution)/shard_map/ppermute | solution.py:47
  74.5 16.7 %collective-permute-start.8 = (bf16[1,512,1024]{2,1,0:T(8,128)(2,1)}, bf16[1,512,1024]{2,1,0:T(8,128)(2,1)}, u32[]{:S(2)}, u32[]{:S(2)}) collective-permute-start(bf16[1,512,1024]{2,1,0:T(8,128)(2,1)} %param.30), channel_id=1, source_target_pairs={{0,1},{1,0},{2,3},{3,2},{4,5},{5,4},{6,7},{7,6},{8,9},{9,8},{10,11... | collective-permute-start | bytes 3145736 | tf_op jit(solution)/shard_map/ppermute | solution.py:47
  258.0 19.6 %collective-permute-start.11 = (bf16[2,272,512]{2,1,0:T(8,128)(2,1)S(1)}, bf16[2,272,512]{2,1,0:T(8,128)(2,1)S(1)}, u32[]{:S(2)}, u32[]{:S(2)}) collective-permute-start(bf16[2,272,512]{2,1,0:T(8,128)(2,1)S(1)} %get-tuple-element.139), channel_id=1, source_target_pairs={{0,24},{1,25},{2,26},{3,27},{4,28},{5,29},{6,30},{7,31},{8,0},{9,1... | collective-permute-start | bytes 1671176 | tf_op jit(solution)/shard_map/ppermute | solution.py:35
  258.9 18.7 %collective-permute-start.9 = (bf16[2,272,512]{2,1,0:T(8,128)(2,1)S(1)}, bf16[2,272,512]{2,1,0:T(8,128)(2,1)S(1)}, u32[]{:S(2)}, u32[]{:S(2)}) collective-permute-start(bf16[2,272,512]{2,1,0:T(8,128)(2,1)S(1)} %get-tuple-element.138), channel_id=1, source_target_pairs={{0,8},{1,9},{2,10},{3,11},{4,12},{5,13},{6,14},{7,15},{8,16},{9,17... | collective-permute-start | bytes 1671176 | tf_op jit(solution)/shard_map/ppermute | solution.py:35
  261.5 18.7 %collective-permute-start.17 = (bf16[2,272,512]{2,1,0:T(8,128)(2,1)S(1)}, bf16[2,272,512]{2,1,0:T(8,128)(2,1)S(1)}, u32[]{:S(2)}, u32[]{:S(2)}) collective-permute-start(bf16[2,272,512]{2,1,0:T(8,128)(2,1)S(1)} %get-tuple-element.144), channel_id=1, source_target_pairs={{0,2},{1,3},{2,4},{3,5},{4,6},{5,7},{6,0},{7,1},{8,10},{9,11},{10,... | collective-permute-start | bytes 1671176 | tf_op jit(solution)/shard_map/ppermute | solution.py:39
  262.0 18.2 %collective-permute-start.19 = (bf16[2,272,512]{2,1,0:T(8,128)(2,1)S(1)}, bf16[2,272,512]{2,1,0:T(8,128)(2,1)S(1)}, u32[]{:S(2)}, u32[]{:S(2)}) collective-permute-start(bf16[2,272,512]{2,1,0:T(8,128)(2,1)S(1)} %get-tuple-element.145), channel_id=1, source_target_pairs={{0,6},{1,7},{2,0},{3,1},{4,2},{5,3},{6,4},{7,5},{8,14},{9,15},{10,... | collective-permute-start | bytes 1671176 | tf_op jit(solution)/shard_map/ppermute | solution.py:39
  277.9 25.2 %collective-permute-start.10 = (bf16[4,272,512]{2,1,0:T(8,128)(2,1)S(1)}, bf16[4,272,512]{2,1,0:T(8,128)(2,1)S(1)}, u32[]{:S(2)}, u32[]{:S(2)}) collective-permute-start(bf16[4,272,512]{2,1,0:T(8,128)(2,1)S(1)} %pad_maximum_fusion.4), channel_id=1, source_target_pairs={{0,8},{1,9},{2,10},{3,11},{4,12},{5,13},{6,14},{7,15},{8,16},{9,17... | collective-permute-start | bytes 3342344 | tf_op jit(solution)/shard_map/ppermute | solution.py:35
  278.1 26.4 %collective-permute-start.12 = (bf16[4,272,512]{2,1,0:T(8,128)(2,1)S(1)}, bf16[4,272,512]{2,1,0:T(8,128)(2,1)S(1)}, u32[]{:S(2)}, u32[]{:S(2)}) collective-permute-start(bf16[4,272,512]{2,1,0:T(8,128)(2,1)S(1)} %pad_maximum_fusion.5), channel_id=1, source_target_pairs={{0,24},{1,25},{2,26},{3,27},{4,28},{5,29},{6,30},{7,31},{8,0},{9,1... | collective-permute-start | bytes 3342344 | tf_op jit(solution)/shard_map/ppermute | solution.py:35
  280.4 28.2 %collective-permute-start.18 = (bf16[4,272,512]{2,1,0:T(8,128)(2,1)S(1)}, bf16[4,272,512]{2,1,0:T(8,128)(2,1)S(1)}, u32[]{:S(2)}, u32[]{:S(2)}) collective-permute-start(bf16[4,272,512]{2,1,0:T(8,128)(2,1)S(1)} %pad_maximum_fusion.6), channel_id=1, source_target_pairs={{0,2},{1,3},{2,4},{3,5},{4,6},{5,7},{6,0},{7,1},{8,10},{9,11},{10,... | collective-permute-start | bytes 3342344 | tf_op jit(solution)/shard_map/ppermute | solution.py:39
  281.5 27.0 %collective-permute-start.20 = (bf16[4,272,512]{2,1,0:T(8,128)(2,1)}, bf16[4,272,512]{2,1,0:T(8,128)(2,1)}, u32[]{:S(2)}, u32[]{:S(2)}) collective-permute-start(bf16[4,272,512]{2,1,0:T(8,128)(2,1)} %pad_maximum_fusion.7), channel_id=1, source_target_pairs={{0,6},{1,7},{2,0},{3,1},{4,2},{5,3},{6,4},{7,5},{8,14},{9,15},{10,... | collective-permute-start | bytes 3342344 | tf_op jit(solution)/shard_map/ppermute | solution.py:39
  312.6 10.1 %collective-permute-start.14 = (bf16[272,512]{1,0:T(8,128)(2,1)S(1)}, bf16[272,512]{1,0:T(8,128)(2,1)S(1)}, u32[]{:S(2)}, u32[]{:S(2)}) collective-permute-start(bf16[272,512]{1,0:T(8,128)(2,1)S(1)} %pad_maximum_fusion.18), channel_id=1, source_target_pairs={{0,2},{1,3},{2,4},{3,5},{4,6},{5,7},{6,0},{7,1},{8,10},{9,11},{10,... | collective-permute-start | bytes 835592 | tf_op jit(solution)/shard_map/ppermute | solution.py:39
  312.7 10.0 %collective-permute-start.16 = (bf16[272,512]{1,0:T(8,128)(2,1)S(1)}, bf16[272,512]{1,0:T(8,128)(2,1)S(1)}, u32[]{:S(2)}, u32[]{:S(2)}) collective-permute-start(bf16[272,512]{1,0:T(8,128)(2,1)S(1)} %pad_maximum_fusion.19), channel_id=1, source_target_pairs={{0,6},{1,7},{2,0},{3,1},{4,2},{5,3},{6,4},{7,5},{8,14},{9,15},{10,... | collective-permute-start | bytes 835592 | tf_op jit(solution)/shard_map/ppermute | solution.py:39
  322.7 142.8 %collective-permute-start.64 = (bf16[3,1024,512]{2,1,0:T(8,128)(2,1)}, bf16[3,1024,512]{2,1,0:T(8,128)(2,1)}, u32[]{:S(2)}, u32[]{:S(2)}) collective-permute-start(bf16[3,1024,512]{2,1,0:T(8,128)(2,1)} %slice_bitcast_fusion), channel_id=1, source_target_pairs={{0,1},{1,0},{2,3},{3,2},{4,5},{5,4},{6,7},{7,6},{8,9},{9,8},{10,11... | collective-permute-start | bytes 9437192 | tf_op jit(solution)/shard_map/ppermute | solution.py:47
  343.5 259.0 %reduce-scatter.2.cloned.1.call-start = ((), (), s32[]{:S(2)}) async-start(), calls=%async_computation.2 | async-start | bytes 3932160 | tf_op jit(solution)/shard_map/reduce_scatter | solution.py:687
  346.1 11.1 %collective-permute-start.41 = (bf16[256,256]{1,0:T(8,128)(2,1)S(1)}, bf16[256,256]{1,0:T(8,128)(2,1)S(1)}, u32[]{:S(2)}, u32[]{:S(2)}) collective-permute-start(bf16[256,256]{1,0:T(8,128)(2,1)S(1)} %bitcast.306), channel_id=1, source_target_pairs={{0,32},{32,64},{64,96},{96,0},{1,33},{33,65},{65,97},{97,1},{2,34}... | collective-permute-start | bytes 393224 | tf_op jit(solution)/shard_map/ppermute | solution.py:43
  347.7 9.4 %collective-permute-start.42 = (bf16[256,256]{1,0:T(8,128)(2,1)S(1)}, bf16[256,256]{1,0:T(8,128)(2,1)S(1)}, u32[]{:S(2)}, u32[]{:S(2)}) collective-permute-start(bf16[256,256]{1,0:T(8,128)(2,1)S(1)} %bitcast.307), channel_id=1, source_target_pairs={{0,64},{32,96},{64,0},{96,32},{1,65},{33,97},{65,1},{97,33},{2,66}... | collective-permute-start | bytes 393224 | tf_op jit(solution)/shard_map/ppermute | solution.py:43
  355.2 51.1 %collective-permute-start.25 = (bf16[2,256,512]{2,1,0:T(8,128)(2,1)}, bf16[2,256,512]{2,1,0:T(8,128)(2,1)}, u32[]{:S(2)}, u32[]{:S(2)}) collective-permute-start(bf16[2,256,512]{2,1,0:T(8,128)(2,1)} %get-tuple-element.150), channel_id=1, source_target_pairs={{0,8},{1,9},{2,10},{3,11},{4,12},{5,13},{6,14},{7,15},{8,16},{9,17... | collective-permute-start | bytes 1572872 | tf_op jit(solution)/shard_map/ppermute | solution.py:35
  375.0 13.6 %collective-permute-start.44 = (bf16[256,512]{1,0:T(8,128)(2,1)}, bf16[256,512]{1,0:T(8,128)(2,1)S(1)}, u32[]{:S(2)}, u32[]{:S(2)}) collective-permute-start(bf16[256,512]{1,0:T(8,128)(2,1)} %get-tuple-element.178), channel_id=1, source_target_pairs={{0,32},{32,64},{64,96},{96,0},{1,33},{33,65},{65,97},{97,1},{2,34}... | collective-permute-start | bytes 786440 | tf_op jit(solution)/shard_map/ppermute | solution.py:43
  375.6 14.7 %collective-permute-start.45 = (bf16[256,512]{1,0:T(8,128)(2,1)}, bf16[256,512]{1,0:T(8,128)(2,1)}, u32[]{:S(2)}, u32[]{:S(2)}) collective-permute-start(bf16[256,512]{1,0:T(8,128)(2,1)} %get-tuple-element.177), channel_id=1, source_target_pairs={{0,64},{32,96},{64,0},{96,32},{1,65},{33,97},{65,1},{97,33},{2,66}... | collective-permute-start | bytes 786440 | tf_op jit(solution)/shard_map/ppermute | solution.py:43
  376.9 15.3 %collective-permute-start.46 = (bf16[256,512]{1,0:T(8,128)(2,1)S(1)}, bf16[256,512]{1,0:T(8,128)(2,1)}, u32[]{:S(2)}, u32[]{:S(2)}) collective-permute-start(bf16[256,512]{1,0:T(8,128)(2,1)S(1)} %get-tuple-element.176), channel_id=1, source_target_pairs={{0,96},{32,0},{64,32},{96,64},{1,97},{33,1},{65,33},{97,65},{2,98}... | collective-permute-start | bytes 786440 | tf_op jit(solution)/shard_map/ppermute | solution.py:43
  388.6 18.0 %collective-permute-start.27 = (bf16[2,256,512]{2,1,0:T(8,128)(2,1)}, bf16[2,256,512]{2,1,0:T(8,128)(2,1)}, u32[]{:S(2)}, u32[]{:S(2)}) collective-permute-start(bf16[2,256,512]{2,1,0:T(8,128)(2,1)} %get-tuple-element.151), channel_id=1, source_target_pairs={{0,24},{1,25},{2,26},{3,27},{4,28},{5,29},{6,30},{7,31},{8,0},{9,1... | collective-permute-start | bytes 1572872 | tf_op jit(solution)/shard_map/ppermute | solution.py:35
  390.4 39.2 %collective-permute-start.33 = (bf16[2,256,512]{2,1,0:T(8,128)(2,1)}, bf16[2,256,512]{2,1,0:T(8,128)(2,1)}, u32[]{:S(2)}, u32[]{:S(2)}) collective-permute-start(bf16[2,256,512]{2,1,0:T(8,128)(2,1)} %get-tuple-element.156), channel_id=1, source_target_pairs={{0,2},{1,3},{2,4},{3,5},{4,6},{5,7},{6,0},{7,1},{8,10},{9,11},{10,... | collective-permute-start | bytes 1572872 | tf_op jit(solution)/shard_map/ppermute | solution.py:39
  392.3 10.0 %collective-permute-start.47 = (bf16[528,512]{1,0:T(8,128)(2,1)}, bf16[528,512]{1,0:T(8,128)(2,1)}, u32[]{:S(2)}, u32[]{:S(2)}) collective-permute-start(bf16[528,512]{1,0:T(8,128)(2,1)} %pad_maximum_fusion.12), channel_id=1, source_target_pairs={{0,1},{1,0},{2,3},{3,2},{4,5},{5,4},{6,7},{7,6},{8,9},{9,8},{10,11... | collective-permute-start | bytes 1622024 | tf_op jit(solution)/shard_map/ppermute | solution.py:47
  403.8 9.5 %collective-permute-start.48 = (bf16[144,512]{1,0:T(8,128)(2,1)S(1)}, bf16[144,512]{1,0:T(8,128)(2,1)S(1)}, u32[]{:S(2)}, u32[]{:S(2)}) collective-permute-start(bf16[144,512]{1,0:T(8,128)(2,1)S(1)} %get-tuple-element.215), channel_id=1, source_target_pairs={{0,8},{1,9},{2,10},{3,11},{4,12},{5,13},{6,14},{7,15},{8,16},{9,17... | collective-permute-start | bytes 442376 | tf_op jit(solution)/shard_map/ppermute | solution.py:35
  406.3 10.2 %collective-permute-start.49 = (bf16[144,512]{1,0:T(8,128)(2,1)S(1)}, bf16[144,512]{1,0:T(8,128)(2,1)S(1)}, u32[]{:S(2)}, u32[]{:S(2)}) collective-permute-start(bf16[144,512]{1,0:T(8,128)(2,1)S(1)} %get-tuple-element.216), channel_id=1, source_target_pairs={{0,16},{1,17},{2,18},{3,19},{4,20},{5,21},{6,22},{7,23},{8,24},{9,... | collective-permute-start | bytes 442376 | tf_op jit(solution)/shard_map/ppermute | solution.py:35
  406.6 10.2 %collective-permute-start.50 = (bf16[144,512]{1,0:T(8,128)(2,1)S(1)}, bf16[144,512]{1,0:T(8,128)(2,1)S(1)}, u32[]{:S(2)}, u32[]{:S(2)}) collective-permute-start(bf16[144,512]{1,0:T(8,128)(2,1)S(1)} %get-tuple-element.217), channel_id=1, source_target_pairs={{0,24},{1,25},{2,26},{3,27},{4,28},{5,29},{6,30},{7,31},{8,0},{9,1... | collective-permute-start | bytes 442376 | tf_op jit(solution)/shard_map/ppermute | solution.py:35
  413.3 21.9 %collective-permute-start.35 = (bf16[2,256,512]{2,1,0:T(8,128)(2,1)S(1)}, bf16[2,256,512]{2,1,0:T(8,128)(2,1)S(1)}, u32[]{:S(2)}, u32[]{:S(2)}) collective-permute-start(bf16[2,256,512]{2,1,0:T(8,128)(2,1)S(1)} %copy-done.48), channel_id=1, source_target_pairs={{0,6},{1,7},{2,0},{3,1},{4,2},{5,3},{6,4},{7,5},{8,14},{9,15},{10,... | collective-permute-start | bytes 1572872 | tf_op jit(solution)/shard_map/ppermute | solution.py:39
  426.4 96.8 %collective-permute-start.26 = (bf16[4,256,512]{2,1,0:T(8,128)(2,1)}, bf16[4,256,512]{2,1,0:T(8,128)(2,1)}, u32[]{:S(2)}, u32[]{:S(2)}) collective-permute-start(bf16[4,256,512]{2,1,0:T(8,128)(2,1)} %pad_maximum_fusion.8), channel_id=1, source_target_pairs={{0,8},{1,9},{2,10},{3,11},{4,12},{5,13},{6,14},{7,15},{8,16},{9,17... | collective-permute-start | bytes 3145736 | tf_op jit(solution)/shard_map/ppermute | solution.py:35
  429.5 93.7 %collective-permute-start.28 = (bf16[4,256,512]{2,1,0:T(8,128)(2,1)}, bf16[4,256,512]{2,1,0:T(8,128)(2,1)}, u32[]{:S(2)}, u32[]{:S(2)}) collective-permute-start(bf16[4,256,512]{2,1,0:T(8,128)(2,1)} %pad_maximum_fusion.9), channel_id=1, source_target_pairs={{0,24},{1,25},{2,26},{3,27},{4,28},{5,29},{6,30},{7,31},{8,0},{9,1... | collective-permute-start | bytes 3145736 | tf_op jit(solution)/shard_map/ppermute | solution.py:35
  429.6 10.4 %collective-permute-start.54 = (bf16[32,512]{1,0:T(8,128)(2,1)S(1)}, bf16[32,512]{1,0:T(8,128)(2,1)S(1)}, u32[]{:S(2)}, u32[]{:S(2)}) collective-permute-start(bf16[32,512]{1,0:T(8,128)(2,1)S(1)} %get-tuple-element.210), channel_id=1, source_target_pairs={{0,6},{1,7},{2,0},{3,1},{4,2},{5,3},{6,4},{7,5},{8,14},{9,15},{10,... | collective-permute-start | bytes 98312 | tf_op jit(solution)/shard_map/ppermute | solution.py:39
  445.3 14.9 %collective-permute-start.57 = (bf16[128,512]{1,0:T(8,128)(2,1)S(1)}, bf16[128,512]{1,0:T(8,128)(2,1)S(1)}, u32[]{:S(2)}, u32[]{:S(2)}) collective-permute-start(bf16[128,512]{1,0:T(8,128)(2,1)S(1)} %constant_dynamic-update-slice_fusion.4), channel_id=1, source_target_pairs={{0,24},{1,25},{2,26},{3,27},{4,28},{5,29},{6,30},{7,31},{8,0},{9,1... | collective-permute-start | bytes 393224 | tf_op jit(solution)/shard_map/ppermute | solution.py:35
  446.4 16.6 %collective-permute-start.58 = (bf16[128,512]{1,0:T(8,128)(2,1)S(1)}, bf16[128,512]{1,0:T(8,128)(2,1)S(1)}, u32[]{:S(2)}, u32[]{:S(2)}) collective-permute-start(bf16[128,512]{1,0:T(8,128)(2,1)S(1)} %constant_dynamic-update-slice_fusion.4), channel_id=1, source_target_pairs={{0,16},{1,17},{2,18},{3,19},{4,20},{5,21},{6,22},{7,23},{8,24},{9,... | collective-permute-start | bytes 393224 | tf_op jit(solution)/shard_map/ppermute | solution.py:35
  465.4 47.7 %collective-permute-start.60 = (bf16[528,512]{1,0:T(8,128)(2,1)S(1)}, bf16[528,512]{1,0:T(8,128)(2,1)S(1)}, u32[]{:S(2)}, u32[]{:S(2)}) collective-permute-start(bf16[528,512]{1,0:T(8,128)(2,1)S(1)} %pad_maximum_fusion.13), channel_id=1, source_target_pairs={{0,32},{32,64},{64,96},{96,0},{1,33},{33,65},{65,97},{97,1},{2,34}... | collective-permute-start | bytes 1622024 | tf_op jit(solution)/shard_map/ppermute | solution.py:43
  472.1 44.1 %collective-permute-start.61 = (bf16[528,512]{1,0:T(8,128)(2,1)S(1)}, bf16[528,512]{1,0:T(8,128)(2,1)}, u32[]{:S(2)}, u32[]{:S(2)}) collective-permute-start(bf16[528,512]{1,0:T(8,128)(2,1)S(1)} %pad_maximum_fusion.13), channel_id=1, source_target_pairs={{0,64},{32,96},{64,0},{96,32},{1,65},{33,97},{65,1},{97,33},{2,66}... | collective-permute-start | bytes 1622024 | tf_op jit(solution)/shard_map/ppermute | solution.py:43
  473.2 46.0 %collective-permute-start.62 = (bf16[528,512]{1,0:T(8,128)(2,1)S(1)}, bf16[528,512]{1,0:T(8,128)(2,1)S(1)}, u32[]{:S(2)}, u32[]{:S(2)}) collective-permute-start(bf16[528,512]{1,0:T(8,128)(2,1)S(1)} %pad_maximum_fusion.13), channel_id=1, source_target_pairs={{0,96},{32,0},{64,32},{96,64},{1,97},{33,1},{65,33},{97,65},{2,98}... | collective-permute-start | bytes 1622024 | tf_op jit(solution)/shard_map/ppermute | solution.py:43
  513.1 27.1 %collective-permute-start.34 = (bf16[4,256,512]{2,1,0:T(8,128)(2,1)}, bf16[4,256,512]{2,1,0:T(8,128)(2,1)S(1)}, u32[]{:S(2)}, u32[]{:S(2)}) collective-permute-start(bf16[4,256,512]{2,1,0:T(8,128)(2,1)} %pad_maximum_fusion.10), channel_id=1, source_target_pairs={{0,2},{1,3},{2,4},{3,5},{4,6},{5,7},{6,0},{7,1},{8,10},{9,11},{10,... | collective-permute-start | bytes 3145736 | tf_op jit(solution)/shard_map/ppermute | solution.py:39
  516.1 24.4 %collective-permute-start.36 = (bf16[4,256,512]{2,1,0:T(8,128)(2,1)}, bf16[4,256,512]{2,1,0:T(8,128)(2,1)S(1)}, u32[]{:S(2)}, u32[]{:S(2)}) collective-permute-start(bf16[4,256,512]{2,1,0:T(8,128)(2,1)} %pad_maximum_fusion.11), channel_id=1, source_target_pairs={{0,6},{1,7},{2,0},{3,1},{4,2},{5,3},{6,4},{7,5},{8,14},{9,15},{10,... | collective-permute-start | bytes 3145736 | tf_op jit(solution)/shard_map/ppermute | solution.py:39
  523.2 40.2 %collective-permute-start.63 = (bf16[4,512,512]{2,1,0:T(8,128)(2,1)}, bf16[4,512,512]{2,1,0:T(8,128)(2,1)}, u32[]{:S(2)}, u32[]{:S(2)}) collective-permute-start(bf16[4,512,512]{2,1,0:T(8,128)(2,1)} %get-tuple-element.161), channel_id=1, source_target_pairs={{0,1},{1,0},{2,3},{3,2},{4,5},{5,4},{6,7},{7,6},{8,9},{9,8},{10,11... | collective-permute-start | bytes 6291464 | tf_op jit(solution)/shard_map/ppermute | solution.py:47
  525.7 18.8 %collective-permute-start.29 = (bf16[128,512]{1,0:T(8,128)(2,1)S(1)}, bf16[128,512]{1,0:T(8,128)(2,1)S(1)}, u32[]{:S(2)}, u32[]{:S(2)}) collective-permute-start(bf16[128,512]{1,0:T(8,128)(2,1)S(1)} %get-tuple-element.182), channel_id=1, source_target_pairs={{0,2},{1,3},{2,4},{3,5},{4,6},{5,7},{6,0},{7,1},{8,10},{9,11},{10,... | collective-permute-start | bytes 393224 | tf_op jit(solution)/shard_map/ppermute | solution.py:39
  526.7 17.8 %collective-permute-start.31 = (bf16[128,512]{1,0:T(8,128)(2,1)S(1)}, bf16[128,512]{1,0:T(8,128)(2,1)S(1)}, u32[]{:S(2)}, u32[]{:S(2)}) collective-permute-start(bf16[128,512]{1,0:T(8,128)(2,1)S(1)} %get-tuple-element.183), channel_id=1, source_target_pairs={{0,6},{1,7},{2,0},{3,1},{4,2},{5,3},{6,4},{7,5},{8,14},{9,15},{10,... | collective-permute-start | bytes 393224 | tf_op jit(solution)/shard_map/ppermute | solution.py:39
  545.2 10.4 %collective-permute-start.30 = (bf16[256,512]{1,0:T(8,128)(2,1)}, bf16[256,512]{1,0:T(8,128)(2,1)}, u32[]{:S(2)}, u32[]{:S(2)}) collective-permute-start(bf16[256,512]{1,0:T(8,128)(2,1)} %pad_maximum_fusion.23), channel_id=1, source_target_pairs={{0,2},{1,3},{2,4},{3,5},{4,6},{5,7},{6,0},{7,1},{8,10},{9,11},{10,... | collective-permute-start | bytes 786440 | tf_op jit(solution)/shard_map/ppermute | solution.py:39
  (86 other events, 682.2 us)
Sparse Core Ops, SparseCore 0:
  72.0 69.7 all-gather.4
  144.5 72.7 all-gather.6
  343.7 163.4 all-reduce.4
  509.5 37.5 reduce-scatter.1

commit v2 on v1

--- a/solution.py
+++ b/solution.py
@@ -60,27 +60,20 @@
     return move(parts[2, :half], 1), move(parts[2, half:], -1)
 
 
-def ring_middle(parts, first, move):
+def ring_operands(parts, first):
     half = parts.shape[1] // 2
     ahead, behind = first
     up = jnp.concatenate([parts[1, :half] + ahead, parts[1, half:]], axis=0)
     down = jnp.concatenate([parts[3, :half], parts[3, half:] + behind], axis=0)
-    return move(up, 1), move(down, -1)
+    return up, down
 
 
 def ring_end(parts, second):
     return parts[0].astype(F32) + second[0].astype(F32) + second[1].astype(F32)
 
 
-def plane_sum(part_a, part_b):
-    for move_a, move_b in ((along_x, along_y), (along_y, along_x)):
-        first_a, first_b = ring_start(part_a, move_a), ring_start(part_b, move_b)
-        second_a = ring_middle(part_a, first_a, move_a)
-        second_b = ring_middle(part_b, first_b, move_b)
-        part_a, part_b = ring_end(part_a, second_a), ring_end(part_b, second_b)
-        if part_a.ndim == 3:
-            part_a, part_b = part_a.astype(BF), part_b.astype(BF)
-    return part_a, part_b
+def low(parts):
+    return parts.astype(BF)
 
 
 def block_at(whole, index, rows):
@@ -97,13 +90,8 @@
     return total[:rows], total[rows:]
 
 
-def gather_rows(part, here, move):
-    rows = part.shape[0]
-    whole = jnp.zeros((SIDE * rows,) + part.shape[1:], part.dtype)
-    pieces = [part, move(part, -1), move(part, 2), move(part, 1)]
-    for r, piece in enumerate(pieces):
-        whole = lax.dynamic_update_slice_in_dim(whole, piece, ((here + r) % SIDE) * rows, 0)
-    return whole
+def ring_pieces(part, move):
+    return [part, move(part, -1), move(part, 2), move(part, 1)]
 
 
 def nt(a, b):
@@ -391,75 +379,84 @@
     )(at, *operands)
 
 
+def expert_lines(routes, experts):
+    line = lax.broadcasted_iota(jnp.int32, (experts, routes.shape[1]), 0).astype(F32)
+    chosen = line == routes[0:1]
+    for k in range(1, TOP):
+        chosen = chosen | (line == routes[k : k + 1])
+    return line, chosen
+
+
+def pick_kernel(at_ref, cot_ref, down_ref, pick_ref, up_ref, dh_ref):
+    tokens = pick_ref.shape[2]
+    pick_iota = lax.broadcasted_iota(jnp.int32, (CAP, tokens), 0).astype(F32)
+    tri = (
+        lax.broadcasted_iota(jnp.int32, (tokens, tokens), 0)
+        <= lax.broadcasted_iota(jnp.int32, (tokens, tokens), 1)
+    ).astype(BF)
+    mine = [at_ref[4 + j].astype(F32) for j in range(2)]
+    members = []
+    for s in range(SIDE):
+        routes = cot_ref[0, s, tokens : tokens + 16, :tokens].astype(F32)
+        for j in range(2):
+            found = jnp.where(routes == mine[j], 1.0, 0.0)
+            members.append(jnp.sum(found, axis=0, keepdims=True))
+    member_all = jnp.concatenate(members, axis=0)
+    rank_all = nn(member_all.astype(BF), tri)
+    rank_all = jnp.where(member_all > 0.5, rank_all - 1.0, -1.0)
+    for s in range(SIDE):
+        for j in range(2):
+            hit = pick_iota == rank_all[s * 2 + j : s * 2 + j + 1]
+            pick_ref[s, j * CAP : (j + 1) * CAP] = jnp.where(hit, 1.0, 0.0).astype(BF)
+        took = nn(pick_ref[s], cot_ref[0, s, :tokens]).astype(BF)
+        for j in range(2):
+            up_ref[j, s * CAP : (s + 1) * CAP] = took[j * CAP : (j + 1) * CAP]
+    for j in range(2):
+        dh_ref[j] = nt(up_ref[j], down_ref[j])
+
+
 def moe_kernel(
     at_ref,
     rows_ref,
-    cot_ref,
+    routes_ref,
+    pick_ref,
+    dh_ref,
     router_ref,
     gate_ref,
     up_ref,
-    down_ref,
-    out_a_ref,
-    out_b_ref,
     back_a_ref,
     back_b_ref,
     x_ref,
     dgate_ref,
     dup_ref,
     hidden_ref,
-    slot_ref,
-    pick_scr,
-    up_scr,
-    gate_scr,
+    scaled_ref,
+    share_ref,
     dgs_scr,
-    o_scr,
     b_scr,
 ):
     tokens = rows_ref.shape[2]
-    width = rows_ref.shape[3]
-    half = width // 2
-    experts = router_ref.shape[0]
+    half = rows_ref.shape[3] // 2
     y_here, chip = at_ref[2], at_ref[3]
-    pick_iota = lax.broadcasted_iota(jnp.int32, (CAP, tokens), 0).astype(F32)
-    expert_iota = lax.broadcasted_iota(jnp.int32, (experts, tokens), 0).astype(F32)
     chip_row = lax.broadcasted_iota(jnp.int32, (SIDE * SIDE, half), 0) == chip
-    tri = (
-        lax.broadcasted_iota(jnp.int32, (tokens, tokens), 0)
-        <= lax.broadcasted_iota(jnp.int32, (tokens, tokens), 1)
-    ).astype(BF)
     mine = [at_ref[4 + j].astype(F32) for j in range(2)]
-    members, gates = [], []
     for s in range(SIDE):
         rows = rows_ref[0, s]
-        routes = cot_ref[0, s, tokens : tokens + 16, :tokens].astype(F32)
+        routes = routes_ref[0, s, :, :tokens].astype(F32)
         logits = nt(router_ref[...], rows)
-        chosen = expert_iota == routes[0:1]
-        for k in range(1, TOP):
-            chosen = chosen | (expert_iota == routes[k : k + 1])
+        line, chosen = expert_lines(routes, router_ref.shape[0])
         top = jnp.max(jnp.where(chosen, logits, masked), axis=0, keepdims=True)
         expo = jnp.where(chosen, jnp.exp(jnp.minimum(logits - top, 0.0)), 0.0)
         share = expo / jnp.sum(expo, axis=0, keepdims=True)
+        took = nn(pick_ref[s], rows).astype(BF)
         for j in range(2):
-            picked = expert_iota == mine[j]
-            gates.append(jnp.sum(jnp.where(picked, share, 0.0), axis=0, keepdims=True))
-            members.append(jnp.sum(jnp.where(picked & chosen, 1.0, 0.0), axis=0, keepdims=True))
-    member_all = jnp.concatenate(members, axis=0)
-    rank_all = nn(member_all.astype(BF), tri)
-    rank_all = jnp.where(member_all > 0.5, rank_all - 1.0, -1.0)
-    for s in range(SIDE):
-        for j in range(2):
-            n = s * 2 + j
-            hit = pick_iota == rank_all[n : n + 1]
-            pick_scr[s, j * CAP : (j + 1) * CAP] = jnp.where(hit, 1.0, 0.0).astype(BF)
-            gate_scr[j, s * CAP : (s + 1) * CAP] = jnp.sum(
-                jnp.where(hit, gates[n], 0.0), axis=1, keepdims=True
+            own = jnp.sum(jnp.where(line == mine[j], share, 0.0), axis=0, keepdims=True)
+            here = slice(s * CAP, (s + 1) * CAP)
+            there = slice(j * CAP, (j + 1) * CAP)
+            share_ref[j, here] = jnp.sum(
+                pick_ref[s, there].astype(F32) * own, axis=1, keepdims=True
             )
-        pick = pick_scr[s]
-        took = nn(pick, rows_ref[0, s]).astype(BF)
-        took_up = nn(pick, cot_ref[0, s, :tokens]).astype(BF)
-        for j in range(2):
-            x_ref[j, s * CAP : (s + 1) * CAP] = took[j * CAP : (j + 1) * CAP]
-            up_scr[j, s * CAP : (s + 1) * CAP] = took_up[j * CAP : (j + 1) * CAP]
+            x_ref[j, here] = took[there]
     for j in range(2):
         x = x_ref[j]
         gate_act = nn(x, gate_ref[j])
@@ -468,105 +465,302 @@
         silu = gate_act * sig
         hidden = (silu * up_act).astype(BF)
         hidden_ref[j] = hidden
-        upstream = up_scr[j].astype(F32)
-        gate_col = gate_scr[j]
-        slot = (gate_col * upstream).astype(BF)
-        slot_ref[j] = slot
-        result = nn(hidden, down_ref[j]).astype(BF).astype(F32)
-        dgs_scr[j] = jnp.sum(upstream * result, axis=1, keepdims=True)
-        gated = (gate_col * result).astype(BF)
-        d_hidden = nt(slot, down_ref[j])
+        scaled_ref[j] = (hidden.astype(F32) * share_ref[j]).astype(BF)
+        raw = dh_ref[j]
+        dgs_scr[j] = jnp.sum(hidden.astype(F32) * raw, axis=1, keepdims=True)
+        d_hidden = raw * share_ref[j]
         d_gate = (d_hidden * up_act * (sig + silu * (1.0 - sig))).astype(BF)
         d_up = (d_hidden * silu).astype(BF)
         dgate_ref[j] = d_gate
         dup_ref[j] = d_up
         d_rows = (nt(d_gate, gate_ref[j]) + nt(d_up, up_ref[j])).astype(BF)
         for s in range(SIDE):
-            o_scr[s, j * CAP : (j + 1) * CAP] = gated[s * CAP : (s + 1) * CAP]
             b_scr[s, j * CAP : (j + 1) * CAP] = d_rows[s * CAP : (s + 1) * CAP]
     for s in range(SIDE):
         dy = lax.rem(s - y_here + SIDE, SIDE)
-        pick = pick_scr[s]
-        back = tn(pick, b_scr[s]).astype(BF)
+        back = tn(pick_ref[s], b_scr[s]).astype(BF)
         back_a_ref[0, dy, :tokens] = back[:, :half]
         back_b_ref[dy, 0, :tokens] = back[:, half:]
-        out = tn(pick, o_scr[s]).astype(BF)
-        out_a_ref[0, dy] = out[:, :half]
-        out_b_ref[dy, 0] = out[:, half:]
         found = []
         for j in range(2):
-            hit = pick_iota == rank_all[s * 2 + j : s * 2 + j + 1]
             col = dgs_scr[j, s * CAP : (s + 1) * CAP]
-            found.append(jnp.sum(jnp.where(hit, col, 0.0), axis=0, keepdims=True))
+            pick = pick_ref[s, j * CAP : (j + 1) * CAP].astype(F32)
+            found.append(jnp.sum(pick * col, axis=0, keepdims=True))
         found = jnp.where(chip_row, jnp.concatenate(found, axis=1), 0.0)
         high = found.astype(BF)
         back_a_ref[0, dy, tokens:] = high
         back_b_ref[dy, 0, tokens:] = (found - high.astype(F32)).astype(BF)
 
 
-def moe(at, rows, cot, router_t, gate, up, down):
-    _, _, tokens, width = rows.shape
-    padded = cot.shape[2]
-    ff = gate.shape[2]
-    slots = SIDE * CAP
-    half = width // 2
-
-    def whole(shape):
-        return pl.BlockSpec(shape, lambda g, at: (0,) * len(shape))
-
-    def source(g, at):
-        return (at[1] + 2 + g) % SIDE
-
-    def first(g, at):
-        return ((2 + g) % SIDE, 0, 0, 0)
-
-    def second(g, at):
-        return (0, (2 + g) % SIDE, 0, 0)
-
-    kept = [width, ff, ff, ff, width]
+def result_kernel(at_ref, hidden_ref, share_ref, pick_ref, down_ref, out_ref, o_scr):
+    for j in range(2):
+        share = share_ref[j]
+        result = nn(hidden_ref[j], down_ref[j]).astype(BF).astype(F32)
+        gated = (share * result).astype(BF)
+        for s in range(SIDE):
+            o_scr[s, j * CAP : (j + 1) * CAP] = gated[s * CAP : (s + 1) * CAP]
+    for s in range(SIDE):
+        out_ref[0, s] = tn(pick_ref[s], o_scr[s]).astype(BF)
+
+
+def over_sources(kernel, at, operands, outs, scratch, flops, name):
     return pl.pallas_call(
-        moe_kernel,
+        kernel,
         grid_spec=pltpu.PrefetchScalarGridSpec(
             num_scalar_prefetch=1,
             grid=(SIDE,),
-            in_specs=[
-                pl.BlockSpec((1, SIDE, tokens, width), lambda g, at: (source(g, at), 0, 0, 0)),
-                pl.BlockSpec((1, SIDE, padded, width), lambda g, at: (source(g, at), 0, 0, 0)),
-                whole(router_t.shape),
-                whole(gate.shape),
-                whole(up.shape),
-                whole(down.shape),
-            ],
-            out_specs=[
-                pl.BlockSpec((1, SIDE, tokens, half), first),
-                pl.BlockSpec((SIDE, 1, tokens, half), second),
-                pl.BlockSpec((1, SIDE, padded, half), first),
-                pl.BlockSpec((SIDE, 1, padded, half), second),
-            ]
-            + [pl.BlockSpec((2, slots, n), lambda g, at: (0, g, 0)) for n in kept],
-            scratch_shapes=[
-                pltpu.VMEM((SIDE, 2 * CAP, tokens), BF),
-                pltpu.VMEM((2, slots, width), BF),
-                pltpu.VMEM((2, slots, 1), F32),
-                pltpu.VMEM((2, slots, 1), F32),
-                pltpu.VMEM((SIDE, 2 * CAP, width), BF),
-                pltpu.VMEM((SIDE, 2 * CAP, width), BF),
-            ],
+            in_specs=[pl.BlockSpec(block, index) for _, block, index in operands],
+            out_specs=[pl.BlockSpec(block, index) for _, block, index in outs],
+            scratch_shapes=scratch,
         ),
-        out_shape=[jax.ShapeDtypeStruct((SIDE, SIDE, tokens, half), BF)] * 2
-        + [jax.ShapeDtypeStruct((SIDE, SIDE, padded, half), BF)] * 2
-        + [jax.ShapeDtypeStruct((2, SIDE * slots, n), BF) for n in kept],
+        out_shape=[jax.ShapeDtypeStruct(*what) for what, _, _ in outs],
         compiler_params=pltpu.CompilerParams(vmem_limit_bytes=60 * MIB),
-        cost_estimate=pl.CostEstimate(
-            flops=22_000_000_000, bytes_accessed=60_000_000, transcendentals=0
+        cost_estimate=pl.CostEstimate(flops=flops, bytes_accessed=30_000_000, transcendentals=0),
+        name=name,
+    )(at, *[array for array, _, _ in operands])
+
+
+def source(g, at):
+    return (at[1] + 2 + g) % SIDE
+
+
+def by_source(rank, axis):
+    return lambda g, at: tuple(source(g, at) if n == axis else 0 for n in range(rank))
+
+
+def fixed(array):
+    return array, array.shape, lambda g, at: (0,) * array.ndim
+
+
+def moe_before(at, cot, down):
+    _, _, padded, width = cot.shape
+    tokens, slots, ff = padded - 16, SIDE * CAP, down.shape[1]
+    return over_sources(
+        pick_kernel,
+        at,
+        [(cot, (1, SIDE, padded, width), by_source(4, 0)), fixed(down)],
+        [
+            (((SIDE * SIDE, 2 * CAP, tokens), BF), (SIDE, 2 * CAP, tokens), by_source(3, 0)),
+            (((2, SIDE * slots, width), BF), (2, slots, width), by_source(3, 1)),
+            (((2, SIDE * slots, ff), F32), (2, slots, ff), by_source(3, 1)),
+        ],
+        [],
+        4_000_000_000,
+        "moe_before",
+    )
+
+
+def moe(at, rows, cot, pick, raw, router_t, gate, up):
+    _, _, tokens, width = rows.shape
+    padded = cot.shape[2]
+    ff, slots, half = gate.shape[2], SIDE * CAP, width // 2
+
+    def first(g, at):
+        return ((2 + g) % SIDE, 0, 0, 0)
+
+    def second(g, at):
+        return (0, (2 + g) % SIDE, 0, 0)
+
+    def kept(cols, dtype):
+        return ((2, SIDE * slots, cols), dtype), (2, slots, cols), by_source(3, 1)
+
+    return over_sources(
+        moe_kernel,
+        at,
+        [
+            (rows, (1, SIDE, tokens, width), by_source(4, 0)),
+            (cot, (1, SIDE, 16, width), lambda g, at: (source(g, at), 0, tokens // 16, 0)),
+            (pick, (SIDE, 2 * CAP, tokens), by_source(3, 0)),
+            (raw, (2, slots, ff), by_source(3, 1)),
+            fixed(router_t),
+            fixed(gate),
+            fixed(up),
+        ],
+        [
+            (((SIDE, SIDE, padded, half), BF), (1, SIDE, padded, half), first),
+            (((SIDE, SIDE, padded, half), BF), (SIDE, 1, padded, half), second),
+            kept(width, BF),
+            kept(ff, BF),
+            kept(ff, BF),
+            kept(ff, BF),
+            kept(ff, BF),
+            kept(1, F32),
+        ],
+        [pltpu.VMEM((2, slots, 1), F32), pltpu.VMEM((SIDE, 2 * CAP, width), BF)],
+        14_000_000_000,
+        "moe",
+    )
+
+
+def moe_result(at, hidden, share, pick, down):
+    slots, ff, width = SIDE * CAP, hidden.shape[2], down.shape[2]
+    tokens = pick.shape[2]
+
+    def part(array):
+        return array, (2, slots, array.shape[2]), by_source(3, 1)
+
+    return over_sources(
+        result_kernel,
+        at,
+        [part(hidden), part(share)]
+        + [(pick, (SIDE, 2 * CAP, tokens), by_source(3, 0)), fixed(down)],
+        [
+            (((SIDE, SIDE, tokens, width), BF), (1, SIDE, tokens, width), by_source(4, 0)),
+        ],
+        [pltpu.VMEM((SIDE, 2 * CAP, width), BF)],
+        4_000_000_000,
+        "moe_result",
+    )[0]
+
+
+def middle_kernel(at_ref, a0_ref, a1_ref, a2_ref, a3_ref, x_ref, w_ref, gain_ref, mid_ref, low_ref):
+    z = at_ref[0]
+    cols = a0_ref.shape[1]
+    total = x_ref[...].astype(F32)
+    for r, a_ref in enumerate((a0_ref, a1_ref, a2_ref, a3_ref)):
+        there = pl.ds(pl.multiple_of(lax.rem(z - r + SIDE, SIDE) * cols, cols), cols)
+        total = total + nn(a_ref[...], w_ref[there])
+    mid_ref[...] = total
+    scale = lax.rsqrt(jnp.mean(total * total, axis=-1, keepdims=True) + epsilon)
+    low_ref[...] = (total * scale * gain_ref[...]).astype(BF)
+
+
+def in_vmem(kernel, at, operands, shapes, scratch, flops, name):
+    def whole(shape):
+        return pl.BlockSpec(shape, lambda g, at: (0,) * len(shape))
+
+    return pl.pallas_call(
+        kernel,
+        grid_spec=pltpu.PrefetchScalarGridSpec(
+            num_scalar_prefetch=1,
+            grid=(1,),
+            in_specs=[whole(a.shape) for a in operands],
+            out_specs=[whole(shape) for shape, _ in shapes],
+            scratch_shapes=scratch,
         ),
-        name="moe",
-    )(at, rows, cot, router_t, gate, up, down)
-
-
-def rms_apply(values, gain):
-    scale = lax.rsqrt(jnp.mean(values * values, axis=-1, keepdims=True) + epsilon)
-    return (values * scale * gain, scale)
+        out_shape=[jax.ShapeDtypeStruct(shape, dtype) for shape, dtype in shapes],
+        compiler_params=pltpu.CompilerParams(vmem_limit_bytes=56 * MIB),
+        cost_estimate=pl.CostEstimate(flops=flops, bytes_accessed=8_000_000, transcendentals=0),
+        name=name,
+    )(at, *operands)
+
+
+def post_kernel(
+    at_ref,
+    a0_ref,
+    a1_ref,
+    a2_ref,
+    b0_ref,
+    b1_ref,
+    b2_ref,
+    mid_ref,
+    low_ref,
+    gain_ref,
+    router_ref,
+    routes_ref,
+    cot_ref,
+    w_ref,
+    d_mid_ref,
+    branch_ref,
+    att0_ref,
+    att1_ref,
+    att2_ref,
+    att3_ref,
+    router_grad_ref,
+    gain_grad_ref,
+):
+    z, core = at_ref[0], at_ref[6]
+    tokens = mid_ref.shape[0]
+    chips = SIDE * SIDE
+    cols = att0_ref.shape[1]
+    side_a = a0_ref[...].astype(F32) + a1_ref[...].astype(F32) + a2_ref[...].astype(F32)
+    side_b = b0_ref[...].astype(F32) + b1_ref[...].astype(F32) + b2_ref[...].astype(F32)
+    found = side_a[tokens:] + side_b[tokens:]
+    d_gates = jnp.concatenate([found[:, :tokens], found[:, tokens:]], axis=0)
+    line = lax.broadcasted_iota(jnp.int32, (2 * chips, tokens), 0)
+    second = line >= chips
+    expert = 2 * jnp.where(second, line - chips, line) + jnp.where(second, 1 - core, core)
+    expert = expert.astype(F32)
+    routes = routes_ref[...].astype(F32)
+    chosen = expert == routes[0:1]
+    for k in range(1, TOP):
+        chosen = chosen | (expert == routes[k : k + 1])
+    logits = nt(router_ref[...], low_ref[...])
+    top = jnp.max(jnp.where(chosen, logits, masked), axis=0, keepdims=True)
+    expo = jnp.where(chosen, jnp.exp(jnp.minimum(logits - top, 0.0)), 0.0)
+    share = expo / jnp.sum(expo, axis=0, keepdims=True)
+    d_gates = jnp.where(chosen, d_gates, 0.0)
+    d_logits = share * (d_gates - jnp.sum(share * d_gates, axis=0, keepdims=True))
+    d_logits = d_logits.astype(BF)
+    router_grad_ref[...] = nn(d_logits, low_ref[...])
+    d_normed = jnp.concatenate([side_a[:tokens], side_b[:tokens]], axis=1)
+    d_normed = d_normed + tn(d_logits, router_ref[...])
+    mid = mid_ref[...]
+    scale = lax.rsqrt(jnp.mean(mid * mid, axis=-1, keepdims=True) + epsilon)
+    gain_grad_ref[...] = jnp.sum(d_normed * mid * scale, axis=0, keepdims=True)
+    weighted = d_normed * gain_ref[...]
+    inner = jnp.mean(weighted * mid, axis=-1, keepdims=True)
+    d_mid = cot_ref[...].astype(F32) + scale * weighted - mid * (scale * scale * scale) * inner
+    d_mid_ref[...] = d_mid
+    branch = d_mid.astype(BF)
+    branch_ref[...] = branch
+    for r, att_ref in enumerate((att0_ref, att1_ref, att2_ref, att3_ref)):
+        there = pl.ds(pl.multiple_of(lax.rem(z + r, SIDE) * cols, cols), cols)
+        att_ref[...] = nt(branch, w_ref[there]).astype(BF)
+
+
+def weights_kernel(at_ref, normed_ref, dqkv_ref, att_ref, b0_ref, b1_ref, b2_ref, b3_ref, out_ref):
+    cols = dqkv_ref.shape[1]
+    rows, heads = att_ref.shape[1:]
+    out_ref[:, :cols] = tn(normed_ref[...], dqkv_ref[...]).astype(BF)
+    total = None
+    for r, b_ref in enumerate((b0_ref, b1_ref, b2_ref, b3_ref)):
+        part = tn(att_ref[(SIDE - r) % SIDE], b_ref[...])
+        total = part if total is None else total + part
+    total = total.astype(BF)
+    for n in range(total.shape[1] // heads):
+        out_ref[n * heads : (n + 1) * heads, cols:] = total[:, n * heads : (n + 1) * heads]
+
+
+def finish_kernel(at_ref, *refs):
+    pieces, (wq_ref, wk_ref, wv_ref, gain_ref) = refs[:16], refs[16:20]
+    q_ref, k_ref, v_ref, o_ref, gain_grad_ref = refs[20:]
+    z, x_at, y_at, core = at_ref[0], at_ref[1], at_ref[2], at_ref[6]
+    width = q_ref.shape[0]
+    heads, kv = width // SIDE, k_ref.shape[1] // SIDE
+    rows = width // (2 * SIDE * SIDE)
+    for own in range(2):
+        base = jnp.where(core == own, 0, width // 2)
+        for side in range(2):
+            for far in range(SIDE):
+                ref = pieces[own * 8 + side * 4 + far]
+
+                for near in range(SIDE):
+                    rx, ry = (far, near) if side == 0 else (near, far)
+                    xs, ys = lax.rem(x_at + rx, SIDE), lax.rem(y_at + ry, SIDE)
+                    row = pl.multiple_of(base + (xs * SIDE + ys) * rows, rows)
+                    here = pl.ds(row, rows)
+                    group = lax.div(row, heads)
+                    inside = row - group * heads
+                    at_o = pl.ds(pl.multiple_of(group * heads, heads), heads)
+                    for rz in range(SIDE):
+                        zs = lax.rem(z + rz, SIDE)
+                        block = ref[near, rz].astype(F32)
+                        at_q = pl.ds(pl.multiple_of(zs * heads, heads), heads)
+                        at_k = pl.ds(pl.multiple_of(zs * kv, kv), kv)
+                        if side == 0:
+                            q_ref[here, at_q] = block[:, :heads]
+                            k_ref[here, at_k] = block[:, heads:]
+                        else:
+                            v_ref[here, at_k] = block[:, :kv]
+                            o_row = pl.multiple_of(zs * heads + inside, rows)
+                            o_ref[pl.ds(o_row, rows), at_o] = block[:, kv:]
+    for n in range(SIDE):
+        here = slice(n * heads, (n + 1) * heads)
+        total = jnp.sum(q_ref[here] * wq_ref[here].astype(F32), axis=1, keepdims=True)
+        total = total + jnp.sum(k_ref[here] * wk_ref[here].astype(F32), axis=1, keepdims=True)
+        total = total + jnp.sum(v_ref[here] * wv_ref[here].astype(F32), axis=1, keepdims=True)
+        gain_grad_ref[here] = total / gain_ref[here]
 
 
 def rms_back(values, scale, gain, upstream):
@@ -600,18 +794,16 @@
     expert_at = lax.axis_index("expert")
     chip, core = expert_at // 2, expert_at % 2
     x_at, y_at = chip // SIDE, chip % SIDE
-    at = jnp.stack([z, x_at, y_at, chip, expert_at, expert_at + 1 - 2 * core]).astype(jnp.int32)
+    at = jnp.stack([z, x_at, y_at, chip, expert_at, expert_at + 1 - 2 * core, core])
+    at = at.astype(jnp.int32)
 
     own = block_input[0]
+    route_rows = jnp.full((16, width), -1.0, BF)
+    route_rows = lax.dynamic_update_slice(route_rows, expert_routes[0].T.astype(BF), (0, 0))
+    cot_rows = jnp.concatenate([cotangent[0], route_rows], axis=0)
+    own, cot_rows = tied(own, cot_rows)
+    cot_all = lax.all_gather(cot_rows, "expert", axis_index_groups=plane_groups())
     x_rel = [own, along_z(own, 1), along_z(own, 2), along_z(own, -1)]
-    routes = expert_routes[0]
-    route_rows = jnp.full((16, width), -1.0, BF)
-    route_rows = lax.dynamic_update_slice(route_rows, routes.T.astype(BF), (0, 0))
-    cot_all = lax.all_gather(
-        jnp.concatenate([cotangent[0], route_rows], axis=0),
-        "expert",
-        axis_index_groups=plane_groups(),
-    ).reshape(SIDE, SIDE, tokens + 16, width)
 
     doc = document_ids[0]
     below_one = jnp.sum((doc < 1).astype(jnp.int32))
@@ -640,80 +832,118 @@
     )
     q_cols, k_cols = q.shape[1], k.shape[1]
 
-    def from_heads(pieces):
-        whole = jnp.zeros((tokens, SIDE, pieces[0].shape[1]), pieces[0].dtype)
-        for r, piece in enumerate(pieces):
-            whole = lax.dynamic_update_slice(whole, piece[:, None], (0, (z - r) % SIDE, 0))
-        return whole
-
-    attended = from_heads(
-        [out_rel[0], along_z(out_rel[1], 1), along_z(out_rel[2], 2), along_z(out_rel[3], -1)]
-    ).reshape(tokens, SIDE * q_cols)
-    inputs = own.astype(F32)
-    middle = inputs + nn(attended, output_proj)
-    normed_two, scale_two = rms_apply(middle, ffn_norm_gain)
-    normed_two = normed_two.astype(BF)
-    rows_all = lax.all_gather(
-        normed_two, "expert", axis_index_groups=plane_groups()
-    ).reshape(SIDE, SIDE, tokens, width)
+    att_rel = [out_rel[0]] + [along_z(out_rel[r], t) for r, t in ((1, 1), (2, 2), (3, -1))]
+    middle, normed_two = in_vmem(
+        middle_kernel,
+        at,
+        [*att_rel, own, output_proj, ffn_norm_gain[None]],
+        [((tokens, width), F32), ((tokens, width), BF)],
+        [],
+        600_000_000,
+        "middle",
+    )
+    normed_two, cot_all = tied(normed_two, cot_all)
+    rows_all = lax.all_gather(normed_two, "expert", axis_index_groups=plane_groups())
     gate_two = jnp.concatenate([expert_gate, swap_core(expert_gate)], axis=0)
     up_two = jnp.concatenate([expert_up, swap_core(expert_up)], axis=0)
     down_two = jnp.concatenate([expert_down, swap_core(expert_down)], axis=0)
-    out_a, out_b, back_a, back_b, kept_x, kept_dg, kept_du, kept_h, kept_s = moe(
-        at, rows_all, cot_all, router_proj.T, gate_two, up_two, down_two
-    )
-
-    logits = nn(normed_two, router_proj)
-    experts = jnp.arange(experts_all, dtype=jnp.int32)
-    chosen = jnp.any(routes[:, :, None] == experts[None, None, :], axis=1)
-    logits = jnp.where(chosen, logits, masked)
-    expo = jnp.where(chosen, jnp.exp(logits - jnp.max(logits, axis=-1, keepdims=True)), 0.0)
-    gate_rows = expo / jnp.sum(expo, axis=-1, keepdims=True)
-
-    sum_a, sum_b = plane_sum(back_a, back_b)
-    back_sum = jnp.concatenate([sum_a[:tokens], sum_b[:tokens]], axis=1)
-    d_gates = (sum_a[tokens:] + sum_b[tokens:]).reshape(SIDE * SIDE, 2, tokens)
-    d_gates = jnp.where(core == 0, d_gates, d_gates[:, ::-1]).reshape(experts_all, tokens).T
-    d_gates = jnp.where(chosen, d_gates, 0.0)
+    cot_all = cot_all.reshape(SIDE, SIDE, tokens + 16, width)
+    pick, upstream, raw = moe_before(at, cot_all, down_two)
+    back_a, back_b, kept_x, kept_dg, kept_du, kept_h, kept_s, share = moe(
+        at,
+        rows_all.reshape(SIDE, SIDE, tokens, width),
+        cot_all,
+        pick,
+        raw,
+        router_proj.T,
+        gate_two,
+        up_two,
+    )
+    out = moe_result(at, kept_h, share, pick, down_two)
 
     def slots_grad(a, b):
         return jnp.einsum("jrd,jrf->jdf", a, b, preferred_element_type=F32).astype(BF)
 
-    whole_w = jnp.stack(
-        [slots_grad(kept_x, kept_dg), slots_grad(kept_x, kept_du), slots_grad(kept_s, kept_h)],
-        axis=1,
-    )
+    first_a, first_b = ring_start(back_a, along_x), ring_start(back_b, along_y)
+    gate_w = slots_grad(kept_x, kept_dg)
+    up_a, down_a = ring_operands(back_a, first_a)
+    up_b, down_b = ring_operands(back_b, first_b)
+    up_a, down_a, up_b, down_b = tied(up_a, down_a, up_b, down_b)
+    second_a = along_x(up_a, 1), along_x(down_a, -1)
+    second_b = along_y(up_b, 1), along_y(down_b, -1)
+    up_w = slots_grad(kept_x, kept_du)
+    down_w = slots_grad(upstream, kept_s)
+    second_a, second_b, gate_w, up_w, down_w, out = tied(
+        second_a, second_b, gate_w, up_w, down_w, out
+    )
+    whole_w = jnp.stack([gate_w, up_w, down_w], axis=1)
     whole_w = (whole_w[0].astype(F32) + swap_core(whole_w[1]).astype(F32)).astype(BF)
-    expert_sum = lax.psum_scatter(whole_w, "dp", scatter_dimension=1, tiled=True).astype(F32)
-    gate_grad, up_grad = expert_sum[0:1], expert_sum[1:2]
-    down_grad = jnp.transpose(expert_sum[2:3], (0, 2, 1))
-
-    upstream = cotangent[0].astype(F32)
-    d_chosen = gate_rows * (d_gates - jnp.sum(gate_rows * d_gates, axis=-1, keepdims=True))
-    d_logits = d_chosen.astype(BF)
-    router_local = tn(d_logits, normed_two)
-    d_normed_two = back_sum + nt(d_logits, router_proj)
-    ffn_gain_local = jnp.sum(d_normed_two * middle * scale_two, axis=0)
-    d_middle = upstream + rms_back(middle, scale_two, ffn_norm_gain, d_normed_two)
-    d_branch = d_middle.astype(BF)
-    d_attended = nt(d_branch, output_proj).astype(BF).reshape(tokens, SIDE, q_cols)
-
-    def heads_of(r):
-        return lax.dynamic_index_in_dim(d_attended, (z + r) % SIDE, axis=1, keepdims=False)
-
-    d_rel = [heads_of(0)] + [along_z(heads_of(r), s) for r, s in ((1, 1), (2, 2), (3, -1))]
+    expert_sum = lax.psum_scatter(whole_w, "dp", scatter_dimension=1, tiled=True)
+    part_a, part_b = low(ring_end(back_a, second_a)), low(ring_end(back_b, second_b))
+    part_a, part_b = tied(part_a, part_b)
+    first_a, first_b = ring_start(part_a, along_y), ring_start(part_b, along_x)
+    up_a, down_a = ring_operands(part_a, first_a)
+    up_b, down_b = ring_operands(part_b, first_b)
+    up_a, down_a, up_b, down_b = tied(up_a, down_a, up_b, down_b)
+    second_a = along_y(up_a, 1), along_y(down_a, -1)
+    second_b = along_x(up_b, 1), along_x(down_b, -1)
+
+    chips = SIDE * SIDE
+    router_two = router_proj.T.reshape(chips, 2, width)
+    router_two = jnp.where(core == 0, router_two, router_two[:, ::-1])
+    router_two = router_two.transpose(1, 0, 2).reshape(experts_all, width)
+    d_middle, d_branch, *d_att, router_local, ffn_gain_local = in_vmem(
+        post_kernel,
+        at,
+        [part_a[0], *second_a, part_b[0], *second_b, middle, normed_two, ffn_norm_gain[None]]
+        + [router_two, route_rows[:, :tokens], cotangent[0], output_proj],
+        [
+            ((tokens, width), F32),
+            ((tokens, width), BF),
+            *[((tokens, q_cols), BF)] * SIDE,
+            ((experts_all, width), F32),
+            ((1, width), F32),
+        ],
+        [],
+        600_000_000,
+        "post",
+    )
+
+    *d_att, out = tied(*d_att, out)
+    d_rel = [d_att[0]] + [along_z(d_att[r], t) for r, t in ((1, 1), (2, 2), (3, -1))]
+    out = lax.psum_scatter(
+        out.reshape(chips * tokens, width),
+        "expert",
+        axis_index_groups=plane_groups(),
+        scatter_dimension=0,
+        tiled=True,
+    )
+    d_rel[1], d_branch_sent = tied(d_rel[1], d_branch)
+    branch_rel = [d_branch] + [along_z(d_branch_sent, t) for t in (1, 2, -1)]
+    router_local = jnp.where(core == 0, router_local, jnp.roll(router_local, chips, axis=0))
+    few = jnp.concatenate([router_local, ffn_gain_local], axis=0)
+    few = jnp.concatenate([few, jnp.zeros((15, width), F32)], axis=0).astype(BF)
+    few, d_rel[2] = tied(few, d_rel[2])
+    few = few.astype(F32) + sum(along_z(few, t).astype(F32) for t in (1, 2, -1))
+    few = lax.dynamic_slice_in_dim(few[: experts_all + 1], z * q_cols, q_cols, axis=1)
+    few = few.reshape(-1, 3 * q_cols)
+    few = jnp.pad(few, ((0, 16 - few.shape[0]), (0, 0))).astype(BF)
     dqkv, gains = attend_back(
         at, d_rel, q, k, v, q_raw, k_raw, query_gain, key_gain, cosine, sine, start
     )
-    output_local = tn(attended, d_branch)
-    early = jnp.concatenate(
-        [output_local, router_local, jnp.pad(ffn_gain_local[None], ((0, 15), (0, 0)))], axis=0
-    )
-    early = lax.psum(early.astype(BF), ("dp", "expert"))
-
-    local = tn(normed_all, dqkv).astype(BF)
-    tail = jnp.concatenate([gains[0], gains[1]])
+
+    local = in_vmem(
+        weights_kernel,
+        at,
+        [normed_all, dqkv, out_rel, *branch_rel],
+        [((width, 2 * q_cols + 2 * k_cols), BF)],
+        [],
+        1_600_000_000,
+        "weights",
+    )[0]
+    tail = jnp.concatenate([gains[0], gains[1], jnp.zeros_like(gains[0])])
     tail = jnp.pad(tail[None], ((0, 15), (0, 0))).astype(BF)
+    tail = jnp.concatenate([tail, few], axis=0)
     half = width // 2
     mine = lax.dynamic_slice_in_dim(local, core * half, half, axis=0)
     other = lax.dynamic_slice_in_dim(local, (1 - core) * half, half, axis=0)
@@ -722,70 +952,73 @@
     tail = (tail.astype(F32) + got[half:]).astype(BF)
     part, tail = scatter_sum(part, tail, x_at, along_x)
     part, tail = scatter_sum(part, tail, y_at, along_y)
-    part = gather_rows(part, y_at, along_y)
-    part = gather_rows(part, x_at, along_x)
-    part = jnp.concatenate([part, tail], axis=0)
-    blocks = gather_heads(part, z)
-    tails = jnp.sum(blocks[:, half].astype(F32), axis=0)
-    query_gain_sum = jnp.sum(tails[:q_cols].reshape(-1, head), axis=0)
-    key_gain_sum = jnp.sum(tails[q_cols : q_cols + k_cols].reshape(-1, head), axis=0)
-    blocks = blocks[:, :half]
-    blocks_other = swap_core(blocks)
-    both = jnp.where(
-        core == 0, jnp.stack([blocks, blocks_other]), jnp.stack([blocks_other, blocks])
-    )
-    both = both.transpose(0, 2, 1, 3).reshape(width, SIDE, q_cols + 2 * k_cols).astype(F32)
-    query_sum = both[:, :, :q_cols].reshape(width, -1)
-    key_sum = both[:, :, q_cols : q_cols + k_cols].reshape(width, -1)
-    value_sum = both[:, :, q_cols + k_cols :].reshape(width, -1)
-    attn_gain_sum = (
-        jnp.sum(query_sum * query_proj.astype(F32), axis=1)
-        + jnp.sum(key_sum * key_proj.astype(F32), axis=1)
-        + jnp.sum(value_sum * value_proj.astype(F32), axis=1)
-    ) / attn_norm_gain
-
-    def block_of(r):
-        return block_at(dqkv, z + r, tokens)
-
-    back = from_heads(
-        [block_of(0)] + [along_z(block_of(r), s) for r, s in ((1, 1), (2, 2), (3, -1))]
-    )
+    pieces = jnp.stack(ring_pieces(jnp.concatenate([part, tail], axis=0), along_z))
+    rows = part.shape[0]
+    gain_sums = jnp.sum(pieces[:, rows].astype(F32), axis=0)
+    few = pieces[:, rows + 16 : rows + 16 + (experts_all + 1) * q_cols // (3 * q_cols)]
+    few = few.astype(F32).reshape(SIDE, experts_all + 1, q_cols)
+    few = jnp.roll(few, z, axis=0).transpose(1, 0, 2).reshape(experts_all + 1, width)
+    router_sum = few[:experts_all].reshape(2, chips, width).transpose(2, 1, 0)
+    router_sum = router_sum.reshape(width, experts_all)
+    split = q_cols + k_cols
+    side_a, side_b = pieces[:, :rows, :split], pieces[:, :rows, split:]
+    side_a = jnp.stack(ring_pieces(side_a, along_y))
+    side_b = jnp.stack(ring_pieces(side_b, along_x))
+    ends = ring_pieces(side_a, along_x) + ring_pieces(side_b, along_y)
+    ends = ends + [swap_core(piece) for piece in ends]
+    query_sum, key_sum, value_sum, output_sum, attn_gain_sum = in_vmem(
+        finish_kernel,
+        at,
+        [*ends, query_proj, key_proj, value_proj, attn_norm_gain[:, None]],
+        [
+            ((width, SIDE * q_cols), F32),
+            ((width, SIDE * k_cols), F32),
+            ((width, SIDE * k_cols), F32),
+            ((SIDE * q_cols, width), F32),
+            ((width, 1), F32),
+        ],
+        [],
+        10_000_000,
+        "finish",
+    )
+    query_gain_sum = jnp.sum(gain_sums[:q_cols].reshape(-1, head), axis=0)
+    key_gain_sum = jnp.sum(gain_sums[q_cols : q_cols + k_cols].reshape(-1, head), axis=0)
+
+    expert_sum = expert_sum.astype(F32)
+    gate_grad, up_grad = expert_sum[0:1], expert_sum[1:2]
+    down_grad = jnp.transpose(expert_sum[2:3], (0, 2, 1))
+
+    back = jnp.zeros((tokens, SIDE, q_cols + 2 * k_cols), BF)
+    for r, step in ((0, 0), (1, 1), (2, 2), (3, -1)):
+        piece = block_at(dqkv, z + r, tokens)
+        piece = along_z(piece, step) if step else piece
+        back = lax.dynamic_update_slice(back, piece[:, None], (0, (z - r) % SIDE, 0))
     d_query = back[:, :, :q_cols].reshape(tokens, -1)
     d_key = back[:, :, q_cols : q_cols + k_cols].reshape(tokens, -1)
     d_value = back[:, :, q_cols + k_cols :].reshape(tokens, -1)
     d_normed = nt(d_query, query_proj) + nt(d_key, key_proj) + nt(d_value, value_proj)
+    inputs = own.astype(F32)
     scale_one = lax.rsqrt(jnp.mean(inputs * inputs, axis=-1, keepdims=True) + epsilon)
     input_grad = d_middle + rms_back(inputs, scale_one, attn_norm_gain, d_normed)
 
-    out_a, out_b, _ = tied(out_a, out_b, d_branch)
-    out_a, out_b = plane_sum(out_a, out_b)
-    block_output = (middle + jnp.concatenate([out_a, out_b], axis=1)).astype(BF)
-
-    early = early.astype(F32)
+    block_output = (middle + out.astype(F32)).astype(BF)
+
     return (
         block_output[None],
         input_grad[None],
-        attn_gain_sum,
+        attn_gain_sum[:, 0],
         query_sum,
         key_sum,
         value_sum,
         query_gain_sum,
         key_gain_sum,
-        early[:width],
-        early[width + experts_all],
-        early[width : width + experts_all].T,
+        output_sum,
+        few[experts_all],
+        router_sum,
         gate_grad,
         up_grad,
         down_grad,
     )
-
-
-def gather_heads(part, z):
-    pieces = [part, along_z(part, 1), along_z(part, 2), along_z(part, -1)]
-    whole = jnp.zeros((SIDE,) + part.shape, part.dtype)
-    for r, piece in enumerate(pieces):
-        whole = lax.dynamic_update_index_in_dim(whole, piece, (z - r) % SIDE, 0)
-    return whole
 
 
 def solution(mesh):

time: 623 us -> 462 us (0.74)
  the two profiles are of different devices: /device:TPU:6 before, /device:TPU:7 now
where the time goes in v2:
time: 462 us; the launch traced here: 453 us
  waiting for transfers between devices  166 us (36%)
  Pallas kernels  102 us (22%)
  starting transfers between devices  79.5 us (17%)
  other arithmetic  36.1 us (8%)
  local copies, waits for them, and re-layouts  33.1 us (7%)
  matrix products  20.4 us (4%)
  between operations  15.3 us (3%)
    all_gather x1, waiting for transfers between devices, body(): lax.all_gather(normed_two, 'expert', axis_index_groups=plane_groups())  52.9 us
    pallas_call x3, Pallas kernels, over_sources(): pl.pallas_call(kernel, grid_spec=pltpu.PrefetchScalarGridSpec(num_scalar_...  49 us
    ppermute x21, waiting for transfers between devices, along_z(): lax.ppermute(value, 'dp', [(i, (i + step) % SIDE) for i in range(SIDE)])  42.7 us
    ppermute x21, starting transfers between devices, along_z(): lax.ppermute(value, 'dp', [(i, (i + step) % SIDE) for i in range(SIDE)])  29.3 us
    pallas_call x4, Pallas kernels, in_vmem(): pl.pallas_call(kernel, grid_spec=pltpu.PrefetchScalarGridSpec(num_scalar_...  28.1 us
    ppermute x17, waiting for transfers between devices, along_x(): return lax.ppermute(value, 'expert', step_pairs(step, 0))  27.1 us
    ppermute x17, starting transfers between devices, along_x(): return lax.ppermute(value, 'expert', step_pairs(step, 0))  19.9 us
    ppermute x17, waiting for transfers between devices, along_y(): return lax.ppermute(value, 'expert', step_pairs(0, step))  19.3 us
  transfers between devices with their start and end apart: 72, of which 27 were waited for; matrix products, arithmetic and copies ran while one was open for 15% of the time, Pallas kernels for 17%

profile of v2, /device:TPU:7, one launch (start us, length us, event | category | flops | bytes accessed | tf_op | source)
XLA Modules:
  0.0 452.5 jit_solution(3851546744641705596)
XLA Ops:
  11.6 3.3 collective-permute-start.1
  23.3 2.2 collective-permute-done.refs_2_
  25.6 12.1 %collective-permute-done.1.refs_3_ = bf16[256,1024]{1,0:T(8,128)(2,1)S(1)} collective-permute-done((bf16[256,1024]{1,0:T(8,128)(2,1)}, bf16[256,1024]{1,0:T(8,128)(2,1)S(1)}, u32[]{:S(2)}, u32[]{:S(2)}) %collective-permute-start.1) | collective-permute-done | bytes 524320 | tf_op jit(solution)/shard_map/ppermute | solution.py:43
  39.5 10.5 %attend.1 = (bf16[1024,1024]{1,0:T(8,128)(2,1)}, bf16[1024,256]{1,0:T(8,128)(2,1)S(1)}, bf16[1024,128]{1,0:T(8,128)(2,1)S(1)}, bf16[1024,128]{1,0:T(8,128)(2,1)S...) custom-call(s32[7]{0:T(128)S(1)} %stack.88.refs_0_.at_ref, ...), custom_call_target="tpu_custom_call" | custom-call | flops 6000000000 | bytes 12000000 | tf_op jit(solution)/shard_map/attend/pallas_call | solution.py:224
  54.0 2.5 collective-permute-start.4
  58.5 3.9 collective-permute-done.4.a2_ref
  63.1 4.4 middle.1
  67.6 18.5 %all-gather.5.cloned.1.call-done = bf16[4352,1024]{1,0:T(8,128)(2,1)} async-done(((bf16[272,1024]{1,0:T(8,128)(2,1)}), bf16[4352,1024]{1,0:T(8,128)(2,1)}) %all-gather.5.cloned.1.call-update) | async-done | bytes 8912912 | tf_op jit(solution)/shard_map/all_gather | solution.py:805
  87.7 2.3 constant_dynamic-update-slice_fusion.1
  94.0 12.3 %moe_before.1 = (bf16[16,160,256]{2,1,0:T(8,128)(2,1)}, bf16[2,1280,1024]{2,1,0:T(8,128)(2,1)}, f32[2,1280,512]{2,1,0:T(8,128)}) custom-call(s32[7]{0:T(128)} %copy-done.5, bf16[4,4,272,1024]{3,2,1,0:T(8,128)(2,1)} %bitcast.201, bf16[2,512,1024]{2,1,0:T(8,128)(2,1)} %constant_dynamic-update-slice_fusion.down_ref), custom_call_target="tpu_custom_call" | custom-call | flops 4000000000 | bytes 30000000 | tf_op jit(solution)/shard_map/moe_before/pallas_call | solution.py:507
  106.3 52.9 %all-gather.7.cloned.1.call-done = bf16[4096,1024]{1,0:T(8,128)(2,1)} async-done(((bf16[256,1024]{1,0:T(8,128)(2,1)}), bf16[4096,1024]{1,0:T(8,128)(2,1)}) %all-gather.7.cloned.1.call-update) | async-done | bytes 8388624 | tf_op jit(solution)/shard_map/all_gather | solution.py:846
  159.2 26.2 %moe.1 = (bf16[4,4,272,512]{3,2,1,0:T(8,128)(2,1)}, bf16[4,4,272,512]{3,2,1,0:T(8,128)(2,1)}, bf16[2,1280,1024]{2,1,0:T(8,128)(2,1)}, bf16[2,1280,512]{2,1,0:T(8...) custom-call(s32[7]{0:T(128)} %copy-done.5, ...), custom_call_target="tpu_custom_call" | custom-call | flops 14000000000 | bytes 30000000 | tf_op jit(solution)/shard_map/moe/pallas_call | solution.py:507
  188.0 2.1 collective-permute-start.9
  192.0 8.0 %convolution_convert_fusion.2 = bf16[2,1024,512]{2,1,0:T(8,128)(2,1)} fusion(bf16[2,1280,1024]{2,1,0:T(8,128)(2,1)} %get-tuple-element.95, bf16[2,1280,512]{2,1,0:T(8,128)(2,1)S(1)} %copy-done.54), kind=kOutput, calls=%fused_computation.15 | convolution fusion | flops 2685403136 | bytes 9961472 | tf_op jit(solution)/shard_map/jrd,jrf->jdf/dot_general | solution.py:865
  200.1 4.1 convolution_convert_fusion.1
  211.7 2.6 collective-permute-start.16
  214.4 10.5 %moe_result.1 = bf16[4,4,256,1024]{3,2,1,0:T(8,128)(2,1)} custom-call(s32[7]{0:T(128)} %copy-done.5, bf16[2,1280,512]{2,1,0:T(8,128)(2,1)} %get-tuple-element.100.hidden_ref, f32[2,1280,1]{2,1,0:T(8,128)} %get-tuple-element.101.share_ref, bf16[16,160,256]{2,1,0:T(8,128)(2,1)} %get-tuple-element.87.pick_ref, ...), custom_call_target="tpu_custom_call" | custom-call | flops 4000000000 | bytes 30000000 | tf_op jit(solution)/shard_map/moe_result/pallas_call | solution.py:507
  224.8 6.4 %convolution_convert_fusion = bf16[2,1024,512]{2,1,0:T(8,128)(2,1)S(1)} fusion(bf16[2,1280,1024]{2,1,0:T(8,128)(2,1)} %get-tuple-element.98, bf16[2,1280,512]{2,1,0:T(8,128)(2,1)} %get-tuple-element.99), kind=kOutput, calls=%fused_computation.13 | convolution fusion | flops 2685403136 | bytes 9961472 | tf_op jit(solution)/shard_map/jrd,jrf->jdf/dot_general | solution.py:865
  231.2 3.6 collective-permute-done.13
  237.9 3.4 collective-permute-start.67
  241.3 5.3 %collective-permute-done.67 = bf16[3,1024,512]{2,1,0:T(8,128)(2,1)S(1)} collective-permute-done((bf16[3,1024,512]{2,1,0:T(8,128)(2,1)S(1)}, bf16[3,1024,512]{2,1,0:T(8,128)(2,1)S(1)}, u32[]{:S(2)}, u32[]{:S(2)}) %collective-permute-start.67) | collective-permute-done | bytes 3145760 | tf_op jit(solution)/shard_map/ppermute | solution.py:47
  246.5 2.8 fusion
  251.5 3.5 fusion.2
  255.0 2.7 collective-permute-start.18
  257.9 2.7 collective-permute-start.19
  260.6 3.1 collective-permute-done.17
  263.9 2.7 collective-permute-start.22
  266.6 2.4 collective-permute-start.23
  272.9 3.1 collective-permute-done.24.b2_ref
  276.7 6.3 %post.1 = (f32[256,1024]{1,0:T(8,128)}, bf16[256,1024]{1,0:T(8,128)(2,1)}, bf16[256,256]{1,0:T(8,128)(2,1)}, bf16[256,256]{1,0:T(8,128)(2,1)}, bf16[256,256]{1,0...) custom-call(s32[7]{0:T(128)} %copy-done.5, ...), custom_call_target="tpu_custom_call" | custom-call | flops 600000000 | bytes 8000000 | tf_op jit(solution)/shard_map/post/pallas_call | solution.py:632
  283.9 3.2 collective-permute-start.26
  287.7 3.2 collective-permute-done.26.refs_3_
  293.7 2.3 collective-permute-start.32
  298.3 14.7 %attend_back.1 = (bf16[1024,512]{1,0:T(8,128)(2,1)S(1)}, f32[8,256]{1,0:T(8,128)S(1)}) custom-call(s32[7]{0:T(128)S(1)} %copy-done.6, bf16[256,256]{1,0:T(8,128)(2,1)S(1)} %copy-done.10, bf16[256,256]{1,0:T(8,128)(2,1)S(1)} %collective-permute-done.25.refs_2_, bf16[256,256]{1,0:T(8,128)(2,1)S(1)} %collective-permute-done.26.refs_3_, ...), custom_call_target="tpu_custom_call" | custom-call | flops 8000000000 | bytes 8000000 | tf_op jit(solution)/shard_map/attend_back/pallas_call | solution.py:360
  314.8 7.6 %collective-permute-done.34 = bf16[48,1024]{1,0:T(8,128)(2,1)S(1)} collective-permute-done((bf16[48,1024]{1,0:T(8,128)(2,1)S(1)}, bf16[48,1024]{1,0:T(8,128)(2,1)S(1)}, u32[]{:S(2)}, u32[]{:S(2)}) %collective-permute-start.34) | collective-permute-done | bytes 98336 | tf_op jit(solution)/shard_map/ppermute | solution.py:43
  322.5 6.6 %weights.1 = bf16[1024,768]{1,0:T(8,128)(2,1)} custom-call(s32[7]{0:T(128)} %copy-done.5, bf16[1024,1024]{1,0:T(8,128)(2,1)} %get-tuple-element.134.normed_ref, bf16[1024,512]{1,0:T(8,128)(2,1)} %copy-done.2, bf16[4,256,256]{2,1,0:T(8,128)(2,1)} %copy-done.4, bf16[256,1024]{1,0:T(8,128)(2,1)} %get-tuple-element.135.b0_ref, ...), custom_call_target="tpu_custom_call" | custom-call | flops 1600000000 | bytes 8000000 | tf_op jit(solution)/shard_map/weights/pallas_call | solution.py:632
  331.4 3.4 collective-permute-start.37
  341.7 10.1 %collective-permute-done.28 = bf16[256,512]{1,0:T(8,128)(2,1)S(1)} collective-permute-done((bf16[256,512]{1,0:T(8,128)(2,1)}, bf16[256,512]{1,0:T(8,128)(2,1)S(1)}, u32[]{:S(2)}, u32[]{:S(2)}) %collective-permute-start.28) | collective-permute-done | bytes 262176 | tf_op jit(solution)/shard_map/ppermute | solution.py:43
  364.6 2.5 collective-permute-done.42
  368.9 3.1 collective-permute-start.45
  376.7 2.0 collective-permute-start.47
  378.8 3.3 collective-permute-start.55
  383.8 3.0 collective-permute-start.53
  392.7 16.0 %collective-permute-done.50.refs_1_ = bf16[4,4,32,384]{3,2,1,0:T(8,128)(2,1)S(1)} collective-permute-done((bf16[4,4,32,384]{3,2,1,0:T(8,128)(2,1)S(1)}, bf16[4,4,32,384]{3,2,1,0:T(8,128)(2,1)S(1)}, u32[]{:S(2)}, u32[]{:S(2)}) %collective-permute-start.50) | collective-permute-done | bytes 393248 | tf_op jit(solution)/shard_map/ppermute | solution.py:35
  411.1 7.8 %collective-permute-done.58.refs_7_ = bf16[4,4,32,384]{3,2,1,0:T(8,128)(2,1)S(1)} collective-permute-done((bf16[4,4,32,384]{3,2,1,0:T(8,128)(2,1)S(1)}, bf16[4,4,32,384]{3,2,1,0:T(8,128)(2,1)S(1)}, u32[]{:S(2)}, u32[]{:S(2)}) %collective-permute-start.58) | collective-permute-done | bytes 393248 | tf_op jit(solution)/shard_map/ppermute | solution.py:39
  418.9 2.5 collective-permute-start.62
  427.3 10.9 %finish.1 = (f32[1024,1024]{1,0:T(8,128)}, f32[1024,512]{1,0:T(8,128)}, f32[1024,512]{1,0:T(8,128)}, f32[1024,1024]{1,0:T(8,128)}, f32[1024,1]{1,0:T(8,128)}) custom-call(s32[7]{0:T(128)} %copy-done.5, bf16[4,4,32,384]{3,2,1,0:T(8,128)(2,1)} %copy-done.27, bf16[4,4,32,384]{3,2,1,0:T(8,128)(2,1)} %copy-done.32, ...), custom_call_target="tpu_custom_call" | custom-call | flops 10000000 | bytes 8000000 | tf_op jit(solution)/shard_map/finish/pallas_call | solution.py:632
  443.6 2.0 fusion.13
  (355 shorter events, 106.5 us)
Async XLA Ops:
  7.2 78.9 %all-gather.5.cloned.1.call-start = ((), (), s32[]{:S(2)}) async-start(), calls=%async_computation.4 | async-start | bytes 9469952 | tf_op jit(solution)/shard_map/all_gather | solution.py:805
  9.8 149.4 %all-gather.7.cloned.1.call-start = ((), (), s32[]{:S(2)}) async-start(), calls=%async_computation.5 | async-start | bytes 8912896 | tf_op jit(solution)/shard_map/all_gather | solution.py:846
  9.9 15.7 %collective-permute-start = (bf16[256,1024]{1,0:T(8,128)(2,1)}, bf16[256,1024]{1,0:T(8,128)(2,1)S(1)}, u32[]{:S(2)}, u32[]{:S(2)}) collective-permute-start(bf16[256,1024]{1,0:T(8,128)(2,1)} %bitcast.153), channel_id=1, source_target_pairs={{0,32},{32,64},{64,96},{96,0},{1,33},{33,65},{65,97},{97,1},{2,34}... | collective-permute-start | bytes 1572872 | tf_op jit(solution)/shard_map/ppermute | solution.py:43
  11.6 26.1 %collective-permute-start.1 = (bf16[256,1024]{1,0:T(8,128)(2,1)}, bf16[256,1024]{1,0:T(8,128)(2,1)S(1)}, u32[]{:S(2)}, u32[]{:S(2)}) collective-permute-start(bf16[256,1024]{1,0:T(8,128)(2,1)} %bitcast.154), channel_id=1, source_target_pairs={{0,64},{32,96},{64,0},{96,32},{1,65},{33,97},{65,1},{97,33},{2,66}... | collective-permute-start | bytes 1572872 | tf_op jit(solution)/shard_map/ppermute | solution.py:43
  14.9 23.6 %collective-permute-start.2 = (bf16[256,1024]{1,0:T(8,128)(2,1)}, bf16[256,1024]{1,0:T(8,128)(2,1)}, u32[]{:S(2)}, u32[]{:S(2)}) collective-permute-start(bf16[256,1024]{1,0:T(8,128)(2,1)} %bitcast.155), channel_id=1, source_target_pairs={{0,96},{32,0},{64,32},{96,64},{1,97},{33,1},{65,33},{97,65},{2,98}... | collective-permute-start | bytes 1572872 | tf_op jit(solution)/shard_map/ppermute | solution.py:43
  54.0 8.5 %collective-permute-start.4 = (bf16[256,256]{1,0:T(8,128)(2,1)S(1)}, bf16[256,256]{1,0:T(8,128)(2,1)S(1)}, u32[]{:S(2)}, u32[]{:S(2)}) collective-permute-start(bf16[256,256]{1,0:T(8,128)(2,1)S(1)} %get-tuple-element.245), channel_id=1, source_target_pairs={{0,64},{32,96},{64,0},{96,32},{1,65},{33,97},{65,1},{97,33},{2,66}... | collective-permute-start | bytes 393224 | tf_op jit(solution)/shard_map/ppermute | solution.py:43
  86.1 353.8 %reduce-scatter.5.cloned.1.call-start = ((), (), s32[]{:S(2)}) async-start(), calls=%async_computation.3 | async-start | bytes 3932160 | tf_op jit(solution)/shard_map/reduce_scatter | solution.py:881
  187.4 16.8 %collective-permute-start.10 = (bf16[2,272,512]{2,1,0:T(8,128)(2,1)S(1)}, bf16[2,272,512]{2,1,0:T(8,128)(2,1)S(1)}, u32[]{:S(2)}, u32[]{:S(2)}) collective-permute-start(bf16[2,272,512]{2,1,0:T(8,128)(2,1)S(1)} %get-tuple-element.215), channel_id=1, source_target_pairs={{0,24},{1,25},{2,26},{3,27},{4,28},{5,29},{6,30},{7,31},{8,0},{9,1... | collective-permute-start | bytes 1671176 | tf_op jit(solution)/shard_map/ppermute | solution.py:35
  188.0 16.2 %collective-permute-start.9 = (bf16[2,272,512]{2,1,0:T(8,128)(2,1)S(1)}, bf16[2,272,512]{2,1,0:T(8,128)(2,1)S(1)}, u32[]{:S(2)}, u32[]{:S(2)}) collective-permute-start(bf16[2,272,512]{2,1,0:T(8,128)(2,1)S(1)} %get-tuple-element.217), channel_id=1, source_target_pairs={{0,8},{1,9},{2,10},{3,11},{4,12},{5,13},{6,14},{7,15},{8,16},{9,17... | collective-permute-start | bytes 1671176 | tf_op jit(solution)/shard_map/ppermute | solution.py:35
  190.3 17.6 %collective-permute-start.12 = (bf16[2,272,512]{2,1,0:T(8,128)(2,1)S(1)}, bf16[2,272,512]{2,1,0:T(8,128)(2,1)S(1)}, u32[]{:S(2)}, u32[]{:S(2)}) collective-permute-start(bf16[2,272,512]{2,1,0:T(8,128)(2,1)S(1)} %get-tuple-element.209), channel_id=1, source_target_pairs={{0,6},{1,7},{2,0},{3,1},{4,2},{5,3},{6,4},{7,5},{8,14},{9,15},{10,... | collective-permute-start | bytes 1671176 | tf_op jit(solution)/shard_map/ppermute | solution.py:39
  191.0 16.9 %collective-permute-start.11 = (bf16[2,272,512]{2,1,0:T(8,128)(2,1)S(1)}, bf16[2,272,512]{2,1,0:T(8,128)(2,1)S(1)}, u32[]{:S(2)}, u32[]{:S(2)}) collective-permute-start(bf16[2,272,512]{2,1,0:T(8,128)(2,1)S(1)} %get-tuple-element.211), channel_id=1, source_target_pairs={{0,2},{1,3},{2,4},{3,5},{4,6},{5,7},{6,0},{7,1},{8,10},{9,11},{10,... | collective-permute-start | bytes 1671176 | tf_op jit(solution)/shard_map/ppermute | solution.py:39
  210.2 24.5 %collective-permute-start.13 = (bf16[4,272,512]{2,1,0:T(8,128)(2,1)}, bf16[4,272,512]{2,1,0:T(8,128)(2,1)S(1)}, u32[]{:S(2)}, u32[]{:S(2)}) collective-permute-start(bf16[4,272,512]{2,1,0:T(8,128)(2,1)} %pad_maximum_fusion.3), channel_id=1, source_target_pairs={{0,8},{1,9},{2,10},{3,11},{4,12},{5,13},{6,14},{7,15},{8,16},{9,17... | collective-permute-start | bytes 3342344 | tf_op jit(solution)/shard_map/ppermute | solution.py:35
  210.4 25.4 %collective-permute-start.14 = (bf16[4,272,512]{2,1,0:T(8,128)(2,1)}, bf16[4,272,512]{2,1,0:T(8,128)(2,1)}, u32[]{:S(2)}, u32[]{:S(2)}) collective-permute-start(bf16[4,272,512]{2,1,0:T(8,128)(2,1)} %pad_maximum_fusion.4), channel_id=1, source_target_pairs={{0,24},{1,25},{2,26},{3,27},{4,28},{5,29},{6,30},{7,31},{8,0},{9,1... | collective-permute-start | bytes 3342344 | tf_op jit(solution)/shard_map/ppermute | solution.py:35
  211.7 25.2 %collective-permute-start.15 = (bf16[4,272,512]{2,1,0:T(8,128)(2,1)}, bf16[4,272,512]{2,1,0:T(8,128)(2,1)}, u32[]{:S(2)}, u32[]{:S(2)}) collective-permute-start(bf16[4,272,512]{2,1,0:T(8,128)(2,1)} %pad_maximum_fusion.5), channel_id=1, source_target_pairs={{0,2},{1,3},{2,4},{3,5},{4,6},{5,7},{6,0},{7,1},{8,10},{9,11},{10,... | collective-permute-start | bytes 3342344 | tf_op jit(solution)/shard_map/ppermute | solution.py:39
  211.7 25.1 %collective-permute-start.16 = (bf16[4,272,512]{2,1,0:T(8,128)(2,1)}, bf16[4,272,512]{2,1,0:T(8,128)(2,1)}, u32[]{:S(2)}, u32[]{:S(2)}) collective-permute-start(bf16[4,272,512]{2,1,0:T(8,128)(2,1)} %pad_maximum_fusion.6), channel_id=1, source_target_pairs={{0,6},{1,7},{2,0},{3,1},{4,2},{5,3},{6,4},{7,5},{8,14},{9,15},{10,... | collective-permute-start | bytes 3342344 | tf_op jit(solution)/shard_map/ppermute | solution.py:39
  237.9 8.7 %collective-permute-start.67 = (bf16[3,1024,512]{2,1,0:T(8,128)(2,1)S(1)}, bf16[3,1024,512]{2,1,0:T(8,128)(2,1)S(1)}, u32[]{:S(2)}, u32[]{:S(2)}) collective-permute-start(bf16[3,1024,512]{2,1,0:T(8,128)(2,1)S(1)} %slice_bitcast_fusion), channel_id=1, source_target_pairs={{0,1},{1,0},{2,3},{3,2},{4,5},{5,4},{6,7},{7,6},{8,9},{9,8},{10,11... | collective-permute-start | bytes 9437192 | tf_op jit(solution)/shard_map/ppermute | solution.py:47
  249.4 194.2 %reduce-scatter.3.cloned.1.call-start = ((), (), s32[]{:S(2)}) async-start(), calls=%async_computation.2 | async-start | bytes 8912896 | tf_op jit(solution)/shard_map/reduce_scatter | solution.py:914
  263.9 8.1 %collective-permute-start.21 = (bf16[272,512]{1,0:T(8,128)(2,1)S(1)}, bf16[272,512]{1,0:T(8,128)(2,1)S(1)}, u32[]{:S(2)}, u32[]{:S(2)}) collective-permute-start(bf16[272,512]{1,0:T(8,128)(2,1)S(1)} %pad_maximum_fusion.16), channel_id=1, source_target_pairs={{0,2},{1,3},{2,4},{3,5},{4,6},{5,7},{6,0},{7,1},{8,10},{9,11},{10,... | collective-permute-start | bytes 835592 | tf_op jit(solution)/shard_map/ppermute | solution.py:39
  263.9 8.0 %collective-permute-start.22 = (bf16[272,512]{1,0:T(8,128)(2,1)S(1)}, bf16[272,512]{1,0:T(8,128)(2,1)S(1)}, u32[]{:S(2)}, u32[]{:S(2)}) collective-permute-start(bf16[272,512]{1,0:T(8,128)(2,1)S(1)} %pad_maximum_fusion.17), channel_id=1, source_target_pairs={{0,6},{1,7},{2,0},{3,1},{4,2},{5,3},{6,4},{7,5},{8,14},{9,15},{10,... | collective-permute-start | bytes 835592 | tf_op jit(solution)/shard_map/ppermute | solution.py:39
  283.2 9.7 %collective-permute-start.25 = (bf16[256,256]{1,0:T(8,128)(2,1)}, bf16[256,256]{1,0:T(8,128)(2,1)S(1)}, u32[]{:S(2)}, u32[]{:S(2)}) collective-permute-start(bf16[256,256]{1,0:T(8,128)(2,1)} %get-tuple-element.120), channel_id=1, source_target_pairs={{0,32},{32,64},{64,96},{96,0},{1,33},{33,65},{65,97},{97,1},{2,34}... | collective-permute-start | bytes 393224 | tf_op jit(solution)/shard_map/ppermute | solution.py:43
  287.1 9.0 %collective-permute-start.27 = (bf16[256,256]{1,0:T(8,128)(2,1)}, bf16[256,256]{1,0:T(8,128)(2,1)S(1)}, u32[]{:S(2)}, u32[]{:S(2)}) collective-permute-start(bf16[256,256]{1,0:T(8,128)(2,1)} %get-tuple-element.127), channel_id=1, source_target_pairs={{0,96},{32,0},{64,32},{96,64},{1,97},{33,1},{65,33},{97,65},{2,98}... | collective-permute-start | bytes 393224 | tf_op jit(solution)/shard_map/ppermute | solution.py:43
  291.0 23.1 %collective-permute-start.36 = (bf16[48,1024]{1,0:T(8,128)(2,1)S(1)}, bf16[48,1024]{1,0:T(8,128)(2,1)S(1)}, u32[]{:S(2)}, u32[]{:S(2)}) collective-permute-start(bf16[48,1024]{1,0:T(8,128)(2,1)S(1)} %maximum_maximum_fusion), channel_id=1, source_target_pairs={{0,96},{32,0},{64,32},{96,64},{1,97},{33,1},{65,33},{97,65},{2,98}... | collective-permute-start | bytes 294920 | tf_op jit(solution)/shard_map/ppermute | solution.py:43
  291.9 22.9 %collective-permute-start.35 = (bf16[48,1024]{1,0:T(8,128)(2,1)S(1)}, bf16[48,1024]{1,0:T(8,128)(2,1)S(1)}, u32[]{:S(2)}, u32[]{:S(2)}) collective-permute-start(bf16[48,1024]{1,0:T(8,128)(2,1)S(1)} %maximum_maximum_fusion), channel_id=1, source_target_pairs={{0,64},{32,96},{64,0},{96,32},{1,65},{33,97},{65,1},{97,33},{2,66}... | collective-permute-start | bytes 294920 | tf_op jit(solution)/shard_map/ppermute | solution.py:43
  292.9 29.6 %collective-permute-start.31 = (bf16[256,1024]{1,0:T(8,128)(2,1)}, bf16[256,1024]{1,0:T(8,128)(2,1)}, u32[]{:S(2)}, u32[]{:S(2)}) collective-permute-start(bf16[256,1024]{1,0:T(8,128)(2,1)} %get-tuple-element.135.b0_ref), channel_id=1, source_target_pairs={{0,32},{32,64},{64,96},{96,0},{1,33},{33,65},{65,97},{97,1},{2,34}... | collective-permute-start | bytes 1572872 | tf_op jit(solution)/shard_map/ppermute | solution.py:43
  293.7 28.9 %collective-permute-start.32 = (bf16[256,1024]{1,0:T(8,128)(2,1)}, bf16[256,1024]{1,0:T(8,128)(2,1)}, u32[]{:S(2)}, u32[]{:S(2)}) collective-permute-start(bf16[256,1024]{1,0:T(8,128)(2,1)} %get-tuple-element.135.b0_ref), channel_id=1, source_target_pairs={{0,64},{32,96},{64,0},{96,32},{1,65},{33,97},{65,1},{97,33},{2,66}... | collective-permute-start | bytes 1572872 | tf_op jit(solution)/shard_map/ppermute | solution.py:43
  296.0 26.5 %collective-permute-start.33 = (bf16[256,1024]{1,0:T(8,128)(2,1)}, bf16[256,1024]{1,0:T(8,128)(2,1)}, u32[]{:S(2)}, u32[]{:S(2)}) collective-permute-start(bf16[256,1024]{1,0:T(8,128)(2,1)} %get-tuple-element.135.b0_ref), channel_id=1, source_target_pairs={{0,96},{32,0},{64,32},{96,64},{1,97},{33,1},{65,33},{97,65},{2,98}... | collective-permute-start | bytes 1572872 | tf_op jit(solution)/shard_map/ppermute | solution.py:43
  314.1 8.4 %collective-permute-start.34 = (bf16[48,1024]{1,0:T(8,128)(2,1)S(1)}, bf16[48,1024]{1,0:T(8,128)(2,1)S(1)}, u32[]{:S(2)}, u32[]{:S(2)}) collective-permute-start(bf16[48,1024]{1,0:T(8,128)(2,1)S(1)} %maximum_maximum_fusion), channel_id=1, source_target_pairs={{0,32},{32,64},{64,96},{96,0},{1,33},{33,65},{65,97},{97,1},{2,34}... | collective-permute-start | bytes 294920 | tf_op jit(solution)/shard_map/ppermute | solution.py:43
  331.4 8.4 %collective-permute-start.37 = (bf16[544,768]{1,0:T(8,128)(2,1)}, bf16[544,768]{1,0:T(8,128)(2,1)S(1)}, u32[]{:S(2)}, u32[]{:S(2)}) collective-permute-start(bf16[544,768]{1,0:T(8,128)(2,1)} %pad_maximum_fusion.7), channel_id=1, source_target_pairs={{0,1},{1,0},{2,3},{3,2},{4,5},{5,4},{6,7},{7,6},{8,9},{9,8},{10,11... | collective-permute-start | bytes 2506760 | tf_op jit(solution)/shard_map/ppermute | solution.py:47
  336.7 15.2 %collective-permute-start.28 = (bf16[256,512]{1,0:T(8,128)(2,1)}, bf16[256,512]{1,0:T(8,128)(2,1)S(1)}, u32[]{:S(2)}, u32[]{:S(2)}) collective-permute-start(bf16[256,512]{1,0:T(8,128)(2,1)} %get-tuple-element.236), channel_id=1, source_target_pairs={{0,32},{32,64},{64,96},{96,0},{1,33},{33,65},{65,97},{97,1},{2,34}... | collective-permute-start | bytes 786440 | tf_op jit(solution)/shard_map/ppermute | solution.py:43
  336.8 16.9 %collective-permute-start.29 = (bf16[256,512]{1,0:T(8,128)(2,1)S(1)}, bf16[256,512]{1,0:T(8,128)(2,1)S(1)}, u32[]{:S(2)}, u32[]{:S(2)}) collective-permute-start(bf16[256,512]{1,0:T(8,128)(2,1)S(1)} %get-tuple-element.235), channel_id=1, source_target_pairs={{0,64},{32,96},{64,0},{96,32},{1,65},{33,97},{65,1},{97,33},{2,66}... | collective-permute-start | bytes 786440 | tf_op jit(solution)/shard_map/ppermute | solution.py:43
  337.8 17.6 %collective-permute-start.30 = (bf16[256,512]{1,0:T(8,128)(2,1)S(1)}, bf16[256,512]{1,0:T(8,128)(2,1)}, u32[]{:S(2)}, u32[]{:S(2)}) collective-permute-start(bf16[256,512]{1,0:T(8,128)(2,1)S(1)} %get-tuple-element.234), channel_id=1, source_target_pairs={{0,96},{32,0},{64,32},{96,64},{1,97},{33,1},{65,33},{97,65},{2,98}... | collective-permute-start | bytes 786440 | tf_op jit(solution)/shard_map/ppermute | solution.py:43
  341.1 15.5 %collective-permute-start.40 = (bf16[160,768]{1,0:T(8,128)(2,1)}, bf16[160,768]{1,0:T(8,128)(2,1)S(1)}, u32[]{:S(2)}, u32[]{:S(2)}) collective-permute-start(bf16[160,768]{1,0:T(8,128)(2,1)} %get-tuple-element.263), channel_id=1, source_target_pairs={{0,24},{1,25},{2,26},{3,27},{4,28},{5,29},{6,30},{7,31},{8,0},{9,1... | collective-permute-start | bytes 737288 | tf_op jit(solution)/shard_map/ppermute | solution.py:35
  341.1 17.5 %collective-permute-start.39 = (bf16[160,768]{1,0:T(8,128)(2,1)}, bf16[160,768]{1,0:T(8,128)(2,1)S(1)}, u32[]{:S(2)}, u32[]{:S(2)}) collective-permute-start(bf16[160,768]{1,0:T(8,128)(2,1)} %get-tuple-element.262), channel_id=1, source_target_pairs={{0,16},{1,17},{2,18},{3,19},{4,20},{5,21},{6,22},{7,23},{8,24},{9,... | collective-permute-start | bytes 737288 | tf_op jit(solution)/shard_map/ppermute | solution.py:35
  376.0 7.8 %collective-permute-start.49 = (bf16[4,32,384]{2,1,0:T(8,128)(2,1)S(1)}, bf16[4,32,384]{2,1,0:T(8,128)(2,1)S(1)}, u32[]{:S(2)}, u32[]{:S(2)}) collective-permute-start(bf16[4,32,384]{2,1,0:T(8,128)(2,1)S(1)} %get-tuple-element.251), channel_id=1, source_target_pairs={{0,2},{1,3},{2,4},{3,5},{4,6},{5,7},{6,0},{7,1},{8,10},{9,11},{10,... | collective-permute-start | bytes 294920 | tf_op jit(solution)/shard_map/ppermute | solution.py:39
  376.1 10.7 %collective-permute-start.48 = (bf16[4,32,384]{2,1,0:T(8,128)(2,1)S(1)}, bf16[4,32,384]{2,1,0:T(8,128)(2,1)S(1)}, u32[]{:S(2)}, u32[]{:S(2)}) collective-permute-start(bf16[4,32,384]{2,1,0:T(8,128)(2,1)S(1)} %get-tuple-element.251), channel_id=1, source_target_pairs={{0,4},{1,5},{2,6},{3,7},{4,0},{5,1},{6,2},{7,3},{8,12},{9,13},{10,... | collective-permute-start | bytes 294920 | tf_op jit(solution)/shard_map/ppermute | solution.py:39
  376.7 10.1 %collective-permute-start.47 = (bf16[4,32,384]{2,1,0:T(8,128)(2,1)S(1)}, bf16[4,32,384]{2,1,0:T(8,128)(2,1)S(1)}, u32[]{:S(2)}, u32[]{:S(2)}) collective-permute-start(bf16[4,32,384]{2,1,0:T(8,128)(2,1)S(1)} %get-tuple-element.251), channel_id=1, source_target_pairs={{0,6},{1,7},{2,0},{3,1},{4,2},{5,3},{6,4},{7,5},{8,14},{9,15},{10,... | collective-permute-start | bytes 294920 | tf_op jit(solution)/shard_map/ppermute | solution.py:39
  378.8 9.2 %collective-permute-start.55 = (bf16[4,32,384]{2,1,0:T(8,128)(2,1)S(1)}, bf16[4,32,384]{2,1,0:T(8,128)(2,1)S(1)}, u32[]{:S(2)}, u32[]{:S(2)}) collective-permute-start(bf16[4,32,384]{2,1,0:T(8,128)(2,1)S(1)} %get-tuple-element.250), channel_id=1, source_target_pairs={{0,8},{1,9},{2,10},{3,11},{4,12},{5,13},{6,14},{7,15},{8,16},{9,17... | collective-permute-start | bytes 294920 | tf_op jit(solution)/shard_map/ppermute | solution.py:35
  382.1 7.6 %collective-permute-start.54 = (bf16[4,32,384]{2,1,0:T(8,128)(2,1)S(1)}, bf16[4,32,384]{2,1,0:T(8,128)(2,1)S(1)}, u32[]{:S(2)}, u32[]{:S(2)}) collective-permute-start(bf16[4,32,384]{2,1,0:T(8,128)(2,1)S(1)} %get-tuple-element.250), channel_id=1, source_target_pairs={{0,16},{1,17},{2,18},{3,19},{4,20},{5,21},{6,22},{7,23},{8,24},{9,... | collective-permute-start | bytes 294920 | tf_op jit(solution)/shard_map/ppermute | solution.py:35
  386.9 21.7 %collective-permute-start.50 = (bf16[4,4,32,384]{3,2,1,0:T(8,128)(2,1)S(1)}, bf16[4,4,32,384]{3,2,1,0:T(8,128)(2,1)S(1)}, u32[]{:S(2)}, u32[]{:S(2)}) collective-permute-start(bf16[4,4,32,384]{3,2,1,0:T(8,128)(2,1)S(1)} %pad_maximum_fusion.14.refs_0_), channel_id=1, source_target_pairs={{0,24},{1,25},{2,26},{3,27},{4,28},{5,29},{6,30},{7,31},{8,0},{9,1... | collective-permute-start | bytes 1179656 | tf_op jit(solution)/shard_map/ppermute | solution.py:35
  387.1 21.6 %collective-permute-start.51 = (bf16[4,4,32,384]{3,2,1,0:T(8,128)(2,1)S(1)}, bf16[4,4,32,384]{3,2,1,0:T(8,128)(2,1)}, u32[]{:S(2)}, u32[]{:S(2)}) collective-permute-start(bf16[4,4,32,384]{3,2,1,0:T(8,128)(2,1)S(1)} %pad_maximum_fusion.14.refs_0_), channel_id=1, source_target_pairs={{0,16},{1,17},{2,18},{3,19},{4,20},{5,21},{6,22},{7,23},{8,24},{9,... | collective-permute-start | bytes 1179656 | tf_op jit(solution)/shard_map/ppermute | solution.py:35
  388.0 22.3 %collective-permute-start.52 = (bf16[4,4,32,384]{3,2,1,0:T(8,128)(2,1)S(1)}, bf16[4,4,32,384]{3,2,1,0:T(8,128)(2,1)}, u32[]{:S(2)}, u32[]{:S(2)}) collective-permute-start(bf16[4,4,32,384]{3,2,1,0:T(8,128)(2,1)S(1)} %pad_maximum_fusion.14.refs_0_), channel_id=1, source_target_pairs={{0,8},{1,9},{2,10},{3,11},{4,12},{5,13},{6,14},{7,15},{8,16},{9,17... | collective-permute-start | bytes 1179656 | tf_op jit(solution)/shard_map/ppermute | solution.py:35
  389.8 20.7 %collective-permute-start.56 = (bf16[4,4,32,384]{3,2,1,0:T(8,128)(2,1)S(1)}, bf16[4,4,32,384]{3,2,1,0:T(8,128)(2,1)}, u32[]{:S(2)}, u32[]{:S(2)}) collective-permute-start(bf16[4,4,32,384]{3,2,1,0:T(8,128)(2,1)S(1)} %pad_maximum_fusion.15.refs_4_), channel_id=1, source_target_pairs={{0,6},{1,7},{2,0},{3,1},{4,2},{5,3},{6,4},{7,5},{8,14},{9,15},{10,... | collective-permute-start | bytes 1179656 | tf_op jit(solution)/shard_map/ppermute | solution.py:39
  391.8 19.1 %collective-permute-start.57 = (bf16[4,4,32,384]{3,2,1,0:T(8,128)(2,1)S(1)}, bf16[4,4,32,384]{3,2,1,0:T(8,128)(2,1)S(1)}, u32[]{:S(2)}, u32[]{:S(2)}) collective-permute-start(bf16[4,4,32,384]{3,2,1,0:T(8,128)(2,1)S(1)} %pad_maximum_fusion.15.refs_4_), channel_id=1, source_target_pairs={{0,4},{1,5},{2,6},{3,7},{4,0},{5,1},{6,2},{7,3},{8,12},{9,13},{10,... | collective-permute-start | bytes 1179656 | tf_op jit(solution)/shard_map/ppermute | solution.py:39
  408.6 10.2 %collective-permute-start.58 = (bf16[4,4,32,384]{3,2,1,0:T(8,128)(2,1)S(1)}, bf16[4,4,32,384]{3,2,1,0:T(8,128)(2,1)S(1)}, u32[]{:S(2)}, u32[]{:S(2)}) collective-permute-start(bf16[4,4,32,384]{3,2,1,0:T(8,128)(2,1)S(1)} %pad_maximum_fusion.15.refs_4_), channel_id=1, source_target_pairs={{0,2},{1,3},{2,4},{3,5},{4,6},{5,7},{6,0},{7,1},{8,10},{9,11},{10,... | collective-permute-start | bytes 1179656 | tf_op jit(solution)/shard_map/ppermute | solution.py:39
  408.7 12.7 %collective-permute-start.59 = (bf16[4,4,32,384]{3,2,1,0:T(8,128)(2,1)S(1)}, bf16[4,4,32,384]{3,2,1,0:T(8,128)(2,1)S(1)}, u32[]{:S(2)}, u32[]{:S(2)}) collective-permute-start(bf16[4,4,32,384]{3,2,1,0:T(8,128)(2,1)S(1)} %pad_maximum_fusion.14.refs_0_), channel_id=1, source_target_pairs={{0,1},{1,0},{2,3},{3,2},{4,5},{5,4},{6,7},{7,6},{8,9},{9,8},{10,11... | collective-permute-start | bytes 1179656 | tf_op jit(solution)/shard_map/ppermute | solution.py:47
  410.3 11.1 %collective-permute-start.63 = (bf16[4,4,32,384]{3,2,1,0:T(8,128)(2,1)S(1)}, bf16[4,4,32,384]{3,2,1,0:T(8,128)(2,1)S(1)}, u32[]{:S(2)}, u32[]{:S(2)}) collective-permute-start(bf16[4,4,32,384]{3,2,1,0:T(8,128)(2,1)S(1)} %pad_maximum_fusion.15.refs_4_), channel_id=1, source_target_pairs={{0,1},{1,0},{2,3},{3,2},{4,5},{5,4},{6,7},{7,6},{8,9},{9,8},{10,11... | collective-permute-start | bytes 1179656 | tf_op jit(solution)/shard_map/ppermute | solution.py:47
  410.5 11.5 %collective-permute-start.60 = (bf16[4,4,32,384]{3,2,1,0:T(8,128)(2,1)S(1)}, bf16[4,4,32,384]{3,2,1,0:T(8,128)(2,1)S(1)}, u32[]{:S(2)}, u32[]{:S(2)}) collective-permute-start(bf16[4,4,32,384]{3,2,1,0:T(8,128)(2,1)S(1)} %collective-permute-done.50.refs_1_), channel_id=1, source_target_pairs={{0,1},{1,0},{2,3},{3,2},{4,5},{5,4},{6,7},{7,6},{8,9},{9,8},{10,11... | collective-permute-start | bytes 1179656 | tf_op jit(solution)/shard_map/ppermute | solution.py:47
  410.9 15.5 %collective-permute-start.61 = (bf16[4,4,32,384]{3,2,1,0:T(8,128)(2,1)}, bf16[4,4,32,384]{3,2,1,0:T(8,128)(2,1)}, u32[]{:S(2)}, u32[]{:S(2)}) collective-permute-start(bf16[4,4,32,384]{3,2,1,0:T(8,128)(2,1)} %collective-permute-done.51.refs_2_), channel_id=1, source_target_pairs={{0,1},{1,0},{2,3},{3,2},{4,5},{5,4},{6,7},{7,6},{8,9},{9,8},{10,11... | collective-permute-start | bytes 1179656 | tf_op jit(solution)/shard_map/ppermute | solution.py:47
  (81 other events, 541.9 us)
Sparse Core Ops, SparseCore 0:
  10.8 75.2 all-gather.4
  88.8 70.3 all-gather.6
  249.5 39.1 reduce-scatter.4
  291.9 91.2 reduce-scatter.2
